TPU v7x, 32 devices: a whole 2x2x4 slice. The times are simulated.
32 devices in a mesh: sub: 8 (over z, x), layer: 4 (over y, core).
Axes of the slice: x: 2, y: 2, z: 4, core: 2. Of those that a mesh axis runs over, the one named last changes fastest.
Arguments:
- local_gap: float32 [8, 4, 1152, 128], P('sub', 'layer'), may hold values from -6 to 6
- route_codes: int32 [8, 4, 1152], P('sub', 'layer'), may hold values from 0 to 1152, as said below
- flexibility: float32 [8, 4, 1152, 1152], P('sub', 'layer'), may hold values from -1 to 3
- dirichlet: float32 [8, 4, 1152, 1152], P('sub', 'layer'), may hold values from -1 to 3
- rigid_modes: float32 [8, 4, 6, 1152], P('sub', 'layer'), may hold values from -6 to 6
- coarse_inverse: float32 [192, 192], P(('sub', 'layer')), may hold values from -1 to 1
- rigid_load: float32 [192, 128], P(('sub', 'layer')), may hold values from -360 to 360
Outputs:
- multipliers: float32 [8, 4, 1152, 128], P('sub', 'layer')
- residual: float32 [8, 4, 1152, 128], P('sub', 'layer')
Inputs may be any that keep to these rules, and one draw needn't show every extreme that they name: `route_codes`: row r of subdomain (i, j) carries d * 288 + k when it is the k-th row it shares with neighbour d (0: sub index i - 1, 1: i + 1, 2: layer index j - 1, 3: j + 1); the row of that neighbour carrying e * 288 + k, e the opposite direction, is the same interface row. 4 * 288 marks a row shared with nobody. Neighbouring subdomains share between 144 and 288 rows, some pair exactly 288; there is no neighbour beyond the ends of an axis.
All inputs are finite; a program needn't handle non-finite values.
Results may differ from a plain program's by a relative error of at most 0.00017.
Values sent between devices are 32-bit elements; how exact they have to be, the bound alone decides.
No kernel may reach another device: no remote copies, remote signals or barrier semaphores. Data moves between devices by JAX's collectives and lax.ppermute only.
A program may use at most 128 MiB of HBM per device.

v0:
```python
import functools

import jax
import jax.numpy as jnp
from jax import lax
from jax.experimental import pallas as pl
from jax.experimental.pallas import tpu as pltpu
from jax.sharding import PartitionSpec as P

theta_mid = 4.25
delta_half = 3.75
sigma_ratio = theta_mid / delta_half
damping = delta_half / theta_mid
damping_next = 1.0 / (2.0 * sigma_ratio - damping)
keep_step = damping_next * damping
new_step = 2.0 * damping_next / delta_half

GROUP = 32
PAD = 8
SIDES = 4


def exact(a, b, contract=((1,), (0,))):
    return lax.dot_general(
        a,
        b,
        (contract, ((), ())),
        precision=lax.Precision.HIGHEST,
        preferred_element_type=jnp.float32,
    )


def one_pass(a, b):
    return jnp.dot(a, b, preferred_element_type=jnp.float32)


def two_pieces(x):
    high = x.astype(jnp.bfloat16)
    low = (x - high.astype(jnp.float32)).astype(jnp.bfloat16)
    return high, low


def slot_by_row(codes_row, start, rows):
    slots = lax.broadcasted_iota(jnp.int32, (rows, codes_row.shape[1]), 0) + start
    return jnp.where(slots == codes_row, 1.0, 0.0).astype(jnp.bfloat16)


def row_by_slot(codes_lanes, slots):
    rows, lanes = codes_lanes.shape
    lane = lax.broadcasted_iota(jnp.int32, (rows, lanes), 1)
    parts = [
        jnp.where(lane + first == codes_lanes, 1.0, 0.0).astype(jnp.bfloat16)
        for first in range(0, slots, lanes)
    ]
    return jnp.concatenate(parts, axis=1)


def fill_pieces(pieces, start, x):
    high, low = two_pieces(x)
    cols = x.shape[1]
    pieces[pl.ds(start, x.shape[0]), 0:cols] = high
    pieces[pl.ds(start, x.shape[0]), cols : 2 * cols] = low


def to_rows(codes_lanes, slot_pieces, write):
    total = slot_pieces.shape[0]
    chunk = total // SIDES
    for c in range(SIDES):
        pick = row_by_slot(codes_lanes[c * chunk : (c + 1) * chunk, :], total)
        write(c * chunk, one_pass(pick, slot_pieces[...]))


def halves(x):
    cols = x.shape[1] // 2
    return x[:, :cols] + x[:, cols:]


def apply_local(matrix, codes_row, codes_lanes, slot_pieces, row_pieces, out_pieces, write, less=None):
    total = slot_pieces.shape[0]
    chunk = total // SIDES

    def keep(start, rows):
        row_pieces[start : start + chunk, :] = rows.astype(jnp.bfloat16)

    to_rows(codes_lanes, slot_pieces, keep)
    apply_rows(matrix, codes_row, row_pieces, out_pieces, write, less)


def apply_rows(matrix, codes_row, row_pieces, out_pieces, write, less=None):
    total = row_pieces.shape[0]
    chunk = total // SIDES
    cols = row_pieces.shape[1] // 2
    for c in range(SIDES):
        high, low = two_pieces(matrix[c * chunk : (c + 1) * chunk, :])
        product = halves(one_pass(high, row_pieces[...])) + one_pass(low, row_pieces[:, :cols])
        if less is not None:
            product = less[c * chunk : (c + 1) * chunk, :] - product
        fill_pieces(out_pieces, c * chunk, product)
    for side in range(SIDES):
        pick = slot_by_row(codes_row[...], side * chunk, chunk)
        write(side, halves(one_pass(pick, out_pieces[...])))


def three_pass(a, b):
    a_high, a_low = two_pieces(a)
    b_high, b_low = two_pieces(b)
    both = jnp.concatenate([b_high, b_low], axis=1)
    return halves(one_pass(a_high, both)) + one_pass(a_low, b_high)


def modes_kernel(mode_count, codes_row, modes, inverse, load, *outs):
    total = codes_row.shape[1]
    cap = total // SIDES
    codes = jnp.broadcast_to(codes_row[...], (128, total)).astype(jnp.float32)
    codes_lanes = jnp.transpose(codes).astype(jnp.int32)
    x = jnp.concatenate(
        [modes[...], jnp.zeros((PAD - mode_count, total), jnp.float32)], axis=0
    )
    high = x.astype(jnp.bfloat16).astype(jnp.float32)
    middle = (x - high).astype(jnp.bfloat16).astype(jnp.float32)
    low = x - high - middle
    pieces = jnp.concatenate([high, middle, low, jnp.zeros_like(low)], axis=0).astype(jnp.bfloat16)
    moved = one_pass(pieces, row_by_slot(codes_lanes, total))
    upper, lower = moved[0:PAD], moved[PAD : 2 * PAD]
    moved = upper + lower + moved[2 * PAD : 3 * PAD]
    for side in range(SIDES):
        outs[side][...] = moved[:, side * cap : (side + 1) * cap]
    coarse = inverse.shape[1]
    padded = coarse // mode_count * PAD
    old = lax.broadcasted_iota(jnp.int32, (coarse, padded), 0)
    new = lax.broadcasted_iota(jnp.int32, (coarse, padded), 1)
    spread = jnp.where((old // mode_count) * PAD + old % mode_count == new, 1.0, 0.0)
    blank = jnp.zeros((PAD - mode_count, coarse), jnp.float32)
    wide = exact(jnp.concatenate([inverse[...], blank], axis=0), spread)
    blank = jnp.zeros((PAD - mode_count, load.shape[1]), jnp.float32)
    loads = jnp.concatenate([load[...], blank], axis=0)
    outs[SIDES][...] = jnp.concatenate([wide, loads], axis=1)
    outs[SIDES + 1][...] = codes_lanes
    outs[SIDES + 2][...] = jnp.concatenate([upper, lower], axis=0)


def around(place, layers):
    return [place, place - layers, place + layers, place - 1, place + 1]


def mode_blocks(own, partner):
    cap = own[0].shape[1]
    rows = []
    for side in range(SIDES):
        column = [own[side][...]]
        for other in range(SIDES):
            if other == side:
                column.append(-partner[side][...])
            else:
                column.append(jnp.zeros((PAD, cap), jnp.float32))
        rows.append(jnp.concatenate(column, axis=0))
    return rows


def lane_spread(mode_count, lanes):
    shape = (PAD * (SIDES + 1), lanes)
    old = lax.broadcasted_iota(jnp.int32, shape, 0)
    new = lax.broadcasted_iota(jnp.int32, shape, 1)
    spot = (old // PAD) * mode_count + old % PAD
    match = (spot == new % GROUP) & (old % PAD < mode_count)
    return jnp.where(match, 1.0, 0.0)


def operators_kernel(mode_count, flex, schur, codes_row, codes_lanes, *refs):
    own, partner = refs[0:4], refs[4:8]
    outs = refs[8:12]
    modes_out = refs[12]
    slot_pieces, row_pieces, out_pieces = refs[13:16]
    total = codes_lanes.shape[0]
    cap = total // SIDES
    half = cap // 2
    lanes = 4 * GROUP
    spread = lane_spread(mode_count, lanes)
    for side, block in enumerate(mode_blocks(own, partner)):
        placed = exact(block, spread, ((0,), (0,)))
        first = lax.broadcasted_iota(jnp.int32, placed.shape, 1) < GROUP
        modes_out[side * cap : (side + 1) * cap, :] = jnp.where(first, placed, 0.0)
        fill_pieces(slot_pieces, side * cap, placed)
    group = lax.broadcasted_iota(jnp.int32, (half, lanes), 1) // GROUP

    def write_schur(side, block):
        outs[side][...] = jnp.where(group == 0, block[:half], block[half:])

    def write_flex(side, block):
        mine = jnp.where(group == 2, block[:half], block[half:])
        outs[side][...] = jnp.where(group < 2, outs[side][...], mine)

    apply_local(schur, codes_row, codes_lanes, slot_pieces, row_pieces, out_pieces, write_schur)
    apply_rows(flex, codes_row, row_pieces, out_pieces, write_flex)


def start_kernel(mode_count, layers, flex, gap, codes_row, codes_lanes, *refs):
    slabs = refs[0:4]
    gathered, modes, place_ref = refs[4:7]
    outs = refs[7:11]
    start_out, inverse_out = refs[11:13]
    slot_pieces, row_pieces, out_pieces = refs[13:16]
    cap = codes_lanes.shape[0] // SIDES
    wide = gathered.shape[0]
    place = place_ref[0]
    spread = lane_spread(mode_count, GROUP)
    for n, centre in enumerate(around(place, layers)):
        rows = []
        for near in around(centre, layers):
            first = jnp.clip(near, 0, wide // PAD - 1) * PAD
            rows.append(gathered[pl.ds(pl.multiple_of(first, PAD), PAD), 0:wide])
        table = jnp.concatenate(rows, axis=0)
        inverse_out[n * GROUP : (n + 1) * GROUP, :] = exact(spread, table, ((0,), (0,)))
    coefficients = repeated(exact(inverse_out[0:GROUP, :], gathered[:, wide:]))
    start = three_pass(modes[...], coefficients)
    start_out[...] = start
    fill_pieces(slot_pieces, 0, start)

    def write(side, block):
        outs[side][0:cap, :] = block
        outs[side][cap:, :] = slabs[side][...]

    apply_local(flex, codes_row, codes_lanes, slot_pieces, row_pieces, out_pieces, write, gap)


def repeated(x):
    return jnp.concatenate([x] * 4, axis=0)


def components_of(own_pieces, block_pieces):
    both = one_pass(own_pieces[...].astype(jnp.bfloat16), block_pieces[...])
    cols = both.shape[1] // 2
    return halves(both[0:PAD]) + both[PAD:, :cols]


def grouped(slab, first):
    group = lax.broadcasted_iota(jnp.int32, slab.shape, 1) // GROUP
    upper = jnp.where(group == first, slab, 0.0)
    lower = jnp.where(group == first + 1, slab, 0.0)
    return jnp.concatenate([upper, lower], axis=0)


def lagged(side, first, mine, theirs, coefficients):
    left = jnp.concatenate([grouped(mine[...], first), grouped(theirs[...], first)], axis=1)
    near = coefficients[(side + 1) * GROUP : (side + 2) * GROUP]
    return three_pass(left, jnp.concatenate([repeated(coefficients[0:GROUP]), repeated(-near)], axis=0))


def first_kernel(schur, codes_row, codes_lanes, *refs):
    received, sent, own = refs[0:4], refs[4:8], refs[8]
    outs = refs[9:13]
    gap_out, parts_out = refs[13:15]
    slot_pieces, row_pieces, out_pieces = refs[15:18]
    cap = codes_lanes.shape[0] // SIDES
    for side in range(SIDES):
        block = sent[side][0:cap, :] - received[side][0:cap, :]
        gap_out[side * cap : (side + 1) * cap, :] = block
        fill_pieces(slot_pieces, side * cap, block)
    parts_out[...] = components_of(own, slot_pieces)

    def write(side, block):
        outs[side][...] = block

    apply_local(schur, codes_row, codes_lanes, slot_pieces, row_pieces, out_pieces, write)


def stage_kernel(stage, counts, matrix, codes_row, codes_lanes, *refs):
    refs = list(refs)

    def take(count):
        taken = refs[:count]
        del refs[:count]
        return taken

    received, sent, mine, theirs = take(4), take(4), take(4), take(4)
    own, gathered, inverse_rows, modes = take(4)
    states_in = take(counts[0])
    outs = take(4) if stage < 5 else []
    states_out = take(counts[1])
    (parts_out,) = take(1)
    slot_pieces, row_pieces, out_pieces = take(3)
    total = codes_lanes.shape[0]
    cap = total // SIDES
    coefficients = exact(inverse_rows[...], gathered[...])
    direct_all = three_pass(modes[...], repeated(coefficients[0:GROUP]))
    tail = pl.ds(cap, cap // 2)
    for side in range(SIDES):
        rows = slice(side * cap, (side + 1) * cap)
        jump = sent[side][...] - received[side][...]
        first = 0 if stage in (2, 4) else 2
        behind = lagged(side, first, mine[side].at[tail], theirs[side].at[tail], coefficients)
        direct = direct_all[rows, :]
        nextin = None
        if stage == 2:
            (gap,) = states_in
            block = 0.5 * (jump - behind)
            nextin = block
            states_out[0][rows, :] = block
            states_out[1][rows, :] = gap[rows, :] - direct
        elif stage == 3:
            precond, residual = states_in
            block = (jump - behind) / theta_mid
            nextin = residual[rows, :] - block
            states_out[0][rows, :] = nextin
            states_out[1][rows, :] = (precond[rows, :] - direct) / theta_mid
        elif stage == 4:
            residual, step = states_in
            block = 0.5 * (jump + behind)
            nextin = keep_step * step[rows, :] + new_step * block
            states_out[0][rows, :] = residual[rows, :] + direct
            states_out[1][rows, :] = nextin
        else:
            residual, raw_step, start, step = states_in
            block = jump - new_step * behind
            states_out[0][rows, :] = residual[rows, :] - block
            second = raw_step[rows, :] - new_step * direct
            states_out[1][rows, :] = second + start[rows, :] + step[rows, :]
        if nextin is not None:
            fill_pieces(slot_pieces, side * cap, nextin)
        fill_pieces(out_pieces, side * cap, block)
    parts_out[...] = components_of(own, out_pieces)
    if stage < 5:

        def write(side, block):
            outs[side][...] = block

        apply_local(matrix, codes_row, codes_lanes, slot_pieces, row_pieces, out_pieces, write)


def rows_kernel(codes_lanes, residual, multipliers, modes, residual_out, multipliers_out, modes_out, pieces):
    total = residual.shape[0]
    cap = total // SIDES
    for n, source in enumerate((residual, multipliers, modes)):
        high, low = two_pieces(source[...])
        pieces[:, 256 * n : 256 * n + 128] = high
        pieces[:, 256 * n + 128 : 256 * (n + 1)] = low

    def keep(begin, rows):
        for n, target in enumerate((residual_out, multipliers_out, modes_out)):
            target[begin : begin + cap, :] = halves(rows[:, 256 * n : 256 * (n + 1)])

    to_rows(codes_lanes, pieces, keep)


def last_kernel(residual, modes, gathered, inverse_rows, out):
    coefficients = repeated(exact(inverse_rows[0:GROUP, :], gathered[...]))
    out[...] = residual[...] + three_pass(modes[...], coefficients)


def call(kernel, name, outs, inputs, scratch=(), smem=(), extra=0):
    vmem = pl.BlockSpec(memory_space=pltpu.VMEM)
    scalar = pl.BlockSpec(memory_space=pltpu.SMEM)
    return pl.pallas_call(
        kernel,
        name=name,
        out_shape=[jax.ShapeDtypeStruct(shape, jnp.float32) if isinstance(shape, tuple) else shape for shape in outs],
        in_specs=[scalar if n in smem else vmem for n in range(len(inputs))],
        out_specs=[vmem] * len(outs),
        scratch_shapes=list(scratch),
        compiler_params=pltpu.CompilerParams(vmem_limit_bytes=28 * 1024 * 1024 + extra),
    )(*inputs)


def exchange(blocks):
    received = []
    for side in range(SIDES):
        axis = "sub" if side < 2 else "layer"
        count = lax.axis_size(axis)
        if side % 2 == 0:
            pairs = [(i, i + 1) for i in range(count - 1)]
        else:
            pairs = [(i + 1, i) for i in range(count - 1)]
        received.append(lax.ppermute(blocks[side + 1 - 2 * (side % 2)], axis, pairs))
    return received


def everywhere(block):
    return lax.all_gather(block, ("sub", "layer"), axis=0, tiled=True)


def per_device(
    local_gap, route_codes, flexibility, dirichlet, rigid_modes, coarse_inverse, rigid_load
):
    gap = local_gap[0, 0]
    flex = flexibility[0, 0]
    schur = dirichlet[0, 0]
    modes = rigid_modes[0, 0]
    mode_count, total = modes.shape
    cap = total // SIDES
    cols = gap.shape[1]
    codes_row = route_codes[0]
    layers = lax.axis_size("layer")
    wide = lax.axis_size("sub") * layers * PAD
    place = (lax.axis_index("sub") * layers + lax.axis_index("layer")).astype(jnp.int32)[None]
    pieces = pltpu.VMEM((total, 2 * cols), jnp.bfloat16)
    scratch = [pieces] * 3
    block = [(cap, cols)] * SIDES
    whole = (total, cols)
    parts = (PAD, cols)
    table = 8 * wide * (wide + cols)

    shown = call(
        functools.partial(modes_kernel, mode_count),
        "modes_to_slots",
        [(PAD, cap)] * SIDES
        + [(PAD, wide + cols), jax.ShapeDtypeStruct((total, 128), jnp.int32), (2 * PAD, total)],
        [codes_row, modes, coarse_inverse, rigid_load],
        extra=table,
    )
    own, (inverse_load, codes_lanes, own_pieces) = shown[:4], shown[4:]
    gathered = everywhere(inverse_load)
    partner = exchange(own)
    shown = call(
        functools.partial(operators_kernel, mode_count),
        "operators_on_modes",
        [(cap // 2, 4 * GROUP)] * SIDES + [(total, 4 * GROUP)],
        [flex, schur, codes_row, codes_lanes, *own, *partner],
        scratch,
    )
    slabs, slot_modes = shown[:4], shown[4]
    shown = call(
        functools.partial(start_kernel, mode_count, layers),
        "start",
        [(cap + cap // 2, cols)] * SIDES + [whole, (5 * GROUP, wide)],
        [flex, gap, codes_row, codes_lanes, *slabs, gathered, slot_modes, place],
        scratch,
        smem=(10,),
        extra=table,
    )
    sent, (start, inverse_rows) = shown[:4], shown[4:]
    received = exchange(sent)
    slab_sent, slab_received = sent, received
    shown = call(
        first_kernel,
        "stage_1",
        block + [whole, parts],
        [schur, codes_row, codes_lanes, *received, *sent, own_pieces],
        scratch,
    )
    sent, (gap_jump, components) = shown[:4], shown[4:]

    def stage(number, matrix, states_in, sent, components):
        gathered = everywhere(components)
        received = exchange(sent)
        inputs = [codes_row, codes_lanes, *received, *sent, *slab_sent, *slab_received]
        inputs += [own_pieces, gathered, inverse_rows, slot_modes, *states_in]
        outs = [whole] * 2 + [parts]
        kernel = functools.partial(stage_kernel, number, (len(states_in), 2))
        if matrix is None:
            kernel = functools.partial(kernel, None)
        else:
            inputs, outs = [matrix] + inputs, block + outs
        return call(kernel, "stage_%d" % number, outs, inputs, scratch)

    shown = stage(2, flex, [gap_jump], sent, components)
    sent, (precond, residual, components) = shown[:4], shown[4:]
    shown = stage(3, schur, [precond, residual], sent, components)
    sent, (residual, step, components) = shown[:4], shown[4:]
    shown = stage(4, flex, [residual, step], sent, components)
    sent, (residual, raw_step, components) = shown[:4], shown[4:]
    shown = stage(5, None, [residual, raw_step, start, step], sent, components)
    residual, multipliers, components = shown

    gathered = everywhere(components)
    residual, multipliers, row_modes = call(
        rows_kernel,
        "slots_to_rows",
        [whole, whole, (total, 4 * GROUP)],
        [codes_lanes, residual, multipliers, slot_modes],
        [pltpu.VMEM((total, 768), jnp.bfloat16)],
    )
    (residual,) = call(
        last_kernel, "residual", [whole], [residual, row_modes, gathered, inverse_rows]
    )
    return (multipliers[None, None], residual[None, None])


def solution(mesh):
    placed = (
        P("sub", "layer", None, None),
        P("sub", "layer", None),
        P("sub", "layer", None, None),
        P("sub", "layer", None, None),
        P("sub", "layer", None, None),
        P(("sub", "layer"), None),
        P(("sub", "layer"), None),
    )
    return jax.shard_map(
        per_device,
        mesh=mesh,
        in_specs=placed,
        out_specs=(P("sub", "layer", None, None), P("sub", "layer", None, None)),
        check_vma=False,
    )
```

profile of v0, /device:TPU:0, one launch (start us, length us, event | category | flops | bytes accessed | tf_op | source)
XLA Modules:
  0.0 338.7 jit_solution(6507224034210594125)
XLA Ops:
  0.6 0.8 copy.11
  1.4 0.7 copy-done.5
  2.1 0.7 copy-done.8
  2.8 0.7 copy-done.9
  3.5 0.9 modes_to_slots.1
  4.3 1.3 collective-permute-start.1
  5.6 5.5 %collective-permute-start = (f32[8,288]{1,0:T(8,128)S(1)}, f32[8,288]{1,0:T(8,128)S(1)}, u32[]{:S(2)}, u32[]{:S(2)}) collective-permute-start(f32[8,288]{1,0:T(8,128)S(1)} %get-tuple-element.55.refs_1_), channel_id=1, source_target_pairs={{0,4},{4,8},{8,12},{12,16},{16,20},{20,24},{24,28},{1,5},{5,9},{9,... | collective-permute-start | bytes 27656 | tf_op jit(solution)/shard_map/ppermute | solution.py:373
  11.1 1.3 collective-permute-start.3
  12.4 3.0 collective-permute-start.2
  15.4 41.3 %all_gather.18.refs_4_ = f32[256,384]{1,0:T(8,128)S(1)} all-gather(f32[8,384]{1,0:T(8,128)S(1)} %get-tuple-element.62), channel_id=1, replica_groups=mesh['sub'=8,'layer'=4] {'sub','layer'}, dimensions={0}, use_global_device_ids=true | all-gather | bytes 405504 | tf_op jit(solution)/shard_map/all_gather | solution.py:378
  56.7 2.5 copy-done
  59.2 2.5 copy-done.2
  61.7 0.7 copy-done.6
  62.4 6.2 %operators_on_modes.1 = (f32[144,128]{1,0:T(8,128)S(1)}, f32[144,128]{1,0:T(8,128)S(1)}, f32[144,128]{1,0:T(8,128)S(1)}, f32[144,128]{1,0:T(8,128)S(1)}, f32[1152,128]{1,0:T(8,128)S(1)}) custom-call(f32[1152,1152]{1,0:T(8,128)S(1)} %bitcast.10, f32[1152,1152]{1,0:T(8,128)S(1)} %bitcast.14, s32[1,1152]{1,0:T(1,128)S(1)} %bitcast.19, ...), custom_call_target="tpu_custom_call" | custom-call | tf_op jit(solution)/shard_map/operators_on_modes/pallas_call | solution.py:353
  68.6 4.0 %start.1 = (f32[432,128]{1,0:T(8,128)S(1)}, f32[432,128]{1,0:T(8,128)S(1)}, f32[432,128]{1,0:T(8,128)S(1)}, f32[432,128]{1,0:T(8,128)S(1)}, f32[1152,128]{1,0:T(8,128)S(1)}, /*index=5*/f32[160,256]{1,0:T(8,128)S(1)}) custom-call(f32[1152,1152]{1,0:T(8,128)S(1)} %bitcast.11, f32[1152,128]{1,0:T(8,128)S(1)} %bitcast.17, s32[1,1152]{1,0:T(1,128)S(1)} %bitcast.20, ...), custom_call_target="tpu_custom_call" | custom-call | tf_op jit(solution)/shard_map/start/pallas_call | solution.py:353
  72.7 1.3 collective-permute-start.4
  74.0 1.3 collective-permute-start.5
  75.3 2.3 collective-permute-start.6
  77.5 1.5 collective-permute-start.7
  79.0 5.1 %collective-permute-done.4.refs_0_.refs_12_ = f32[432,128]{1,0:T(8,128)S(1)} collective-permute-done((f32[432,128]{1,0:T(8,128)S(1)}, f32[432,128]{1,0:T(8,128)S(1)}, u32[]{:S(2)}, u32[]{:S(2)}) %collective-permute-start.4) | collective-permute-done | bytes 221216 | tf_op jit(solution)/shard_map/ppermute | solution.py:373
  84.2 3.4 stage_1.1
  87.5 4.4 %collective-permute-start.8 = (f32[288,128]{1,0:T(8,128)S(1)}, f32[288,128]{1,0:T(8,128)S(1)}, u32[]{:S(2)}, u32[]{:S(2)}) collective-permute-start(f32[288,128]{1,0:T(8,128)S(1)} %get-tuple-element.69.refs_5_), channel_id=1, source_target_pairs={{0,4},{4,8},{8,12},{12,16},{16,20},{20,24},{24,28},{1,5},{5,9},{9,... | collective-permute-start | bytes 442376 | tf_op jit(solution)/shard_map/ppermute | solution.py:373
  92.0 1.3 collective-permute-start.9
  93.2 2.1 collective-permute-start.10
  95.4 1.3 collective-permute-start.11
  96.7 41.7 %all_gather.19.refs_17_ = f32[256,128]{1,0:T(8,128)S(1)} all-gather(f32[8,128]{1,0:T(8,128)S(1)} %get-tuple-element.73), channel_id=1, replica_groups=mesh['sub'=8,'layer'=4] {'sub','layer'}, dimensions={0}, use_global_device_ids=true | all-gather | bytes 135168 | tf_op jit(solution)/shard_map/all_gather | solution.py:378
  138.4 4.6 %stage_2.1 = (f32[288,128]{1,0:T(8,128)S(1)}, f32[288,128]{1,0:T(8,128)S(1)}, f32[288,128]{1,0:T(8,128)S(1)}, f32[288,128]{1,0:T(8,128)S(1)}, f32[1152,128]{1,0:...) custom-call(f32[1152,1152]{1,0:T(8,128)S(1)} %bitcast.12, s32[1,1152]{1,0:T(1,128)S(1)} %bitcast.22, ...), custom_call_target="tpu_custom_call" | custom-call | tf_op jit(solution)/shard_map/stage_2/pallas_call | solution.py:353
  143.0 1.3 collective-permute-start.12
  144.3 1.3 collective-permute-start.13
  145.6 2.3 collective-permute-start.14
  147.9 1.3 collective-permute-start.15
  149.2 41.6 %all_gather.20.refs_17_ = f32[256,128]{1,0:T(8,128)S(1)} all-gather(f32[8,128]{1,0:T(8,128)S(1)} %get-tuple-element.80), channel_id=1, replica_groups=mesh['sub'=8,'layer'=4] {'sub','layer'}, dimensions={0}, use_global_device_ids=true | all-gather | bytes 135168 | tf_op jit(solution)/shard_map/all_gather | solution.py:378
  190.8 4.7 %stage_3.1 = (f32[288,128]{1,0:T(8,128)S(1)}, f32[288,128]{1,0:T(8,128)S(1)}, f32[288,128]{1,0:T(8,128)S(1)}, f32[288,128]{1,0:T(8,128)S(1)}, f32[1152,128]{1,0:...) custom-call(f32[1152,1152]{1,0:T(8,128)S(1)} %bitcast.16, s32[1,1152]{1,0:T(1,128)S(1)} %bitcast.23, ...), custom_call_target="tpu_custom_call" | custom-call | tf_op jit(solution)/shard_map/stage_3/pallas_call | solution.py:353
  195.5 1.3 collective-permute-start.16
  196.8 1.3 collective-permute-start.17
  198.1 2.3 collective-permute-start.18
  200.3 1.3 collective-permute-start.19
  201.6 41.3 %all_gather.21.refs_17_ = f32[256,128]{1,0:T(8,128)S(1)} all-gather(f32[8,128]{1,0:T(8,128)S(1)} %get-tuple-element.87), channel_id=1, replica_groups=mesh['sub'=8,'layer'=4] {'sub','layer'}, dimensions={0}, use_global_device_ids=true | all-gather | bytes 135168 | tf_op jit(solution)/shard_map/all_gather | solution.py:378
  243.0 4.7 %stage_4.1 = (f32[288,128]{1,0:T(8,128)S(1)}, f32[288,128]{1,0:T(8,128)S(1)}, f32[288,128]{1,0:T(8,128)S(1)}, f32[288,128]{1,0:T(8,128)S(1)}, f32[1152,128]{1,0:...) custom-call(f32[1152,1152]{1,0:T(8,128)S(1)} %bitcast.13, s32[1,1152]{1,0:T(1,128)S(1)} %bitcast.24, ...), custom_call_target="tpu_custom_call" | custom-call | tf_op jit(solution)/shard_map/stage_4/pallas_call | solution.py:353
  247.7 1.3 collective-permute-start.20
  249.0 1.3 collective-permute-start.21
  250.3 2.3 collective-permute-start.22
  252.6 1.3 collective-permute-start.23
  253.9 41.3 %all_gather.22.refs_17_ = f32[256,128]{1,0:T(8,128)S(1)} all-gather(f32[8,128]{1,0:T(8,128)S(1)} %get-tuple-element.94), channel_id=1, replica_groups=mesh['sub'=8,'layer'=4] {'sub','layer'}, dimensions={0}, use_global_device_ids=true | all-gather | bytes 135168 | tf_op jit(solution)/shard_map/all_gather | solution.py:378
  295.2 1.5 stage_5.1
  296.7 37.2 %all_gather.23.gathered = f32[256,128]{1,0:T(8,128)S(1)} all-gather(f32[8,128]{1,0:T(8,128)S(1)} %get-tuple-element.103), channel_id=1, replica_groups=mesh['sub'=8,'layer'=4] {'sub','layer'}, dimensions={0}, use_global_device_ids=true | all-gather | bytes 135168 | tf_op jit(solution)/shard_map/all_gather | solution.py:378
  334.0 3.3 slots_to_rows.1
  337.3 1.4 residual.1
  (37 shorter events, 0.1 us)
Async XLA Ops:
  1.4 0.7 copy-start.5
  2.1 0.7 copy-start.8
  2.8 0.7 copy-start.9
  4.3 52.4 %collective-permute-start.1 = (f32[8,288]{1,0:T(8,128)S(1)}, f32[8,288]{1,0:T(8,128)S(1)}, u32[]{:S(2)}, u32[]{:S(2)}) collective-permute-start(f32[8,288]{1,0:T(8,128)S(1)} %get-tuple-element.54.refs_0_), channel_id=1, source_target_pairs={{4,0},{8,4},{12,8},{16,12},{20,16},{24,20},{28,24},{5,1},{9,5},{13... | collective-permute-start | bytes 27656 | tf_op jit(solution)/shard_map/ppermute | solution.py:373
  5.6 51.1 %collective-permute-start = (f32[8,288]{1,0:T(8,128)S(1)}, f32[8,288]{1,0:T(8,128)S(1)}, u32[]{:S(2)}, u32[]{:S(2)}) collective-permute-start(f32[8,288]{1,0:T(8,128)S(1)} %get-tuple-element.55.refs_1_), channel_id=1, source_target_pairs={{0,4},{4,8},{8,12},{12,16},{16,20},{20,24},{24,28},{1,5},{5,9},{9,... | collective-permute-start | bytes 27656 | tf_op jit(solution)/shard_map/ppermute | solution.py:373
  11.1 45.6 %collective-permute-start.3 = (f32[8,288]{1,0:T(8,128)S(1)}, f32[8,288]{1,0:T(8,128)S(1)}, u32[]{:S(2)}, u32[]{:S(2)}) collective-permute-start(f32[8,288]{1,0:T(8,128)S(1)} %get-tuple-element.56.refs_2_), channel_id=1, source_target_pairs={{1,0},{2,1},{3,2},{5,4},{6,5},{7,6},{9,8},{10,9},{11,10},{13,12},{... | collective-permute-start | bytes 27656 | tf_op jit(solution)/shard_map/ppermute | solution.py:373
  12.4 44.3 %collective-permute-start.2 = (f32[8,288]{1,0:T(8,128)S(1)}, f32[8,288]{1,0:T(8,128)S(1)}, u32[]{:S(2)}, u32[]{:S(2)}) collective-permute-start(f32[8,288]{1,0:T(8,128)S(1)} %get-tuple-element.57.refs_3_), channel_id=1, source_target_pairs={{0,1},{1,2},{2,3},{4,5},{5,6},{6,7},{8,9},{9,10},{10,11},{12,13},{... | collective-permute-start | bytes 27656 | tf_op jit(solution)/shard_map/ppermute | solution.py:373
  56.7 2.5 copy-start
  59.2 2.5 copy-start.2
  61.7 0.7 copy-start.6
  62.4 6.2 %copy-start.1 = (f32[1,1,1152,1152]{3,2,1,0:T(8,128)S(1)}, f32[1,1,1152,1152]{3,2,1,0:T(8,128)}, u32[]{:S(2)}) copy-start(f32[1,1,1152,1152]{3,2,1,0:T(8,128)} %param.9) | copy-start | bytes 15925252
  62.4 6.2 %copy-start.4 = (f32[1,1,1152,128]{3,2,1,0:T(8,128)S(1)}, f32[1,1,1152,128]{3,2,1,0:T(8,128)}, u32[]{:S(2)}) copy-start(f32[1,1,1152,128]{3,2,1,0:T(8,128)} %param.7) | copy-start | bytes 1769476
  62.4 6.2 %copy-start.7 = (s32[1,1,1152]{2,1,0:T(1,128)S(1)}, s32[1,1,1152]{2,1,0:T(1,128)}, u32[]{:S(2)}) copy-start(s32[1,1,1152]{2,1,0:T(1,128)} %param.8) | copy-start | bytes 13828
  68.6 15.6 %copy-start.3 = (f32[1,1,1152,1152]{3,2,1,0:T(8,128)S(1)}, f32[1,1,1152,1152]{3,2,1,0:T(8,128)}, u32[]{:S(2)}) copy-start(f32[1,1,1152,1152]{3,2,1,0:T(8,128)} %param.10) | copy-start | bytes 15925252
  72.7 11.5 %collective-permute-start.4 = (f32[432,128]{1,0:T(8,128)S(1)}, f32[432,128]{1,0:T(8,128)S(1)}, u32[]{:S(2)}, u32[]{:S(2)}) collective-permute-start(f32[432,128]{1,0:T(8,128)S(1)} %get-tuple-element.64.refs_5_.refs_9_), channel_id=1, source_target_pairs={{0,4},{4,8},{8,12},{12,16},{16,20},{20,24},{24,28},{1,5},{5,9},{9,... | collective-permute-start | bytes 663560 | tf_op jit(solution)/shard_map/ppermute | solution.py:373
  74.0 10.2 %collective-permute-start.5 = (f32[432,128]{1,0:T(8,128)S(1)}, f32[432,128]{1,0:T(8,128)S(1)}, u32[]{:S(2)}, u32[]{:S(2)}) collective-permute-start(f32[432,128]{1,0:T(8,128)S(1)} %get-tuple-element.65.refs_4_.refs_8_), channel_id=1, source_target_pairs={{4,0},{8,4},{12,8},{16,12},{20,16},{24,20},{28,24},{5,1},{9,5},{13... | collective-permute-start | bytes 663560 | tf_op jit(solution)/shard_map/ppermute | solution.py:373
  75.3 8.9 %collective-permute-start.6 = (f32[432,128]{1,0:T(8,128)S(1)}, f32[432,128]{1,0:T(8,128)S(1)}, u32[]{:S(2)}, u32[]{:S(2)}) collective-permute-start(f32[432,128]{1,0:T(8,128)S(1)} %get-tuple-element.66.refs_7_.refs_11_), channel_id=1, source_target_pairs={{0,1},{1,2},{2,3},{4,5},{5,6},{6,7},{8,9},{9,10},{10,11},{12,13},{... | collective-permute-start | bytes 663560 | tf_op jit(solution)/shard_map/ppermute | solution.py:373
  77.5 6.6 %collective-permute-start.7 = (f32[432,128]{1,0:T(8,128)S(1)}, f32[432,128]{1,0:T(8,128)S(1)}, u32[]{:S(2)}, u32[]{:S(2)}) collective-permute-start(f32[432,128]{1,0:T(8,128)S(1)} %get-tuple-element.67.refs_6_.refs_10_), channel_id=1, source_target_pairs={{1,0},{2,1},{3,2},{5,4},{6,5},{7,6},{9,8},{10,9},{11,10},{13,12},{... | collective-permute-start | bytes 663560 | tf_op jit(solution)/shard_map/ppermute | solution.py:373
  87.5 50.8 %collective-permute-start.8 = (f32[288,128]{1,0:T(8,128)S(1)}, f32[288,128]{1,0:T(8,128)S(1)}, u32[]{:S(2)}, u32[]{:S(2)}) collective-permute-start(f32[288,128]{1,0:T(8,128)S(1)} %get-tuple-element.69.refs_5_), channel_id=1, source_target_pairs={{0,4},{4,8},{8,12},{12,16},{16,20},{20,24},{24,28},{1,5},{5,9},{9,... | collective-permute-start | bytes 442376 | tf_op jit(solution)/shard_map/ppermute | solution.py:373
  92.0 46.4 %collective-permute-start.9 = (f32[288,128]{1,0:T(8,128)S(1)}, f32[288,128]{1,0:T(8,128)S(1)}, u32[]{:S(2)}, u32[]{:S(2)}) collective-permute-start(f32[288,128]{1,0:T(8,128)S(1)} %get-tuple-element.70.refs_4_), channel_id=1, source_target_pairs={{4,0},{8,4},{12,8},{16,12},{20,16},{24,20},{28,24},{5,1},{9,5},{13... | collective-permute-start | bytes 442376 | tf_op jit(solution)/shard_map/ppermute | solution.py:373
  93.2 45.1 %collective-permute-start.10 = (f32[288,128]{1,0:T(8,128)S(1)}, f32[288,128]{1,0:T(8,128)S(1)}, u32[]{:S(2)}, u32[]{:S(2)}) collective-permute-start(f32[288,128]{1,0:T(8,128)S(1)} %get-tuple-element.71.refs_7_), channel_id=1, source_target_pairs={{0,1},{1,2},{2,3},{4,5},{5,6},{6,7},{8,9},{9,10},{10,11},{12,13},{... | collective-permute-start | bytes 442376 | tf_op jit(solution)/shard_map/ppermute | solution.py:373
  95.4 43.0 %collective-permute-start.11 = (f32[288,128]{1,0:T(8,128)S(1)}, f32[288,128]{1,0:T(8,128)S(1)}, u32[]{:S(2)}, u32[]{:S(2)}) collective-permute-start(f32[288,128]{1,0:T(8,128)S(1)} %get-tuple-element.72.refs_6_), channel_id=1, source_target_pairs={{1,0},{2,1},{3,2},{5,4},{6,5},{7,6},{9,8},{10,9},{11,10},{13,12},{... | collective-permute-start | bytes 442376 | tf_op jit(solution)/shard_map/ppermute | solution.py:373
  143.0 47.7 %collective-permute-start.12 = (f32[288,128]{1,0:T(8,128)S(1)}, f32[288,128]{1,0:T(8,128)S(1)}, u32[]{:S(2)}, u32[]{:S(2)}) collective-permute-start(f32[288,128]{1,0:T(8,128)S(1)} %get-tuple-element.76.refs_5_), channel_id=1, source_target_pairs={{0,4},{4,8},{8,12},{12,16},{16,20},{20,24},{24,28},{1,5},{5,9},{9,... | collective-permute-start | bytes 442376 | tf_op jit(solution)/shard_map/ppermute | solution.py:373
  144.3 46.4 %collective-permute-start.13 = (f32[288,128]{1,0:T(8,128)S(1)}, f32[288,128]{1,0:T(8,128)S(1)}, u32[]{:S(2)}, u32[]{:S(2)}) collective-permute-start(f32[288,128]{1,0:T(8,128)S(1)} %get-tuple-element.77.refs_4_), channel_id=1, source_target_pairs={{4,0},{8,4},{12,8},{16,12},{20,16},{24,20},{28,24},{5,1},{9,5},{13... | collective-permute-start | bytes 442376 | tf_op jit(solution)/shard_map/ppermute | solution.py:373
  145.6 45.1 %collective-permute-start.14 = (f32[288,128]{1,0:T(8,128)S(1)}, f32[288,128]{1,0:T(8,128)S(1)}, u32[]{:S(2)}, u32[]{:S(2)}) collective-permute-start(f32[288,128]{1,0:T(8,128)S(1)} %get-tuple-element.78.refs_7_), channel_id=1, source_target_pairs={{0,1},{1,2},{2,3},{4,5},{5,6},{6,7},{8,9},{9,10},{10,11},{12,13},{... | collective-permute-start | bytes 442376 | tf_op jit(solution)/shard_map/ppermute | solution.py:373
  147.9 42.9 %collective-permute-start.15 = (f32[288,128]{1,0:T(8,128)S(1)}, f32[288,128]{1,0:T(8,128)S(1)}, u32[]{:S(2)}, u32[]{:S(2)}) collective-permute-start(f32[288,128]{1,0:T(8,128)S(1)} %get-tuple-element.79.refs_6_), channel_id=1, source_target_pairs={{1,0},{2,1},{3,2},{5,4},{6,5},{7,6},{9,8},{10,9},{11,10},{13,12},{... | collective-permute-start | bytes 442376 | tf_op jit(solution)/shard_map/ppermute | solution.py:373
  195.5 47.5 %collective-permute-start.16 = (f32[288,128]{1,0:T(8,128)S(1)}, f32[288,128]{1,0:T(8,128)S(1)}, u32[]{:S(2)}, u32[]{:S(2)}) collective-permute-start(f32[288,128]{1,0:T(8,128)S(1)} %get-tuple-element.83.refs_5_), channel_id=1, source_target_pairs={{0,4},{4,8},{8,12},{12,16},{16,20},{20,24},{24,28},{1,5},{5,9},{9,... | collective-permute-start | bytes 442376 | tf_op jit(solution)/shard_map/ppermute | solution.py:373
  196.8 46.2 %collective-permute-start.17 = (f32[288,128]{1,0:T(8,128)S(1)}, f32[288,128]{1,0:T(8,128)S(1)}, u32[]{:S(2)}, u32[]{:S(2)}) collective-permute-start(f32[288,128]{1,0:T(8,128)S(1)} %get-tuple-element.84.refs_4_), channel_id=1, source_target_pairs={{4,0},{8,4},{12,8},{16,12},{20,16},{24,20},{28,24},{5,1},{9,5},{13... | collective-permute-start | bytes 442376 | tf_op jit(solution)/shard_map/ppermute | solution.py:373
  198.1 44.9 %collective-permute-start.18 = (f32[288,128]{1,0:T(8,128)S(1)}, f32[288,128]{1,0:T(8,128)S(1)}, u32[]{:S(2)}, u32[]{:S(2)}) collective-permute-start(f32[288,128]{1,0:T(8,128)S(1)} %get-tuple-element.85.refs_7_), channel_id=1, source_target_pairs={{0,1},{1,2},{2,3},{4,5},{5,6},{6,7},{8,9},{9,10},{10,11},{12,13},{... | collective-permute-start | bytes 442376 | tf_op jit(solution)/shard_map/ppermute | solution.py:373
  200.3 42.7 %collective-permute-start.19 = (f32[288,128]{1,0:T(8,128)S(1)}, f32[288,128]{1,0:T(8,128)S(1)}, u32[]{:S(2)}, u32[]{:S(2)}) collective-permute-start(f32[288,128]{1,0:T(8,128)S(1)} %get-tuple-element.86.refs_6_), channel_id=1, source_target_pairs={{1,0},{2,1},{3,2},{5,4},{6,5},{7,6},{9,8},{10,9},{11,10},{13,12},{... | collective-permute-start | bytes 442376 | tf_op jit(solution)/shard_map/ppermute | solution.py:373
  247.7 47.5 %collective-permute-start.20 = (f32[288,128]{1,0:T(8,128)S(1)}, f32[288,128]{1,0:T(8,128)S(1)}, u32[]{:S(2)}, u32[]{:S(2)}) collective-permute-start(f32[288,128]{1,0:T(8,128)S(1)} %get-tuple-element.90.refs_5_), channel_id=1, source_target_pairs={{0,4},{4,8},{8,12},{12,16},{16,20},{20,24},{24,28},{1,5},{5,9},{9,... | collective-permute-start | bytes 442376 | tf_op jit(solution)/shard_map/ppermute | solution.py:373
  249.0 46.2 %collective-permute-start.21 = (f32[288,128]{1,0:T(8,128)S(1)}, f32[288,128]{1,0:T(8,128)S(1)}, u32[]{:S(2)}, u32[]{:S(2)}) collective-permute-start(f32[288,128]{1,0:T(8,128)S(1)} %get-tuple-element.91.refs_4_), channel_id=1, source_target_pairs={{4,0},{8,4},{12,8},{16,12},{20,16},{24,20},{28,24},{5,1},{9,5},{13... | collective-permute-start | bytes 442376 | tf_op jit(solution)/shard_map/ppermute | solution.py:373
  250.3 44.9 %collective-permute-start.22 = (f32[288,128]{1,0:T(8,128)S(1)}, f32[288,128]{1,0:T(8,128)S(1)}, u32[]{:S(2)}, u32[]{:S(2)}) collective-permute-start(f32[288,128]{1,0:T(8,128)S(1)} %get-tuple-element.92.refs_7_), channel_id=1, source_target_pairs={{0,1},{1,2},{2,3},{4,5},{5,6},{6,7},{8,9},{9,10},{10,11},{12,13},{... | collective-permute-start | bytes 442376 | tf_op jit(solution)/shard_map/ppermute | solution.py:373
  252.6 42.7 %collective-permute-start.23 = (f32[288,128]{1,0:T(8,128)S(1)}, f32[288,128]{1,0:T(8,128)S(1)}, u32[]{:S(2)}, u32[]{:S(2)}) collective-permute-start(f32[288,128]{1,0:T(8,128)S(1)} %get-tuple-element.93.refs_6_), channel_id=1, source_target_pairs={{1,0},{2,1},{3,2},{5,4},{6,5},{7,6},{9,8},{10,9},{11,10},{13,12},{... | collective-permute-start | bytes 442376 | tf_op jit(solution)/shard_map/ppermute | solution.py:373
where the time goes:
time: 340 us; the launch traced here: 339 us
  blocking collectives  244 us (72%)
  starting transfers between devices  44.9 us (13%)
  Pallas kernels  34.6 us (10%)
  local copies, waits for them, and re-layouts  8.53 us (3%)
  waiting for transfers between devices  5.2 us (2%)
    all_gather x6, blocking collectives, everywhere(): return lax.all_gather(block, ('sub', 'layer'), axis=0, tiled=True)  244 us
    ppermute x24, starting transfers between devices, exchange(): lax.ppermute(blocks[side + 1 - 2 * (side % 2)], axis, pairs)  44.9 us
    pallas_call x10, Pallas kernels, call(): pl.pallas_call(kernel, name=name, out_shape=[jax.ShapeDtypeStruct(shape,...  34.6 us
    unnamed x21, local copies, waits for them, and re-layouts  8.53 us
  transfers between devices with their start and end apart: 24, of which 1 were waited for; matrix products, arithmetic and copies ran while one was open for 0% of the time, Pallas kernels for 0%

commit v1 on v0

--- a/solution.py
+++ b/solution.py
@@ -108,10 +108,22 @@
     return halves(one_pass(a_high, both)) + one_pass(a_low, b_high)
 
 
-def modes_kernel(mode_count, codes_row, modes, inverse, load, *outs):
+def copies(ref, block):
+    rows = block.shape[0]
+    for q in range(ref.shape[0] // rows):
+        ref[q * rows : (q + 1) * rows, :] = block
+
+
+def modes_kernel(mode_count, codes_row, modes, inverse, load, place, *outs):
     total = codes_row.shape[1]
     cap = total // SIDES
-    codes = jnp.broadcast_to(codes_row[...], (128, total)).astype(jnp.float32)
+    codes = codes_row[...]
+    heading = codes // cap
+    even = jnp.where(heading < 2, 1 - lax.rem(place[0], 2), 1 - lax.rem(place[1], 2))
+    turn = jnp.where(heading < SIDES, even * (1 - 2 * (heading % 2)), 0)
+    codes = codes + turn * cap
+    outs[SIDES + 3][...] = codes
+    codes = jnp.broadcast_to(codes, (128, total)).astype(jnp.float32)
     codes_lanes = jnp.transpose(codes).astype(jnp.int32)
     x = jnp.concatenate(
         [modes[...], jnp.zeros((PAD - mode_count, total), jnp.float32)], axis=0
@@ -134,13 +146,14 @@
     wide = exact(jnp.concatenate([inverse[...], blank], axis=0), spread)
     blank = jnp.zeros((PAD - mode_count, load.shape[1]), jnp.float32)
     loads = jnp.concatenate([load[...], blank], axis=0)
-    outs[SIDES][...] = jnp.concatenate([wide, loads], axis=1)
+    copies(outs[SIDES], jnp.concatenate([wide, loads], axis=1))
     outs[SIDES + 1][...] = codes_lanes
     outs[SIDES + 2][...] = jnp.concatenate([upper, lower], axis=0)
 
 
-def around(place, layers):
-    return [place, place - layers, place + layers, place - 1, place + 1]
+def around(i, j):
+    right, up = 1 - 2 * (i % 2), 1 - 2 * (j % 2)
+    return [(i, j), (i + right, j), (i - right, j), (i, j + up), (i, j - up)]
 
 
 def mode_blocks(own, partner):
@@ -202,12 +215,11 @@
     slot_pieces, row_pieces, out_pieces = refs[13:16]
     cap = codes_lanes.shape[0] // SIDES
     wide = gathered.shape[0]
-    place = place_ref[0]
     spread = lane_spread(mode_count, GROUP)
-    for n, centre in enumerate(around(place, layers)):
+    for n, centre in enumerate(around(place_ref[0], place_ref[1])):
         rows = []
-        for near in around(centre, layers):
-            first = jnp.clip(near, 0, wide // PAD - 1) * PAD
+        for i, j in around(*centre):
+            first = jnp.clip(i * layers + j, 0, wide // PAD - 1) * PAD
             rows.append(gathered[pl.ds(pl.multiple_of(first, PAD), PAD), 0:wide])
         table = jnp.concatenate(rows, axis=0)
         inverse_out[n * GROUP : (n + 1) * GROUP, :] = exact(spread, table, ((0,), (0,)))
@@ -256,7 +268,7 @@
         block = sent[side][0:cap, :] - received[side][0:cap, :]
         gap_out[side * cap : (side + 1) * cap, :] = block
         fill_pieces(slot_pieces, side * cap, block)
-    parts_out[...] = components_of(own, slot_pieces)
+    copies(parts_out, components_of(own, slot_pieces))
 
     def write(side, block):
         outs[side][...] = block
@@ -318,7 +330,7 @@
         if nextin is not None:
             fill_pieces(slot_pieces, side * cap, nextin)
         fill_pieces(out_pieces, side * cap, block)
-    parts_out[...] = components_of(own, out_pieces)
+    copies(parts_out, components_of(own, out_pieces))
     if stage < 5:
 
         def write(side, block):
@@ -363,19 +375,17 @@
 
 def exchange(blocks):
     received = []
-    for side in range(SIDES):
+    for side, block in enumerate(blocks):
         axis = "sub" if side < 2 else "layer"
-        count = lax.axis_size(axis)
-        if side % 2 == 0:
-            pairs = [(i, i + 1) for i in range(count - 1)]
-        else:
-            pairs = [(i + 1, i) for i in range(count - 1)]
-        received.append(lax.ppermute(blocks[side + 1 - 2 * (side % 2)], axis, pairs))
+        pairs = []
+        for i in range(side % 2, lax.axis_size(axis) - 1, 2):
+            pairs += [(i, i + 1), (i + 1, i)]
+        received.append(lax.ppermute(block, axis, pairs))
     return received
 
 
-def everywhere(block):
-    return lax.all_gather(block, ("sub", "layer"), axis=0, tiled=True)
+def everywhere(stacked):
+    return lax.all_to_all(stacked, ("sub", "layer"), split_axis=0, concat_axis=0, tiled=True)
 
 
 def per_device(
@@ -388,26 +398,27 @@
     mode_count, total = modes.shape
     cap = total // SIDES
     cols = gap.shape[1]
-    codes_row = route_codes[0]
     layers = lax.axis_size("layer")
     wide = lax.axis_size("sub") * layers * PAD
-    place = (lax.axis_index("sub") * layers + lax.axis_index("layer")).astype(jnp.int32)[None]
+    place = jnp.stack([lax.axis_index("sub"), lax.axis_index("layer")]).astype(jnp.int32)
     pieces = pltpu.VMEM((total, 2 * cols), jnp.bfloat16)
     scratch = [pieces] * 3
     block = [(cap, cols)] * SIDES
     whole = (total, cols)
-    parts = (PAD, cols)
+    parts = (wide, cols)
     table = 8 * wide * (wide + cols)
 
     shown = call(
         functools.partial(modes_kernel, mode_count),
         "modes_to_slots",
         [(PAD, cap)] * SIDES
-        + [(PAD, wide + cols), jax.ShapeDtypeStruct((total, 128), jnp.int32), (2 * PAD, total)],
-        [codes_row, modes, coarse_inverse, rigid_load],
+        + [(wide, wide + cols), jax.ShapeDtypeStruct((total, 128), jnp.int32), (2 * PAD, total)]
+        + [jax.ShapeDtypeStruct((1, total), jnp.int32)],
+        [route_codes[0], modes, coarse_inverse, rigid_load, place],
+        smem=(4,),
         extra=table,
     )
-    own, (inverse_load, codes_lanes, own_pieces) = shown[:4], shown[4:]
+    own, (inverse_load, codes_lanes, own_pieces, codes_row) = shown[:4], shown[4:]
     gathered = everywhere(inverse_load)
     partner = exchange(own)
     shown = call(

time: 340 us -> 225 us (0.66)
  blocking collectives: 244 us -> 0 us
  local copies, waits for them, and re-layouts: 8.53 us -> 87.4 us
  starting transfers between devices: 44.9 us -> 69.8 us
  waiting for transfers between devices: 5.2 us -> 28.4 us
    all_gather x6 -> x0, blocking collectives: 244 us -> none  [everywhere(): return lax.all_gather(block, ('sub', 'layer'), axis=0, tiled=True)]
    unnamed x21 -> x195, local copies, waits for them, and re-layouts: 8.53 us -> 87.4 us
    all_to_all x0 -> x6, starting transfers between devices: none -> 44.3 us  [everywhere(): lax.all_to_all(stacked, ('sub', 'layer'), split_axis=0, concat_axis=0, ti...]
    ppermute x24, waiting for transfers between devices: 5.2 us -> 25.9 us  [exchange(): received.append(lax.ppermute(block, axis, pairs))]
    ppermute x24, starting transfers between devices: 44.9 us -> 25.5 us  [exchange(): received.append(lax.ppermute(block, axis, pairs))]
  transfers between devices with their start and end apart: 24 -> 30, of which waited for: 1 -> 7; matrix products, arithmetic and copies ran while one was open for 0% -> 0% of each run, Pallas kernels for 0% -> 4%
where the time goes in v1:
time: 225 us; the launch traced here: 223 us
  local copies, waits for them, and re-layouts  87.4 us (39%)
  starting transfers between devices  69.8 us (31%)
  Pallas kernels  35.9 us (16%)
  waiting for transfers between devices  28.4 us (13%)
    unnamed x195, local copies, waits for them, and re-layouts  87.4 us
    all_to_all x6, starting transfers between devices, everywhere(): lax.all_to_all(stacked, ('sub', 'layer'), split_axis=0, concat_axis=0, ti...  44.3 us
    pallas_call x10, Pallas kernels, call(): pl.pallas_call(kernel, name=name, out_shape=[jax.ShapeDtypeStruct(shape,...  35.9 us
    ppermute x24, waiting for transfers between devices, exchange(): received.append(lax.ppermute(block, axis, pairs))  25.9 us
    ppermute x24, starting transfers between devices, exchange(): received.append(lax.ppermute(block, axis, pairs))  25.5 us
  transfers between devices with their start and end apart: 30, of which 7 were waited for; matrix products, arithmetic and copies ran while one was open for 0% of the time, Pallas kernels for 4%

profile of v1, /device:TPU:0, one launch (start us, length us, event | category | flops | bytes accessed | tf_op | source)
XLA Modules:
  0.0 222.6 jit_solution(18257753077252721785)
XLA Ops:
  3.5 2.2 modes_to_slots.1
  5.7 7.3 %all-to-all-start = ((f32[32,8,384]{2,1,0:T(8,128)}), f32[32,8,384]{2,1,0:T(8,128)S(1)}, u32[]{:S(2)}, u32[]{:S(2)}) async-start(f32[32,8,384]{2,1,0:T(8,128)} %bitcast.6), calls=%async_computation | async-start | bytes 786432 | tf_op jit(solution)/shard_map/all_to_all | solution.py:388
  13.0 1.8 collective-permute-start
  16.3 1.3 collective-permute-done.refs_4_
  17.6 2.5 %copy-done = f32[1,1,1152,1152]{3,2,1,0:T(8,128)S(1)} copy-done((f32[1,1,1152,1152]{3,2,1,0:T(8,128)S(1)}, f32[1,1,1152,1152]{3,2,1,0:T(8,128)}, u32[]{:S(2)}) %copy-start) | copy-done | bytes 5308440
  20.1 2.5 %copy-done.4 = f32[1,1,1152,1152]{3,2,1,0:T(8,128)S(1)} copy-done((f32[1,1,1152,1152]{3,2,1,0:T(8,128)S(1)}, f32[1,1,1152,1152]{3,2,1,0:T(8,128)}, u32[]{:S(2)}) %copy-start.4) | copy-done | bytes 5308440
  22.6 6.0 %operators_on_modes.1 = (f32[144,128]{1,0:T(8,128)S(1)}, f32[144,128]{1,0:T(8,128)S(1)}, f32[144,128]{1,0:T(8,128)S(1)}, f32[144,128]{1,0:T(8,128)S(1)}, f32[1152,128]{1,0:T(8,128)S(1)}) custom-call(f32[1152,1152]{1,0:T(8,128)S(1)} %bitcast.23, f32[1152,1152]{1,0:T(8,128)S(1)} %bitcast.27, s32[1,1152]{1,0:T(1,128)S(1)} %get-tuple-element.55.codes_row, ...), custom_call_target="tpu_custom_call" | custom-call | tf_op jit(solution)/shard_map/operators_on_modes/pallas_call | solution.py:365
  28.6 2.5 %copy-done.1 = f32[1,1,1152,1152]{3,2,1,0:T(8,128)S(1)} copy-done((f32[1,1,1152,1152]{3,2,1,0:T(8,128)S(1)}, f32[1,1,1152,1152]{3,2,1,0:T(8,128)}, u32[]{:S(2)}) %copy-start.1) | copy-done | bytes 5308440
  31.1 1.1 copy-done.28
  32.2 4.5 %start.1 = (f32[432,128]{1,0:T(8,128)S(1)}, f32[432,128]{1,0:T(8,128)S(1)}, f32[432,128]{1,0:T(8,128)S(1)}, f32[432,128]{1,0:T(8,128)S(1)}, f32[1152,128]{1,0:T(8,128)S(1)}, /*index=5*/f32[160,256]{1,0:T(8,128)S(1)}) custom-call(f32[1152,1152]{1,0:T(8,128)S(1)} %bitcast.24, f32[1152,128]{1,0:T(8,128)S(1)} %bitcast.31, ...), custom_call_target="tpu_custom_call" | custom-call | tf_op jit(solution)/shard_map/start/pallas_call | solution.py:365
  36.6 4.5 %collective-permute-start.4 = (f32[432,128]{1,0:T(8,128)S(1)}, f32[432,128]{1,0:T(8,128)S(1)}, u32[]{:S(2)}, u32[]{:S(2)}) collective-permute-start(f32[432,128]{1,0:T(8,128)S(1)} %get-tuple-element.66.refs_4_.refs_8_), channel_id=1, source_target_pairs={{0,4},{4,0},{8,12},{12,8},{16,20},{20,16},{24,28},{28,24},{1,5},{5... | collective-permute-start | bytes 663560 | tf_op jit(solution)/shard_map/ppermute | solution.py:383
  41.8 3.2 %collective-permute-start.6 = (f32[432,128]{1,0:T(8,128)S(1)}, f32[432,128]{1,0:T(8,128)S(1)}, u32[]{:S(2)}, u32[]{:S(2)}) collective-permute-start(f32[432,128]{1,0:T(8,128)S(1)} %get-tuple-element.68.refs_6_.refs_10_), channel_id=1, source_target_pairs={{0,1},{1,0},{2,3},{3,2},{4,5},{5,4},{6,7},{7,6},{8,9},{9,8},{10,11... | collective-permute-start | bytes 663560 | tf_op jit(solution)/shard_map/ppermute | solution.py:383
  46.1 3.3 %stage_1.1 = (f32[288,128]{1,0:T(8,128)S(1)}, f32[288,128]{1,0:T(8,128)S(1)}, f32[288,128]{1,0:T(8,128)S(1)}, f32[288,128]{1,0:T(8,128)S(1)}, f32[1152,128]{1,0:T(8,128)S(1)}, /*index=5*/f32[256,128]{1,0:T(8,128)S(1)}) custom-call(f32[1152,1152]{1,0:T(8,128)S(1)} %bitcast.28, s32[1,1152]{1,0:T(1,128)S(1)} %get-tuple-element.55.codes_row, ...), custom_call_target="tpu_custom_call" | custom-call | tf_op jit(solution)/shard_map/stage_1/pallas_call | solution.py:365
  52.9 13.4 %all-to-all-start.1 = ((f32[32,8,128]{2,1,0:T(8,128)}), f32[32,8,128]{2,1,0:T(8,128)S(1)}, u32[]{:S(2)}, u32[]{:S(2)}) async-start(f32[32,8,128]{2,1,0:T(8,128)} %bitcast.41), calls=%async_computation.1 | async-start | bytes 262144 | tf_op jit(solution)/shard_map/all_to_all | solution.py:388
  66.3 1.8 collective-permute-start.8
  69.6 6.0 %collective-permute-done.8.refs_0_ = f32[288,128]{1,0:T(8,128)S(1)} collective-permute-done((f32[288,128]{1,0:T(8,128)S(1)}, f32[288,128]{1,0:T(8,128)S(1)}, u32[]{:S(2)}, u32[]{:S(2)}) %collective-permute-start.8) | collective-permute-done | bytes 147488 | tf_op jit(solution)/shard_map/ppermute | solution.py:383
  78.3 2.5 %copy-done.2 = f32[1,1,1152,1152]{3,2,1,0:T(8,128)S(1)} copy-done((f32[1,1,1152,1152]{3,2,1,0:T(8,128)S(1)}, f32[1,1,1152,1152]{3,2,1,0:T(8,128)}, u32[]{:S(2)}) %copy-start.2) | copy-done | bytes 5308440
  80.8 1.1 copy-done.23
  81.8 0.9 copy-done.58
  89.1 4.5 %stage_2.1 = (f32[288,128]{1,0:T(8,128)S(1)}, f32[288,128]{1,0:T(8,128)S(1)}, f32[288,128]{1,0:T(8,128)S(1)}, f32[288,128]{1,0:T(8,128)S(1)}, f32[1152,128]{1,0:...) custom-call(f32[1152,1152]{1,0:T(8,128)S(1)} %bitcast.25, s32[1,1152]{1,0:T(1,128)S(1)} %get-tuple-element.55.codes_row, ...), custom_call_target="tpu_custom_call" | custom-call | tf_op jit(solution)/shard_map/stage_2/pallas_call | solution.py:365
  97.9 5.9 %all-to-all-start.2 = ((f32[32,8,128]{2,1,0:T(8,128)}), f32[32,8,128]{2,1,0:T(8,128)S(1)}, u32[]{:S(2)}, u32[]{:S(2)}) async-start(f32[32,8,128]{2,1,0:T(8,128)} %bitcast.39), calls=%async_computation.2 | async-start | bytes 262144 | tf_op jit(solution)/shard_map/all_to_all | solution.py:388
  103.8 1.8 collective-permute-start.12
  107.3 5.8 %collective-permute-done.12.refs_0_ = f32[288,128]{1,0:T(8,128)S(1)} collective-permute-done((f32[288,128]{1,0:T(8,128)S(1)}, f32[288,128]{1,0:T(8,128)S(1)}, u32[]{:S(2)}, u32[]{:S(2)}) %collective-permute-start.12) | collective-permute-done | bytes 147488 | tf_op jit(solution)/shard_map/ppermute | solution.py:383
  115.8 2.5 %copy-done.6 = f32[1,1,1152,1152]{3,2,1,0:T(8,128)S(1)} copy-done((f32[1,1,1152,1152]{3,2,1,0:T(8,128)S(1)}, f32[1,1,1152,1152]{3,2,1,0:T(8,128)}, u32[]{:S(2)}) %copy-start.6) | copy-done | bytes 5308440
  118.3 1.1 copy-done.19
  119.3 1.1 copy-done.21
  126.8 4.6 %stage_3.1 = (f32[288,128]{1,0:T(8,128)S(1)}, f32[288,128]{1,0:T(8,128)S(1)}, f32[288,128]{1,0:T(8,128)S(1)}, f32[288,128]{1,0:T(8,128)S(1)}, f32[1152,128]{1,0:...) custom-call(f32[1152,1152]{1,0:T(8,128)S(1)} %bitcast.29, s32[1,1152]{1,0:T(1,128)S(1)} %get-tuple-element.55.codes_row, ...), custom_call_target="tpu_custom_call" | custom-call | tf_op jit(solution)/shard_map/stage_3/pallas_call | solution.py:365
  136.3 5.9 %all-to-all-start.3 = ((f32[32,8,128]{2,1,0:T(8,128)}), f32[32,8,128]{2,1,0:T(8,128)S(1)}, u32[]{:S(2)}, u32[]{:S(2)}) async-start(f32[32,8,128]{2,1,0:T(8,128)} %bitcast.38), calls=%async_computation.3 | async-start | bytes 262144 | tf_op jit(solution)/shard_map/all_to_all | solution.py:388
  142.2 1.8 collective-permute-start.16
  145.4 6.4 %collective-permute-done.16.refs_0_ = f32[288,128]{1,0:T(8,128)S(1)} collective-permute-done((f32[288,128]{1,0:T(8,128)}, f32[288,128]{1,0:T(8,128)S(1)}, u32[]{:S(2)}, u32[]{:S(2)}) %collective-permute-start.16) | collective-permute-done | bytes 147488 | tf_op jit(solution)/shard_map/ppermute | solution.py:383
  154.4 2.5 %copy-done.3 = f32[1,1,1152,1152]{3,2,1,0:T(8,128)S(1)} copy-done((f32[1,1,1152,1152]{3,2,1,0:T(8,128)S(1)}, f32[1,1,1152,1152]{3,2,1,0:T(8,128)}, u32[]{:S(2)}) %copy-start.3) | copy-done | bytes 5308440
  156.9 1.1 copy-done.8
  158.0 1.1 copy-done.17
  166.3 4.6 %stage_4.1 = (f32[288,128]{1,0:T(8,128)S(1)}, f32[288,128]{1,0:T(8,128)S(1)}, f32[288,128]{1,0:T(8,128)S(1)}, f32[288,128]{1,0:T(8,128)S(1)}, f32[1152,128]{1,0:...) custom-call(f32[1152,1152]{1,0:T(8,128)S(1)} %bitcast.26, s32[1,1152]{1,0:T(1,128)S(1)} %get-tuple-element.55.codes_row, ...), custom_call_target="tpu_custom_call" | custom-call | tf_op jit(solution)/shard_map/stage_4/pallas_call | solution.py:365
  175.2 5.6 %all-to-all-start.4 = ((f32[32,8,128]{2,1,0:T(8,128)}), f32[32,8,128]{2,1,0:T(8,128)S(1)}, u32[]{:S(2)}, u32[]{:S(2)}) async-start(f32[32,8,128]{2,1,0:T(8,128)} %bitcast.40), calls=%async_computation.4 | async-start | bytes 262144 | tf_op jit(solution)/shard_map/all_to_all | solution.py:388
  180.8 1.8 collective-permute-start.20
  184.0 6.0 %collective-permute-done.20.refs_0_ = f32[288,128]{1,0:T(8,128)S(1)} collective-permute-done((f32[288,128]{1,0:T(8,128)S(1)}, f32[288,128]{1,0:T(8,128)S(1)}, u32[]{:S(2)}, u32[]{:S(2)}) %collective-permute-start.20) | collective-permute-done | bytes 147488 | tf_op jit(solution)/shard_map/ppermute | solution.py:383
  192.7 1.1 copy-done.9
  193.8 1.1 copy-done.11
  194.8 1.1 copy-done.13
  195.9 1.1 copy-done.15
  203.3 1.5 stage_5.1
  207.1 6.2 %all-to-all-start.5 = ((f32[32,8,128]{2,1,0:T(8,128)}), f32[32,8,128]{2,1,0:T(8,128)S(1)}, u32[]{:S(2)}, u32[]{:S(2)}) async-start(f32[32,8,128]{2,1,0:T(8,128)} %bitcast.42), calls=%async_computation.5 | async-start | bytes 262144 | tf_op jit(solution)/shard_map/all_to_all | solution.py:388
  213.3 1.1 copy-done.25
  214.4 1.1 copy-done.27
  215.4 3.3 %slots_to_rows.1 = (f32[1152,128]{1,0:T(8,128)S(1)}, f32[1152,128]{1,0:T(8,128)}, f32[1152,128]{1,0:T(8,128)S(1)}) custom-call(s32[1152,128]{1,0:T(8,128)S(1)} %get-tuple-element.54.codes_lanes, f32[1152,128]{1,0:T(8,128)S(1)} %copy-done.25, f32[1152,128]{1,0:T(8,128)S(1)} %copy-done.27, f32[1152,128]{1,0:T(8,128)S(1)} %get-tuple-element.65.refs_5_.refs_19_.modes), custom_call_target="tpu_custom_call" | custom-call | tf_op jit(solution)/shard_map/slots_to_rows/pallas_call | solution.py:365
  218.8 2.5 %all-to-all-done.5 = f32[32,8,128]{2,1,0:T(8,128)S(1)} async-done(((f32[32,8,128]{2,1,0:T(8,128)}), f32[32,8,128]{2,1,0:T(8,128)S(1)}, u32[]{:S(2)}, u32[]{:S(2)}) %all-to-all-start.5) | async-done | bytes 131104 | tf_op jit(solution)/shard_map/all_to_all | solution.py:388
  221.3 1.4 residual.1
  (218 shorter events, 67.9 us)
Async XLA Ops:
  5.7 22.9 %all-to-all-start = ((f32[32,8,384]{2,1,0:T(8,128)}), f32[32,8,384]{2,1,0:T(8,128)S(1)}, u32[]{:S(2)}, u32[]{:S(2)}) async-start(f32[32,8,384]{2,1,0:T(8,128)} %bitcast.6), calls=%async_computation | async-start | bytes 786432 | tf_op jit(solution)/shard_map/all_to_all | solution.py:388
  13.0 4.5 %collective-permute-start = (f32[8,288]{1,0:T(8,128)S(1)}, f32[8,288]{1,0:T(8,128)S(1)}, u32[]{:S(2)}, u32[]{:S(2)}) collective-permute-start(f32[8,288]{1,0:T(8,128)S(1)} %get-tuple-element.56.refs_0_), channel_id=1, source_target_pairs={{0,4},{4,0},{8,12},{12,8},{16,20},{20,16},{24,28},{28,24},{1,5},{5... | collective-permute-start | bytes 27656 | tf_op jit(solution)/shard_map/ppermute | solution.py:383
  14.9 2.7 %collective-permute-start.1 = (f32[8,288]{1,0:T(8,128)S(1)}, f32[8,288]{1,0:T(8,128)S(1)}, u32[]{:S(2)}, u32[]{:S(2)}) collective-permute-start(f32[8,288]{1,0:T(8,128)S(1)} %get-tuple-element.57.refs_1_), channel_id=1, source_target_pairs={{4,8},{8,4},{12,16},{16,12},{20,24},{24,20},{5,9},{9,5},{13,17},{1... | collective-permute-start | bytes 27656 | tf_op jit(solution)/shard_map/ppermute | solution.py:383
  15.5 2.0 collective-permute-start.2
  15.6 2.0 collective-permute-start.3
  17.6 2.5 %copy-start = (f32[1,1,1152,1152]{3,2,1,0:T(8,128)S(1)}, f32[1,1,1152,1152]{3,2,1,0:T(8,128)}, u32[]{:S(2)}) copy-start(f32[1,1,1152,1152]{3,2,1,0:T(8,128)} %param.9) | copy-start | bytes 15925252
  20.1 2.5 %copy-start.4 = (f32[1,1,1152,1152]{3,2,1,0:T(8,128)S(1)}, f32[1,1,1152,1152]{3,2,1,0:T(8,128)}, u32[]{:S(2)}) copy-start(f32[1,1,1152,1152]{3,2,1,0:T(8,128)} %param.10) | copy-start | bytes 15925252
  28.6 2.5 %copy-start.1 = (f32[1,1,1152,1152]{3,2,1,0:T(8,128)S(1)}, f32[1,1,1152,1152]{3,2,1,0:T(8,128)}, u32[]{:S(2)}) copy-start(f32[1,1,1152,1152]{3,2,1,0:T(8,128)} %param.9) | copy-start | bytes 15925252
  31.1 1.1 copy-start.28
  32.2 13.9 %copy-start.5 = (f32[1,1,1152,1152]{3,2,1,0:T(8,128)S(1)}, f32[1,1,1152,1152]{3,2,1,0:T(8,128)}, u32[]{:S(2)}) copy-start(f32[1,1,1152,1152]{3,2,1,0:T(8,128)} %param.10) | copy-start | bytes 15925252
  36.6 12.8 %copy-start.10 = (f32[1152,128]{1,0:T(8,128)}, f32[1152,128]{1,0:T(8,128)S(1)}, u32[]{:S(2)}) copy-start(f32[1152,128]{1,0:T(8,128)S(1)} %get-tuple-element.99.refs_22_) | copy-start | bytes 1769476
  36.6 9.2 %collective-permute-start.4 = (f32[432,128]{1,0:T(8,128)S(1)}, f32[432,128]{1,0:T(8,128)S(1)}, u32[]{:S(2)}, u32[]{:S(2)}) collective-permute-start(f32[432,128]{1,0:T(8,128)S(1)} %get-tuple-element.66.refs_4_.refs_8_), channel_id=1, source_target_pairs={{0,4},{4,0},{8,12},{12,8},{16,20},{20,16},{24,28},{28,24},{1,5},{5... | collective-permute-start | bytes 663560 | tf_op jit(solution)/shard_map/ppermute | solution.py:383
  41.2 4.7 %collective-permute-start.5 = (f32[432,128]{1,0:T(8,128)S(1)}, f32[432,128]{1,0:T(8,128)S(1)}, u32[]{:S(2)}, u32[]{:S(2)}) collective-permute-start(f32[432,128]{1,0:T(8,128)S(1)} %get-tuple-element.67.refs_5_.refs_9_), channel_id=1, source_target_pairs={{4,8},{8,4},{12,16},{16,12},{20,24},{24,20},{5,9},{9,5},{13,17},{1... | collective-permute-start | bytes 663560 | tf_op jit(solution)/shard_map/ppermute | solution.py:383
  41.8 4.3 %collective-permute-start.6 = (f32[432,128]{1,0:T(8,128)S(1)}, f32[432,128]{1,0:T(8,128)S(1)}, u32[]{:S(2)}, u32[]{:S(2)}) collective-permute-start(f32[432,128]{1,0:T(8,128)S(1)} %get-tuple-element.68.refs_6_.refs_10_), channel_id=1, source_target_pairs={{0,1},{1,0},{2,3},{3,2},{4,5},{5,4},{6,7},{7,6},{8,9},{9,8},{10,11... | collective-permute-start | bytes 663560 | tf_op jit(solution)/shard_map/ppermute | solution.py:383
  45.0 1.1 collective-permute-start.7
  52.9 25.4 %copy-start.57 = (f32[288,128]{1,0:T(8,128)}, f32[288,128]{1,0:T(8,128)S(1)}, u32[]{:S(2)}) copy-start(f32[288,128]{1,0:T(8,128)S(1)} %get-tuple-element.71.refs_4_) | copy-start | bytes 442372
  52.9 25.4 %all-to-all-start.1 = ((f32[32,8,128]{2,1,0:T(8,128)}), f32[32,8,128]{2,1,0:T(8,128)S(1)}, u32[]{:S(2)}, u32[]{:S(2)}) async-start(f32[32,8,128]{2,1,0:T(8,128)} %bitcast.41), calls=%async_computation.1 | async-start | bytes 262144 | tf_op jit(solution)/shard_map/all_to_all | solution.py:388
  66.3 9.3 %collective-permute-start.8 = (f32[288,128]{1,0:T(8,128)S(1)}, f32[288,128]{1,0:T(8,128)S(1)}, u32[]{:S(2)}, u32[]{:S(2)}) collective-permute-start(f32[288,128]{1,0:T(8,128)S(1)} %get-tuple-element.71.refs_4_), channel_id=1, source_target_pairs={{0,4},{4,0},{8,12},{12,8},{16,20},{20,16},{24,28},{28,24},{1,5},{5... | collective-permute-start | bytes 442376 | tf_op jit(solution)/shard_map/ppermute | solution.py:383
  68.1 8.1 %collective-permute-start.9 = (f32[288,128]{1,0:T(8,128)}, f32[288,128]{1,0:T(8,128)S(1)}, u32[]{:S(2)}, u32[]{:S(2)}) collective-permute-start(f32[288,128]{1,0:T(8,128)} %copy-done.59), channel_id=1, source_target_pairs={{4,8},{8,4},{12,16},{16,12},{20,24},{24,20},{5,9},{9,5},{13,17},{1... | collective-permute-start | bytes 442376 | tf_op jit(solution)/shard_map/ppermute | solution.py:383
  68.8 8.1 %collective-permute-start.10 = (f32[288,128]{1,0:T(8,128)}, f32[288,128]{1,0:T(8,128)S(1)}, u32[]{:S(2)}, u32[]{:S(2)}) collective-permute-start(f32[288,128]{1,0:T(8,128)} %copy-done.61), channel_id=1, source_target_pairs={{0,1},{1,0},{2,3},{3,2},{4,5},{5,4},{6,7},{7,6},{8,9},{9,8},{10,11... | collective-permute-start | bytes 442376 | tf_op jit(solution)/shard_map/ppermute | solution.py:383
  68.9 8.7 %collective-permute-start.11 = (f32[288,128]{1,0:T(8,128)}, f32[288,128]{1,0:T(8,128)S(1)}, u32[]{:S(2)}, u32[]{:S(2)}) collective-permute-start(f32[288,128]{1,0:T(8,128)} %copy-done.63), channel_id=1, source_target_pairs={{1,2},{2,1},{5,6},{6,5},{9,10},{10,9},{13,14},{14,13},{17,18},{18,... | collective-permute-start | bytes 442376 | tf_op jit(solution)/shard_map/ppermute | solution.py:383
  78.3 2.5 %copy-start.2 = (f32[1,1,1152,1152]{3,2,1,0:T(8,128)S(1)}, f32[1,1,1152,1152]{3,2,1,0:T(8,128)}, u32[]{:S(2)}) copy-start(f32[1,1,1152,1152]{3,2,1,0:T(8,128)} %param.9) | copy-start | bytes 15925252
  80.8 1.1 copy-start.23
  97.9 17.8 %all-to-all-start.2 = ((f32[32,8,128]{2,1,0:T(8,128)}), f32[32,8,128]{2,1,0:T(8,128)S(1)}, u32[]{:S(2)}, u32[]{:S(2)}) async-start(f32[32,8,128]{2,1,0:T(8,128)} %bitcast.39), calls=%async_computation.2 | async-start | bytes 262144 | tf_op jit(solution)/shard_map/all_to_all | solution.py:388
  103.8 9.3 %collective-permute-start.12 = (f32[288,128]{1,0:T(8,128)S(1)}, f32[288,128]{1,0:T(8,128)S(1)}, u32[]{:S(2)}, u32[]{:S(2)}) collective-permute-start(f32[288,128]{1,0:T(8,128)S(1)} %get-tuple-element.78.refs_4_), channel_id=1, source_target_pairs={{0,4},{4,0},{8,12},{12,8},{16,20},{20,16},{24,28},{28,24},{1,5},{5... | collective-permute-start | bytes 442376 | tf_op jit(solution)/shard_map/ppermute | solution.py:383
  105.7 8.1 %collective-permute-start.13 = (f32[288,128]{1,0:T(8,128)}, f32[288,128]{1,0:T(8,128)S(1)}, u32[]{:S(2)}, u32[]{:S(2)}) collective-permute-start(f32[288,128]{1,0:T(8,128)} %copy-done.51), channel_id=1, source_target_pairs={{4,8},{8,4},{12,16},{16,12},{20,24},{24,20},{5,9},{9,5},{13,17},{1... | collective-permute-start | bytes 442376 | tf_op jit(solution)/shard_map/ppermute | solution.py:383
  106.3 8.1 %collective-permute-start.14 = (f32[288,128]{1,0:T(8,128)}, f32[288,128]{1,0:T(8,128)S(1)}, u32[]{:S(2)}, u32[]{:S(2)}) collective-permute-start(f32[288,128]{1,0:T(8,128)} %copy-done.53), channel_id=1, source_target_pairs={{0,1},{1,0},{2,3},{3,2},{4,5},{5,4},{6,7},{7,6},{8,9},{9,8},{10,11... | collective-permute-start | bytes 442376 | tf_op jit(solution)/shard_map/ppermute | solution.py:383
  106.4 8.7 %collective-permute-start.15 = (f32[288,128]{1,0:T(8,128)}, f32[288,128]{1,0:T(8,128)S(1)}, u32[]{:S(2)}, u32[]{:S(2)}) collective-permute-start(f32[288,128]{1,0:T(8,128)} %copy-done.55), channel_id=1, source_target_pairs={{1,2},{2,1},{5,6},{6,5},{9,10},{10,9},{13,14},{14,13},{17,18},{18,... | collective-permute-start | bytes 442376 | tf_op jit(solution)/shard_map/ppermute | solution.py:383
  115.8 2.5 %copy-start.6 = (f32[1,1,1152,1152]{3,2,1,0:T(8,128)S(1)}, f32[1,1,1152,1152]{3,2,1,0:T(8,128)}, u32[]{:S(2)}) copy-start(f32[1,1,1152,1152]{3,2,1,0:T(8,128)} %param.10) | copy-start | bytes 15925252
  118.3 1.1 copy-start.19
  119.3 1.1 copy-start.21
  136.3 18.1 %all-to-all-start.3 = ((f32[32,8,128]{2,1,0:T(8,128)}), f32[32,8,128]{2,1,0:T(8,128)S(1)}, u32[]{:S(2)}, u32[]{:S(2)}) async-start(f32[32,8,128]{2,1,0:T(8,128)} %bitcast.38), calls=%async_computation.3 | async-start | bytes 262144 | tf_op jit(solution)/shard_map/all_to_all | solution.py:388
  142.2 9.6 %collective-permute-start.16 = (f32[288,128]{1,0:T(8,128)}, f32[288,128]{1,0:T(8,128)S(1)}, u32[]{:S(2)}, u32[]{:S(2)}) collective-permute-start(f32[288,128]{1,0:T(8,128)} %copy-done.43), channel_id=1, source_target_pairs={{0,4},{4,0},{8,12},{12,8},{16,20},{20,16},{24,28},{28,24},{1,5},{5... | collective-permute-start | bytes 442376 | tf_op jit(solution)/shard_map/ppermute | solution.py:383
  144.0 8.4 %collective-permute-start.17 = (f32[288,128]{1,0:T(8,128)}, f32[288,128]{1,0:T(8,128)S(1)}, u32[]{:S(2)}, u32[]{:S(2)}) collective-permute-start(f32[288,128]{1,0:T(8,128)} %copy-done.45), channel_id=1, source_target_pairs={{4,8},{8,4},{12,16},{16,12},{20,24},{24,20},{5,9},{9,5},{13,17},{1... | collective-permute-start | bytes 442376 | tf_op jit(solution)/shard_map/ppermute | solution.py:383
  144.7 8.4 %collective-permute-start.18 = (f32[288,128]{1,0:T(8,128)}, f32[288,128]{1,0:T(8,128)S(1)}, u32[]{:S(2)}, u32[]{:S(2)}) collective-permute-start(f32[288,128]{1,0:T(8,128)} %copy-done.47), channel_id=1, source_target_pairs={{0,1},{1,0},{2,3},{3,2},{4,5},{5,4},{6,7},{7,6},{8,9},{9,8},{10,11... | collective-permute-start | bytes 442376 | tf_op jit(solution)/shard_map/ppermute | solution.py:383
  144.8 9.0 %collective-permute-start.19 = (f32[288,128]{1,0:T(8,128)}, f32[288,128]{1,0:T(8,128)S(1)}, u32[]{:S(2)}, u32[]{:S(2)}) collective-permute-start(f32[288,128]{1,0:T(8,128)} %copy-done.49), channel_id=1, source_target_pairs={{1,2},{2,1},{5,6},{6,5},{9,10},{10,9},{13,14},{14,13},{17,18},{18,... | collective-permute-start | bytes 442376 | tf_op jit(solution)/shard_map/ppermute | solution.py:383
  154.4 2.5 %copy-start.3 = (f32[1,1,1152,1152]{3,2,1,0:T(8,128)S(1)}, f32[1,1,1152,1152]{3,2,1,0:T(8,128)}, u32[]{:S(2)}) copy-start(f32[1,1,1152,1152]{3,2,1,0:T(8,128)} %param.9) | copy-start | bytes 15925252
  156.9 1.1 copy-start.8
  158.0 1.1 copy-start.17
  175.2 17.5 %all-to-all-start.4 = ((f32[32,8,128]{2,1,0:T(8,128)}), f32[32,8,128]{2,1,0:T(8,128)S(1)}, u32[]{:S(2)}, u32[]{:S(2)}) async-start(f32[32,8,128]{2,1,0:T(8,128)} %bitcast.40), calls=%async_computation.4 | async-start | bytes 262144 | tf_op jit(solution)/shard_map/all_to_all | solution.py:388
  180.8 9.3 %collective-permute-start.20 = (f32[288,128]{1,0:T(8,128)S(1)}, f32[288,128]{1,0:T(8,128)S(1)}, u32[]{:S(2)}, u32[]{:S(2)}) collective-permute-start(f32[288,128]{1,0:T(8,128)S(1)} %get-tuple-element.92.refs_4_), channel_id=1, source_target_pairs={{0,4},{4,0},{8,12},{12,8},{16,20},{20,16},{24,28},{28,24},{1,5},{5... | collective-permute-start | bytes 442376 | tf_op jit(solution)/shard_map/ppermute | solution.py:383
  182.6 8.1 %collective-permute-start.21 = (f32[288,128]{1,0:T(8,128)}, f32[288,128]{1,0:T(8,128)S(1)}, u32[]{:S(2)}, u32[]{:S(2)}) collective-permute-start(f32[288,128]{1,0:T(8,128)} %copy-done.29), channel_id=1, source_target_pairs={{4,8},{8,4},{12,16},{16,12},{20,24},{24,20},{5,9},{9,5},{13,17},{1... | collective-permute-start | bytes 442376 | tf_op jit(solution)/shard_map/ppermute | solution.py:383
  183.3 8.1 %collective-permute-start.22 = (f32[288,128]{1,0:T(8,128)}, f32[288,128]{1,0:T(8,128)S(1)}, u32[]{:S(2)}, u32[]{:S(2)}) collective-permute-start(f32[288,128]{1,0:T(8,128)} %copy-done.31), channel_id=1, source_target_pairs={{0,1},{1,0},{2,3},{3,2},{4,5},{5,4},{6,7},{7,6},{8,9},{9,8},{10,11... | collective-permute-start | bytes 442376 | tf_op jit(solution)/shard_map/ppermute | solution.py:383
  183.3 8.7 %collective-permute-start.23 = (f32[288,128]{1,0:T(8,128)}, f32[288,128]{1,0:T(8,128)S(1)}, u32[]{:S(2)}, u32[]{:S(2)}) collective-permute-start(f32[288,128]{1,0:T(8,128)} %copy-done.33), channel_id=1, source_target_pairs={{1,2},{2,1},{5,6},{6,5},{9,10},{10,9},{13,14},{14,13},{17,18},{18,... | collective-permute-start | bytes 442376 | tf_op jit(solution)/shard_map/ppermute | solution.py:383
  192.7 1.1 copy-start.9
  207.1 14.1 %all-to-all-start.5 = ((f32[32,8,128]{2,1,0:T(8,128)}), f32[32,8,128]{2,1,0:T(8,128)S(1)}, u32[]{:S(2)}, u32[]{:S(2)}) async-start(f32[32,8,128]{2,1,0:T(8,128)} %bitcast.42), calls=%async_computation.5 | async-start | bytes 262144 | tf_op jit(solution)/shard_map/all_to_all | solution.py:388
  213.3 1.1 copy-start.25
  214.4 1.1 copy-start.27
  (79 other events, 62.2 us)

commit v2 on v1

--- a/solution.py
+++ b/solution.py
@@ -385,7 +385,9 @@
 
 
 def everywhere(stacked):
-    return lax.all_to_all(stacked, ("sub", "layer"), split_axis=0, concat_axis=0, tiled=True)
+    own = lax.axis_index("sub") * lax.axis_size("layer") + lax.axis_index("layer")
+    rows = lax.broadcasted_iota(jnp.int32, stacked.shape, 0) // PAD
+    return lax.psum(jnp.where(rows == own, stacked, 0.0), ("sub", "layer"))
 
 
 def per_device(

time: 225 us -> 876 us (3.89)
  waiting for transfers between devices: 28.4 us -> 737 us
  starting transfers between devices: 69.8 us -> 26.8 us
  local copies, waits for them, and re-layouts: 87.4 us -> 47.9 us
  between operations: 1.08 us -> 14.4 us
    psum x0 -> x6, waiting for transfers between devices: none -> 729 us  [everywhere(): return lax.psum(jnp.where(rows == own, stacked, 0.0), ('sub', 'layer'))]
    all_to_all x6 -> x0, starting transfers between devices: 44.3 us -> none  [everywhere(): lax.all_to_all(stacked, ('sub', 'layer'), split_axis=0, concat_axis=0, ti...]
    unnamed x195 -> x101, local copies, waits for them, and re-layouts: 87.4 us -> 47.9 us
    ppermute x24, waiting for transfers between devices: 25.9 us -> 7.54 us  [exchange(): received.append(lax.ppermute(block, axis, pairs))]
  transfers between devices with their start and end apart: 30 -> 30, of which waited for: 7 -> 9; matrix products, arithmetic and copies ran while one was open for 0% -> 0% of each run, Pallas kernels for 4% -> 1%
where the time goes in v2:
time: 876 us; the launch traced here: 874 us
  waiting for transfers between devices  737 us (84%)
  local copies, waits for them, and re-layouts  47.9 us (5%)
  Pallas kernels  43.2 us (5%)
  starting transfers between devices  26.8 us (3%)
  between operations  14.4 us (2%)
    psum x6, waiting for transfers between devices, everywhere(): return lax.psum(jnp.where(rows == own, stacked, 0.0), ('sub', 'layer'))  729 us
    unnamed x101, local copies, waits for them, and re-layouts  47.9 us
    pallas_call x10, Pallas kernels, call(): pl.pallas_call(kernel, name=name, out_shape=[jax.ShapeDtypeStruct(shape,...  43.2 us
    ppermute x24, starting transfers between devices, exchange(): received.append(lax.ppermute(block, axis, pairs))  26.1 us
  transfers between devices with their start and end apart: 30, of which 9 were waited for; matrix products, arithmetic and copies ran while one was open for 0% of the time, Pallas kernels for 1%

profile of v2, /device:TPU:0, one launch (start us, length us, event | category | flops | bytes accessed | tf_op | source)
XLA Modules:
  0.0 874.3 jit_solution(8483388414246449245)
XLA Ops:
  10.1 1.4 modes_to_slots.1
  12.6 3.0 collective-permute-start
  17.5 2.5 copy-done
  20.0 2.5 copy-done.4
  22.6 6.2 operators_on_modes.1
  28.7 115.3 %all-reduce.7.cloned.1.call-done.refs_4_ = f32[256,384]{1,0:T(8,128)} async-done(((f32[256,384]{1,0:T(8,128)}), f32[256,384]{1,0:T(8,128)}) %all-reduce.7.cloned.1.call-update) | async-done | bytes 393232 | tf_op jit(solution)/shard_map/psum | solution.py:390
  144.1 2.5 copy-done.1
  147.6 4.5 start.1
  152.1 1.5 collective-permute-start.4
  155.2 7.0 collective-permute-done.4.refs_0_.refs_12_
  162.2 4.1 stage_1.1
  167.1 2.5 collective-permute-start.8
  169.6 1.3 collective-permute-start.9
  170.9 1.2 collective-permute-start.10
  172.1 1.3 collective-permute-start.11
  174.3 123.5 %all-reduce.9.cloned.1.call-done.refs_17_ = f32[256,128]{1,0:T(8,128)} async-done(((f32[256,128]{1,0:T(8,128)}), f32[256,128]{1,0:T(8,128)}) %all-reduce.9.cloned.1.call-update) | async-done | bytes 131088 | tf_op jit(solution)/shard_map/psum | solution.py:390
  297.9 2.5 copy-done.2
  300.4 1.1 copy-done.23
  304.2 6.5 stage_2.1
  312.3 1.5 collective-permute-start.12
  313.8 1.3 collective-permute-start.13
  315.1 1.3 collective-permute-start.15
  317.5 124.6 %all-reduce.11.cloned.1.call-done.refs_17_ = f32[256,128]{1,0:T(8,128)} async-done(((f32[256,128]{1,0:T(8,128)}), f32[256,128]{1,0:T(8,128)}) %all-reduce.11.cloned.1.call-update) | async-done | bytes 131088 | tf_op jit(solution)/shard_map/psum | solution.py:390
  442.2 2.5 copy-done.6
  444.7 1.1 copy-done.19
  445.8 1.1 copy-done.21
  449.6 6.6 stage_3.1
  457.8 1.5 collective-permute-start.16
  459.2 1.3 collective-permute-start.17
  460.5 1.3 collective-permute-start.19
  462.7 124.9 %all-reduce.13.cloned.1.call-done.refs_17_ = f32[256,128]{1,0:T(8,128)} async-done(((f32[256,128]{1,0:T(8,128)}), f32[256,128]{1,0:T(8,128)}) %all-reduce.13.cloned.1.call-update) | async-done | bytes 131088 | tf_op jit(solution)/shard_map/psum | solution.py:390
  587.7 2.5 copy-done.3
  590.2 1.1 copy-done.8
  591.3 1.1 copy-done.17
  595.1 6.5 stage_4.1
  603.2 1.5 collective-permute-start.20
  604.7 1.3 collective-permute-start.21
  606.0 1.3 collective-permute-start.23
  608.5 124.6 %all-reduce.15.cloned.1.call-done.refs_17_ = f32[256,128]{1,0:T(8,128)} async-done(((f32[256,128]{1,0:T(8,128)}), f32[256,128]{1,0:T(8,128)}) %all-reduce.15.cloned.1.call-update) | async-done | bytes 131088 | tf_op jit(solution)/shard_map/psum | solution.py:390
  733.1 1.1 copy-done.9
  734.2 1.1 copy-done.11
  735.2 1.1 copy-done.13
  736.3 1.1 copy-done.15
  738.3 2.7 stage_5.1
  744.6 1.1 copy-done.27
  745.6 3.3 slots_to_rows.1
  749.0 116.2 %all-reduce.17.cloned.1.call-done.gathered = f32[256,128]{1,0:T(8,128)} async-done(((f32[256,128]{1,0:T(8,128)}), f32[256,128]{1,0:T(8,128)}) %all-reduce.17.cloned.1.call-update) | async-done | bytes 131088 | tf_op jit(solution)/shard_map/psum | solution.py:390
  866.1 1.4 residual.1
  (138 shorter events, 31.7 us)
Async XLA Ops:
  7.2 136.9 %all-reduce.7.cloned.1.call-start = ((), (), s32[]{:S(2)}) async-start(), calls=%async_computation | async-start | bytes 786432 | tf_op jit(solution)/shard_map/psum | solution.py:390
  12.5 285.3 %all-reduce.9.cloned.1.call-start = ((), (), s32[]{:S(2)}) async-start(), calls=%async_computation.1 | async-start | bytes 262144 | tf_op jit(solution)/shard_map/psum | solution.py:390
  12.6 4.7 collective-permute-start
  15.6 1.7 collective-permute-start.1
  16.2 1.2 collective-permute-start.2
  16.3 1.2 collective-permute-start.3
  17.5 2.5 copy-start
  20.0 2.5 copy-start.4
  22.6 121.5 %copy-start.28 = (f32[1,1,1152,128]{3,2,1,0:T(8,128)S(1)}, f32[1,1,1152,128]{3,2,1,0:T(8,128)}, u32[]{:S(2)}) copy-start(f32[1,1,1152,128]{3,2,1,0:T(8,128)} %param.7) | copy-start | bytes 1769476
  144.1 2.5 copy-start.1
  147.6 14.7 %copy-start.5 = (f32[1,1,1152,1152]{3,2,1,0:T(8,128)S(1)}, f32[1,1,1152,1152]{3,2,1,0:T(8,128)}, u32[]{:S(2)}) copy-start(f32[1,1,1152,1152]{3,2,1,0:T(8,128)} %param.10) | copy-start | bytes 15925252
  152.1 14.2 %copy-start.10 = (f32[1152,128]{1,0:T(8,128)}, f32[1152,128]{1,0:T(8,128)S(1)}, u32[]{:S(2)}) copy-start(f32[1152,128]{1,0:T(8,128)S(1)} %get-tuple-element.99.refs_22_) | copy-start | bytes 1769476
  152.1 10.1 %collective-permute-start.4 = (f32[432,128]{1,0:T(8,128)S(1)}, f32[432,128]{1,0:T(8,128)S(1)}, u32[]{:S(2)}, u32[]{:S(2)}) collective-permute-start(f32[432,128]{1,0:T(8,128)S(1)} %get-tuple-element.66.refs_4_.refs_8_), channel_id=1, source_target_pairs={{0,4},{4,0},{8,12},{12,8},{16,20},{20,16},{24,28},{28,24},{1,5},{5... | collective-permute-start | bytes 663560 | tf_op jit(solution)/shard_map/ppermute | solution.py:383
  153.6 8.6 collective-permute-start.5
  154.3 7.9 collective-permute-start.6
  154.4 7.9 collective-permute-start.7
  167.1 130.7 %copy-start.38 = (f32[288,128]{1,0:T(8,128)}, f32[288,128]{1,0:T(8,128)S(1)}, u32[]{:S(2)}) copy-start(f32[288,128]{1,0:T(8,128)S(1)} %get-tuple-element.71.refs_4_) | copy-start | bytes 442372
  167.1 130.7 %copy-start.40 = (f32[288,128]{1,0:T(8,128)}, f32[288,128]{1,0:T(8,128)S(1)}, u32[]{:S(2)}) copy-start(f32[288,128]{1,0:T(8,128)S(1)} %get-tuple-element.72.refs_5_) | copy-start | bytes 442372
  167.1 130.7 %collective-permute-start.8 = (f32[288,128]{1,0:T(8,128)S(1)}, f32[288,128]{1,0:T(8,128)}, u32[]{:S(2)}, u32[]{:S(2)}) collective-permute-start(f32[288,128]{1,0:T(8,128)S(1)} %get-tuple-element.71.refs_4_), channel_id=1, source_target_pairs={{0,4},{4,0},{8,12},{12,8},{16,20},{20,16},{24,28},{28,24},{1,5},{5... | collective-permute-start | bytes 442376 | tf_op jit(solution)/shard_map/ppermute | solution.py:383
  169.6 128.2 %collective-permute-start.9 = (f32[288,128]{1,0:T(8,128)S(1)}, f32[288,128]{1,0:T(8,128)}, u32[]{:S(2)}, u32[]{:S(2)}) collective-permute-start(f32[288,128]{1,0:T(8,128)S(1)} %get-tuple-element.72.refs_5_), channel_id=1, source_target_pairs={{4,8},{8,4},{12,16},{16,12},{20,24},{24,20},{5,9},{9,5},{13,17},{1... | collective-permute-start | bytes 442376 | tf_op jit(solution)/shard_map/ppermute | solution.py:383
  170.9 126.9 %collective-permute-start.10 = (f32[288,128]{1,0:T(8,128)}, f32[288,128]{1,0:T(8,128)}, u32[]{:S(2)}, u32[]{:S(2)}) collective-permute-start(f32[288,128]{1,0:T(8,128)} %get-tuple-element.73.refs_6_), channel_id=1, source_target_pairs={{0,1},{1,0},{2,3},{3,2},{4,5},{5,4},{6,7},{7,6},{8,9},{9,8},{10,11... | collective-permute-start | bytes 442376 | tf_op jit(solution)/shard_map/ppermute | solution.py:383
  172.1 125.7 %collective-permute-start.11 = (f32[288,128]{1,0:T(8,128)}, f32[288,128]{1,0:T(8,128)}, u32[]{:S(2)}, u32[]{:S(2)}) collective-permute-start(f32[288,128]{1,0:T(8,128)} %get-tuple-element.74.refs_7_), channel_id=1, source_target_pairs={{1,2},{2,1},{5,6},{6,5},{9,10},{10,9},{13,14},{14,13},{17,18},{18,... | collective-permute-start | bytes 442376 | tf_op jit(solution)/shard_map/ppermute | solution.py:383
  174.3 267.9 %all-reduce.11.cloned.1.call-start = ((), (), s32[]{:S(2)}) async-start(), calls=%async_computation.2 | async-start | bytes 262144 | tf_op jit(solution)/shard_map/psum | solution.py:390
  297.9 2.5 copy-start.2
  312.3 129.9 %copy-start.34 = (f32[288,128]{1,0:T(8,128)}, f32[288,128]{1,0:T(8,128)S(1)}, u32[]{:S(2)}) copy-start(f32[288,128]{1,0:T(8,128)S(1)} %get-tuple-element.78.refs_4_) | copy-start | bytes 442372
  312.3 129.9 %copy-start.36 = (f32[288,128]{1,0:T(8,128)}, f32[288,128]{1,0:T(8,128)S(1)}, u32[]{:S(2)}) copy-start(f32[288,128]{1,0:T(8,128)S(1)} %get-tuple-element.79.refs_5_) | copy-start | bytes 442372
  312.3 129.9 %collective-permute-start.12 = (f32[288,128]{1,0:T(8,128)S(1)}, f32[288,128]{1,0:T(8,128)}, u32[]{:S(2)}, u32[]{:S(2)}) collective-permute-start(f32[288,128]{1,0:T(8,128)S(1)} %get-tuple-element.78.refs_4_), channel_id=1, source_target_pairs={{0,4},{4,0},{8,12},{12,8},{16,20},{20,16},{24,28},{28,24},{1,5},{5... | collective-permute-start | bytes 442376 | tf_op jit(solution)/shard_map/ppermute | solution.py:383
  313.8 128.4 %collective-permute-start.13 = (f32[288,128]{1,0:T(8,128)S(1)}, f32[288,128]{1,0:T(8,128)}, u32[]{:S(2)}, u32[]{:S(2)}) collective-permute-start(f32[288,128]{1,0:T(8,128)S(1)} %get-tuple-element.79.refs_5_), channel_id=1, source_target_pairs={{4,8},{8,4},{12,16},{16,12},{20,24},{24,20},{5,9},{9,5},{13,17},{1... | collective-permute-start | bytes 442376 | tf_op jit(solution)/shard_map/ppermute | solution.py:383
  315.1 127.1 %collective-permute-start.14 = (f32[288,128]{1,0:T(8,128)}, f32[288,128]{1,0:T(8,128)}, u32[]{:S(2)}, u32[]{:S(2)}) collective-permute-start(f32[288,128]{1,0:T(8,128)} %get-tuple-element.80.refs_6_), channel_id=1, source_target_pairs={{0,1},{1,0},{2,3},{3,2},{4,5},{5,4},{6,7},{7,6},{8,9},{9,8},{10,11... | collective-permute-start | bytes 442376 | tf_op jit(solution)/shard_map/ppermute | solution.py:383
  315.1 127.1 %collective-permute-start.15 = (f32[288,128]{1,0:T(8,128)}, f32[288,128]{1,0:T(8,128)}, u32[]{:S(2)}, u32[]{:S(2)}) collective-permute-start(f32[288,128]{1,0:T(8,128)} %get-tuple-element.81.refs_7_), channel_id=1, source_target_pairs={{1,2},{2,1},{5,6},{6,5},{9,10},{10,9},{13,14},{14,13},{17,18},{18,... | collective-permute-start | bytes 442376 | tf_op jit(solution)/shard_map/ppermute | solution.py:383
  317.3 270.4 %all-reduce.13.cloned.1.call-start = ((), (), s32[]{:S(2)}) async-start(), calls=%async_computation.3 | async-start | bytes 262144 | tf_op jit(solution)/shard_map/psum | solution.py:390
  442.2 2.5 copy-start.6
  457.7 129.9 %copy-start.30 = (f32[288,128]{1,0:T(8,128)}, f32[288,128]{1,0:T(8,128)S(1)}, u32[]{:S(2)}) copy-start(f32[288,128]{1,0:T(8,128)S(1)} %get-tuple-element.85.refs_4_) | copy-start | bytes 442372
  457.8 129.9 %copy-start.32 = (f32[288,128]{1,0:T(8,128)}, f32[288,128]{1,0:T(8,128)S(1)}, u32[]{:S(2)}) copy-start(f32[288,128]{1,0:T(8,128)S(1)} %get-tuple-element.86.refs_5_) | copy-start | bytes 442372
  457.8 129.9 %collective-permute-start.16 = (f32[288,128]{1,0:T(8,128)S(1)}, f32[288,128]{1,0:T(8,128)}, u32[]{:S(2)}, u32[]{:S(2)}) collective-permute-start(f32[288,128]{1,0:T(8,128)S(1)} %get-tuple-element.85.refs_4_), channel_id=1, source_target_pairs={{0,4},{4,0},{8,12},{12,8},{16,20},{20,16},{24,28},{28,24},{1,5},{5... | collective-permute-start | bytes 442376 | tf_op jit(solution)/shard_map/ppermute | solution.py:383
  459.2 128.5 %collective-permute-start.17 = (f32[288,128]{1,0:T(8,128)S(1)}, f32[288,128]{1,0:T(8,128)}, u32[]{:S(2)}, u32[]{:S(2)}) collective-permute-start(f32[288,128]{1,0:T(8,128)S(1)} %get-tuple-element.86.refs_5_), channel_id=1, source_target_pairs={{4,8},{8,4},{12,16},{16,12},{20,24},{24,20},{5,9},{9,5},{13,17},{1... | collective-permute-start | bytes 442376 | tf_op jit(solution)/shard_map/ppermute | solution.py:383
  460.5 127.1 %collective-permute-start.18 = (f32[288,128]{1,0:T(8,128)}, f32[288,128]{1,0:T(8,128)}, u32[]{:S(2)}, u32[]{:S(2)}) collective-permute-start(f32[288,128]{1,0:T(8,128)} %get-tuple-element.87.refs_6_), channel_id=1, source_target_pairs={{0,1},{1,0},{2,3},{3,2},{4,5},{5,4},{6,7},{7,6},{8,9},{9,8},{10,11... | collective-permute-start | bytes 442376 | tf_op jit(solution)/shard_map/ppermute | solution.py:383
  460.5 127.1 %collective-permute-start.19 = (f32[288,128]{1,0:T(8,128)}, f32[288,128]{1,0:T(8,128)}, u32[]{:S(2)}, u32[]{:S(2)}) collective-permute-start(f32[288,128]{1,0:T(8,128)} %get-tuple-element.88.refs_7_), channel_id=1, source_target_pairs={{1,2},{2,1},{5,6},{6,5},{9,10},{10,9},{13,14},{14,13},{17,18},{18,... | collective-permute-start | bytes 442376 | tf_op jit(solution)/shard_map/ppermute | solution.py:383
  462.7 270.4 %all-reduce.15.cloned.1.call-start = ((), (), s32[]{:S(2)}) async-start(), calls=%async_computation.4 | async-start | bytes 262144 | tf_op jit(solution)/shard_map/psum | solution.py:390
  587.7 2.5 copy-start.3
  590.2 1.1 copy-start.8
  603.2 129.9 %collective-permute-start.20 = (f32[288,128]{1,0:T(8,128)S(1)}, f32[288,128]{1,0:T(8,128)}, u32[]{:S(2)}, u32[]{:S(2)}) collective-permute-start(f32[288,128]{1,0:T(8,128)S(1)} %get-tuple-element.92.refs_4_), channel_id=1, source_target_pairs={{0,4},{4,0},{8,12},{12,8},{16,20},{20,16},{24,28},{28,24},{1,5},{5... | collective-permute-start | bytes 442376 | tf_op jit(solution)/shard_map/ppermute | solution.py:383
  604.7 128.4 %collective-permute-start.21 = (f32[288,128]{1,0:T(8,128)S(1)}, f32[288,128]{1,0:T(8,128)}, u32[]{:S(2)}, u32[]{:S(2)}) collective-permute-start(f32[288,128]{1,0:T(8,128)S(1)} %get-tuple-element.93.refs_5_), channel_id=1, source_target_pairs={{4,8},{8,4},{12,16},{16,12},{20,24},{24,20},{5,9},{9,5},{13,17},{1... | collective-permute-start | bytes 442376 | tf_op jit(solution)/shard_map/ppermute | solution.py:383
  606.0 127.1 %collective-permute-start.22 = (f32[288,128]{1,0:T(8,128)}, f32[288,128]{1,0:T(8,128)}, u32[]{:S(2)}, u32[]{:S(2)}) collective-permute-start(f32[288,128]{1,0:T(8,128)} %get-tuple-element.94.refs_6_), channel_id=1, source_target_pairs={{0,1},{1,0},{2,3},{3,2},{4,5},{5,4},{6,7},{7,6},{8,9},{9,8},{10,11... | collective-permute-start | bytes 442376 | tf_op jit(solution)/shard_map/ppermute | solution.py:383
  606.0 127.1 %collective-permute-start.23 = (f32[288,128]{1,0:T(8,128)}, f32[288,128]{1,0:T(8,128)}, u32[]{:S(2)}, u32[]{:S(2)}) collective-permute-start(f32[288,128]{1,0:T(8,128)} %get-tuple-element.95.refs_7_), channel_id=1, source_target_pairs={{1,2},{2,1},{5,6},{6,5},{9,10},{10,9},{13,14},{14,13},{17,18},{18,... | collective-permute-start | bytes 442376 | tf_op jit(solution)/shard_map/ppermute | solution.py:383
  608.2 257.0 %all-reduce.17.cloned.1.call-start = ((), (), s32[]{:S(2)}) async-start(), calls=%async_computation.5 | async-start | bytes 262144 | tf_op jit(solution)/shard_map/psum | solution.py:390
  733.1 1.1 copy-start.9
  743.5 1.1 copy-start.25
  (32 other events, 28.9 us)
Sparse Core Ops, SparseCore 0:
  13.9 130.1 all-reduce.6
  174.4 123.3 all-reduce.8
  317.4 124.7 all-reduce.10
  462.8 124.7 all-reduce.12
  608.3 124.7 all-reduce.14
  743.6 121.4 all-reduce.16

commit v3 on v1

--- a/solution.py
+++ b/solution.py
@@ -108,10 +108,19 @@
     return halves(one_pass(a_high, both)) + one_pass(a_low, b_high)
 
 
-def copies(ref, block):
-    rows = block.shape[0]
-    for q in range(ref.shape[0] // rows):
-        ref[q * rows : (q + 1) * rows, :] = block
+def turned(x, bits):
+    flipped = 0
+    for b in range(bits):
+        flipped = flipped | (((x >> b) & 1) << (bits - 1 - b))
+    return flipped
+
+
+def in_order(gathered, columns, here, table):
+    count = table.shape[0] // PAD
+    bits = count.bit_length() - 1
+    for q in range(count):
+        first = pl.multiple_of((here ^ turned(q, bits)) * PAD, PAD)
+        table[pl.ds(first, PAD), :] = gathered[q * PAD : (q + 1) * PAD, columns]
 
 
 def modes_kernel(mode_count, codes_row, modes, inverse, load, place, *outs):
@@ -146,7 +155,7 @@
     wide = exact(jnp.concatenate([inverse[...], blank], axis=0), spread)
     blank = jnp.zeros((PAD - mode_count, load.shape[1]), jnp.float32)
     loads = jnp.concatenate([load[...], blank], axis=0)
-    copies(outs[SIDES], jnp.concatenate([wide, loads], axis=1))
+    outs[SIDES][...] = jnp.concatenate([wide, loads], axis=1)
     outs[SIDES + 1][...] = codes_lanes
     outs[SIDES + 2][...] = jnp.concatenate([upper, lower], axis=0)
 
@@ -212,18 +221,23 @@
     gathered, modes, place_ref = refs[4:7]
     outs = refs[7:11]
     start_out, inverse_out = refs[11:13]
-    slot_pieces, row_pieces, out_pieces = refs[13:16]
+    slot_pieces, row_pieces, out_pieces, table = refs[13:17]
     cap = codes_lanes.shape[0] // SIDES
     wide = gathered.shape[0]
+    devices = wide // PAD
+    bits = devices.bit_length() - 1
+    here = place_ref[0] * layers + place_ref[1]
     spread = lane_spread(mode_count, GROUP)
     for n, centre in enumerate(around(place_ref[0], place_ref[1])):
         rows = []
         for i, j in around(*centre):
-            first = jnp.clip(i * layers + j, 0, wide // PAD - 1) * PAD
+            near = jnp.clip(i * layers + j, 0, devices - 1)
+            first = turned(here ^ near, bits) * PAD
             rows.append(gathered[pl.ds(pl.multiple_of(first, PAD), PAD), 0:wide])
-        table = jnp.concatenate(rows, axis=0)
-        inverse_out[n * GROUP : (n + 1) * GROUP, :] = exact(spread, table, ((0,), (0,)))
-    coefficients = repeated(exact(inverse_out[0:GROUP, :], gathered[:, wide:]))
+        rows = jnp.concatenate(rows, axis=0)
+        inverse_out[n * GROUP : (n + 1) * GROUP, :] = exact(spread, rows, ((0,), (0,)))
+    in_order(gathered, slice(wide, None), here, table)
+    coefficients = repeated(exact(inverse_out[0:GROUP, :], table[...]))
     start = three_pass(modes[...], coefficients)
     start_out[...] = start
     fill_pieces(slot_pieces, 0, start)
@@ -268,7 +282,7 @@
         block = sent[side][0:cap, :] - received[side][0:cap, :]
         gap_out[side * cap : (side + 1) * cap, :] = block
         fill_pieces(slot_pieces, side * cap, block)
-    copies(parts_out, components_of(own, slot_pieces))
+    parts_out[...] = components_of(own, slot_pieces)
 
     def write(side, block):
         outs[side][...] = block
@@ -276,7 +290,7 @@
     apply_local(schur, codes_row, codes_lanes, slot_pieces, row_pieces, out_pieces, write)
 
 
-def stage_kernel(stage, counts, matrix, codes_row, codes_lanes, *refs):
+def stage_kernel(stage, layers, counts, matrix, codes_row, codes_lanes, place_ref, *refs):
     refs = list(refs)
 
     def take(count):
@@ -290,10 +304,11 @@
     outs = take(4) if stage < 5 else []
     states_out = take(counts[1])
     (parts_out,) = take(1)
-    slot_pieces, row_pieces, out_pieces = take(3)
+    slot_pieces, row_pieces, out_pieces, table = take(4)
     total = codes_lanes.shape[0]
     cap = total // SIDES
-    coefficients = exact(inverse_rows[...], gathered[...])
+    in_order(gathered, slice(None), place_ref[0] * layers + place_ref[1], table)
+    coefficients = exact(inverse_rows[...], table[...])
     direct_all = three_pass(modes[...], repeated(coefficients[0:GROUP]))
     tail = pl.ds(cap, cap // 2)
     for side in range(SIDES):
@@ -330,7 +345,7 @@
         if nextin is not None:
             fill_pieces(slot_pieces, side * cap, nextin)
         fill_pieces(out_pieces, side * cap, block)
-    copies(parts_out, components_of(own, out_pieces))
+    parts_out[...] = components_of(own, out_pieces)
     if stage < 5:
 
         def write(side, block):
@@ -354,8 +369,9 @@
     to_rows(codes_lanes, pieces, keep)
 
 
-def last_kernel(residual, modes, gathered, inverse_rows, out):
-    coefficients = repeated(exact(inverse_rows[0:GROUP, :], gathered[...]))
+def last_kernel(layers, residual, modes, gathered, inverse_rows, place_ref, out, table):
+    in_order(gathered, slice(None), place_ref[0] * layers + place_ref[1], table)
+    coefficients = repeated(exact(inverse_rows[0:GROUP, :], table[...]))
     out[...] = residual[...] + three_pass(modes[...], coefficients)
 
 
@@ -384,8 +400,15 @@
     return received
 
 
-def everywhere(stacked):
-    return lax.all_to_all(stacked, ("sub", "layer"), split_axis=0, concat_axis=0, tiled=True)
+def everywhere(block):
+    for axis in ("sub", "layer"):
+        count = lax.axis_size(axis)
+        step = count // 2
+        while step > 0:
+            other = lax.ppermute(block, axis, [(i, i ^ step) for i in range(count)])
+            block = jnp.concatenate([block, other], axis=0)
+            step //= 2
+    return block
 
 
 def per_device(
@@ -405,14 +428,15 @@
     scratch = [pieces] * 3
     block = [(cap, cols)] * SIDES
     whole = (total, cols)
-    parts = (wide, cols)
+    parts = (PAD, cols)
+    ordered = pltpu.VMEM((wide, cols), jnp.float32)
     table = 8 * wide * (wide + cols)
 
     shown = call(
         functools.partial(modes_kernel, mode_count),
         "modes_to_slots",
         [(PAD, cap)] * SIDES
-        + [(wide, wide + cols), jax.ShapeDtypeStruct((total, 128), jnp.int32), (2 * PAD, total)]
+        + [(PAD, wide + cols), jax.ShapeDtypeStruct((total, 128), jnp.int32), (2 * PAD, total)]
         + [jax.ShapeDtypeStruct((1, total), jnp.int32)],
         [route_codes[0], modes, coarse_inverse, rigid_load, place],
         smem=(4,),
@@ -434,7 +458,7 @@
         "start",
         [(cap + cap // 2, cols)] * SIDES + [whole, (5 * GROUP, wide)],
         [flex, gap, codes_row, codes_lanes, *slabs, gathered, slot_modes, place],
-        scratch,
+        scratch + [ordered],
         smem=(10,),
         extra=table,
     )
@@ -453,15 +477,16 @@
     def stage(number, matrix, states_in, sent, components):
         gathered = everywhere(components)
         received = exchange(sent)
-        inputs = [codes_row, codes_lanes, *received, *sent, *slab_sent, *slab_received]
+        inputs = [codes_row, codes_lanes, place, *received, *sent, *slab_sent, *slab_received]
         inputs += [own_pieces, gathered, inverse_rows, slot_modes, *states_in]
         outs = [whole] * 2 + [parts]
-        kernel = functools.partial(stage_kernel, number, (len(states_in), 2))
+        kernel = functools.partial(stage_kernel, number, layers, (len(states_in), 2))
         if matrix is None:
             kernel = functools.partial(kernel, None)
         else:
             inputs, outs = [matrix] + inputs, block + outs
-        return call(kernel, "stage_%d" % number, outs, inputs, scratch)
+        scalar = (2,) if matrix is None else (3,)
+        return call(kernel, "stage_%d" % number, outs, inputs, scratch + [ordered], smem=scalar)
 
     shown = stage(2, flex, [gap_jump], sent, components)
     sent, (precond, residual, components) = shown[:4], shown[4:]
@@ -481,7 +506,12 @@
         [pltpu.VMEM((total, 768), jnp.bfloat16)],
     )
     (residual,) = call(
-        last_kernel, "residual", [whole], [residual, row_modes, gathered, inverse_rows]
+        functools.partial(last_kernel, layers),
+        "residual",
+        [whole],
+        [residual, row_modes, gathered, inverse_rows, place],
+        [ordered],
+        smem=(4,),
     )
     return (multipliers[None, None], residual[None, None])
 

time: 225 us -> 211 us (0.938)
  local copies, waits for them, and re-layouts: 87.4 us -> 8 us
  waiting for transfers between devices: 28.4 us -> 66.7 us
  starting transfers between devices: 69.8 us -> 94.8 us
  Pallas kernels: 35.9 us -> 39.2 us
    unnamed x195 -> x41, local copies, waits for them, and re-layouts: 87.4 us -> 7.9 us
    ppermute x0 -> x30, starting transfers between devices: none -> 66.6 us  [everywhere(): other = lax.ppermute(block, axis, [(i, i ^ step) for i in range(count)])]
    ppermute x0 -> x30, waiting for transfers between devices: none -> 47.7 us  [everywhere(): other = lax.ppermute(block, axis, [(i, i ^ step) for i in range(count)])]
    all_to_all x6 -> x0, starting transfers between devices: 44.3 us -> none  [everywhere(): lax.all_to_all(stacked, ('sub', 'layer'), split_axis=0, concat_axis=0, ti...]
    ppermute x24, waiting for transfers between devices: 25.9 us -> 19 us  [exchange(): received.append(lax.ppermute(block, axis, pairs))]
    pallas_call x10, Pallas kernels: 35.9 us -> 39.2 us  [call(): pl.pallas_call(kernel, name=name, out_shape=[jax.ShapeDtypeStruct(shape,...]
    ppermute x24, starting transfers between devices: 25.5 us -> 28.1 us  [exchange(): received.append(lax.ppermute(block, axis, pairs))]
    all_to_all x6 -> x0, waiting for transfers between devices: 2.52 us -> none  [everywhere(): lax.all_to_all(stacked, ('sub', 'layer'), split_axis=0, concat_axis=0, ti...]
  transfers between devices with their start and end apart: 30 -> 54, of which waited for: 7 -> 30; matrix products, arithmetic and copies ran while one was open for 0% -> 0% of each run, Pallas kernels for 4% -> 5%
where the time goes in v3:
time: 211 us; the launch traced here: 210 us
  starting transfers between devices  94.8 us (45%)
  waiting for transfers between devices  66.7 us (32%)
  Pallas kernels  39.2 us (19%)
  local copies, waits for them, and re-layouts  8 us (4%)
    ppermute x30, starting transfers between devices, everywhere(): other = lax.ppermute(block, axis, [(i, i ^ step) for i in range(count)])  66.6 us
    ppermute x30, waiting for transfers between devices, everywhere(): other = lax.ppermute(block, axis, [(i, i ^ step) for i in range(count)])  47.7 us
    pallas_call x10, Pallas kernels, call(): pl.pallas_call(kernel, name=name, out_shape=[jax.ShapeDtypeStruct(shape,...  39.2 us
    ppermute x24, starting transfers between devices, exchange(): received.append(lax.ppermute(block, axis, pairs))  28.1 us
    ppermute x24, waiting for transfers between devices, exchange(): received.append(lax.ppermute(block, axis, pairs))  19 us
    unnamed x41, local copies, waits for them, and re-layouts  7.9 us
  transfers between devices with their start and end apart: 54, of which 30 were waited for; matrix products, arithmetic and copies ran while one was open for 0% of the time, Pallas kernels for 5%

profile of v3, /device:TPU:0, one launch (start us, length us, event | category | flops | bytes accessed | tf_op | source)
XLA Modules:
  0.0 209.8 jit_solution(17957973995752852494)
XLA Ops:
  5.0 4.1 %collective-permute-start.4 = (f32[8,384]{1,0:T(8,128)S(1)}, f32[8,384]{1,0:T(8,128)S(1)}, u32[]{:S(2)}, u32[]{:S(2)}) collective-permute-start(f32[8,384]{1,0:T(8,128)S(1)} %get-tuple-element.64), channel_id=1, source_target_pairs={{0,16},{4,20},{8,24},{12,28},{16,0},{20,4},{24,8},{28,12},{1,17},{... | collective-permute-start | bytes 36872 | tf_op jit(solution)/shard_map/ppermute | solution.py:408
  10.7 1.9 collective-permute-start.5
  12.6 1.9 collective-permute-done.5
  16.4 2.3 %collective-permute-done.6 = f32[32,384]{1,0:T(8,128)S(1)} collective-permute-done((f32[32,384]{1,0:T(8,128)S(1)}, f32[32,384]{1,0:T(8,128)S(1)}, u32[]{:S(2)}, u32[]{:S(2)}) %collective-permute-start.6) | collective-permute-done | bytes 49184 | tf_op jit(solution)/shard_map/ppermute | solution.py:408
  18.6 1.9 collective-permute-start.7
  20.6 2.8 %collective-permute-done.7 = f32[64,384]{1,0:T(8,128)S(1)} collective-permute-done((f32[64,384]{1,0:T(8,128)S(1)}, f32[64,384]{1,0:T(8,128)S(1)}, u32[]{:S(2)}, u32[]{:S(2)}) %collective-permute-start.7) | collective-permute-done | bytes 98336 | tf_op jit(solution)/shard_map/ppermute | solution.py:408
  23.4 1.9 collective-permute-start
  27.2 2.5 %copy-done = f32[1,1,1152,1152]{3,2,1,0:T(8,128)S(1)} copy-done((f32[1,1,1152,1152]{3,2,1,0:T(8,128)S(1)}, f32[1,1,1152,1152]{3,2,1,0:T(8,128)}, u32[]{:S(2)}) %copy-start) | copy-done | bytes 5308440
  29.7 2.5 %copy-done.2 = f32[1,1,1152,1152]{3,2,1,0:T(8,128)S(1)} copy-done((f32[1,1,1152,1152]{3,2,1,0:T(8,128)S(1)}, f32[1,1,1152,1152]{3,2,1,0:T(8,128)}, u32[]{:S(2)}) %copy-start.2) | copy-done | bytes 5308440
  32.2 6.2 %operators_on_modes.1 = (f32[144,128]{1,0:T(8,128)S(1)}, f32[144,128]{1,0:T(8,128)S(1)}, f32[144,128]{1,0:T(8,128)S(1)}, f32[144,128]{1,0:T(8,128)S(1)}, f32[1152,128]{1,0:T(8,128)S(1)}) custom-call(f32[1152,1152]{1,0:T(8,128)S(1)} %bitcast.11, f32[1152,1152]{1,0:T(8,128)S(1)} %bitcast.15, s32[1,1152]{1,0:T(1,128)S(1)} %get-tuple-element.55.codes_row, ...), custom_call_target="tpu_custom_call" | custom-call | tf_op jit(solution)/shard_map/operators_on_modes/pallas_call | solution.py:381
  38.5 4.6 %start.1 = (f32[432,128]{1,0:T(8,128)S(1)}, f32[432,128]{1,0:T(8,128)S(1)}, f32[432,128]{1,0:T(8,128)S(1)}, f32[432,128]{1,0:T(8,128)S(1)}, f32[1152,128]{1,0:T(8,128)S(1)}, /*index=5*/f32[160,256]{1,0:T(8,128)S(1)}) custom-call(f32[1152,1152]{1,0:T(8,128)S(1)} %bitcast.12, f32[1152,128]{1,0:T(8,128)S(1)} %bitcast.18, ...), custom_call_target="tpu_custom_call" | custom-call | tf_op jit(solution)/shard_map/start/pallas_call | solution.py:381
  43.1 4.8 %collective-permute-start.9 = (f32[432,128]{1,0:T(8,128)S(1)}, f32[432,128]{1,0:T(8,128)S(1)}, u32[]{:S(2)}, u32[]{:S(2)}) collective-permute-start(f32[432,128]{1,0:T(8,128)S(1)} %get-tuple-element.66.refs_4_.refs_8_), channel_id=1, source_target_pairs={{0,4},{4,0},{8,12},{12,8},{16,20},{20,16},{24,28},{28,24},{1,5},{5... | collective-permute-start | bytes 663560 | tf_op jit(solution)/shard_map/ppermute | solution.py:399
  48.7 3.6 %collective-permute-start.11 = (f32[432,128]{1,0:T(8,128)S(1)}, f32[432,128]{1,0:T(8,128)S(1)}, u32[]{:S(2)}, u32[]{:S(2)}) collective-permute-start(f32[432,128]{1,0:T(8,128)S(1)} %get-tuple-element.68.refs_6_.refs_10_), channel_id=1, source_target_pairs={{0,1},{1,0},{2,3},{3,2},{4,5},{5,4},{6,7},{7,6},{8,9},{9,8},{10,11... | collective-permute-start | bytes 663560 | tf_op jit(solution)/shard_map/ppermute | solution.py:399
  53.4 3.4 %stage_1.1 = (f32[288,128]{1,0:T(8,128)S(1)}, f32[288,128]{1,0:T(8,128)S(1)}, f32[288,128]{1,0:T(8,128)S(1)}, f32[288,128]{1,0:T(8,128)S(1)}, f32[1152,128]{1,0:T(8,128)S(1)}, /*index=5*/f32[8,128]{1,0:T(8,128)S(1)}) custom-call(f32[1152,1152]{1,0:T(8,128)S(1)} %bitcast.16, s32[1,1152]{1,0:T(1,128)S(1)} %get-tuple-element.55.codes_row, ...), custom_call_target="tpu_custom_call" | custom-call | tf_op jit(solution)/shard_map/stage_1/pallas_call | solution.py:381
  56.8 6.5 %collective-permute-start.17 = (f32[8,128]{1,0:T(8,128)S(1)}, f32[8,128]{1,0:T(8,128)S(1)}, u32[]{:S(2)}, u32[]{:S(2)}) collective-permute-start(f32[8,128]{1,0:T(8,128)S(1)} %get-tuple-element.75), channel_id=1, source_target_pairs={{0,16},{4,20},{8,24},{12,28},{16,0},{20,4},{24,8},{28,12},{1,17},{... | collective-permute-start | bytes 12296 | tf_op jit(solution)/shard_map/ppermute | solution.py:408
  64.9 4.9 %collective-permute-start.18 = (f32[16,128]{1,0:T(8,128)S(1)}, f32[16,128]{1,0:T(8,128)S(1)}, u32[]{:S(2)}, u32[]{:S(2)}) collective-permute-start(f32[16,128]{1,0:T(8,128)S(1)} %pad_maximum_fusion.13), channel_id=1, source_target_pairs={{0,8},{4,12},{8,0},{12,4},{16,24},{20,28},{24,16},{28,20},{1,9},{5... | collective-permute-start | bytes 24584 | tf_op jit(solution)/shard_map/ppermute | solution.py:408
  71.4 3.7 %collective-permute-done.19 = f32[32,128]{1,0:T(8,128)S(1)} collective-permute-done((f32[32,128]{1,0:T(8,128)S(1)}, f32[32,128]{1,0:T(8,128)S(1)}, u32[]{:S(2)}, u32[]{:S(2)}) %collective-permute-start.19) | collective-permute-done | bytes 16416 | tf_op jit(solution)/shard_map/ppermute | solution.py:408
  75.1 3.4 %collective-permute-start.20 = (f32[64,128]{1,0:T(8,128)S(1)}, f32[64,128]{1,0:T(8,128)S(1)}, u32[]{:S(2)}, u32[]{:S(2)}) collective-permute-start(f32[64,128]{1,0:T(8,128)S(1)} %pad_maximum_fusion.2), channel_id=1, source_target_pairs={{0,2},{1,3},{2,0},{3,1},{4,6},{5,7},{6,4},{7,5},{8,10},{9,11},{10,... | collective-permute-start | bytes 98312 | tf_op jit(solution)/shard_map/ppermute | solution.py:408
  80.4 2.1 collective-permute-start.13
  84.1 2.9 %collective-permute-done.13.refs_0_ = f32[288,128]{1,0:T(8,128)S(1)} collective-permute-done((f32[288,128]{1,0:T(8,128)S(1)}, f32[288,128]{1,0:T(8,128)S(1)}, u32[]{:S(2)}, u32[]{:S(2)}) %collective-permute-start.13) | collective-permute-done | bytes 147488 | tf_op jit(solution)/shard_map/ppermute | solution.py:399
  86.9 5.3 %stage_2.1 = (f32[288,128]{1,0:T(8,128)S(1)}, f32[288,128]{1,0:T(8,128)S(1)}, f32[288,128]{1,0:T(8,128)S(1)}, f32[288,128]{1,0:T(8,128)S(1)}, f32[1152,128]{1,0:...) custom-call(f32[1152,1152]{1,0:T(8,128)S(1)} %bitcast.13, s32[1,1152]{1,0:T(1,128)S(1)} %get-tuple-element.55.codes_row, ...), custom_call_target="tpu_custom_call" | custom-call | tf_op jit(solution)/shard_map/stage_2/pallas_call | solution.py:381
  92.2 4.5 %collective-permute-start.26 = (f32[8,128]{1,0:T(8,128)S(1)}, f32[8,128]{1,0:T(8,128)S(1)}, u32[]{:S(2)}, u32[]{:S(2)}) collective-permute-start(f32[8,128]{1,0:T(8,128)S(1)} %get-tuple-element.82), channel_id=1, source_target_pairs={{0,16},{4,20},{8,24},{12,28},{16,0},{20,4},{24,8},{28,12},{1,17},{... | collective-permute-start | bytes 12296 | tf_op jit(solution)/shard_map/ppermute | solution.py:408
  98.3 4.3 %collective-permute-start.27 = (f32[16,128]{1,0:T(8,128)S(1)}, f32[16,128]{1,0:T(8,128)S(1)}, u32[]{:S(2)}, u32[]{:S(2)}) collective-permute-start(f32[16,128]{1,0:T(8,128)S(1)} %pad_maximum_fusion.14), channel_id=1, source_target_pairs={{0,8},{4,12},{8,0},{12,4},{16,24},{20,28},{24,16},{28,20},{1,9},{5... | collective-permute-start | bytes 24584 | tf_op jit(solution)/shard_map/ppermute | solution.py:408
  105.4 2.6 %collective-permute-done.28 = f32[32,128]{1,0:T(8,128)S(1)} collective-permute-done((f32[32,128]{1,0:T(8,128)S(1)}, f32[32,128]{1,0:T(8,128)S(1)}, u32[]{:S(2)}, u32[]{:S(2)}) %collective-permute-start.28) | collective-permute-done | bytes 16416 | tf_op jit(solution)/shard_map/ppermute | solution.py:408
  108.0 3.2 %collective-permute-start.29 = (f32[64,128]{1,0:T(8,128)S(1)}, f32[64,128]{1,0:T(8,128)S(1)}, u32[]{:S(2)}, u32[]{:S(2)}) collective-permute-start(f32[64,128]{1,0:T(8,128)S(1)} %pad_maximum_fusion.3), channel_id=1, source_target_pairs={{0,2},{1,3},{2,0},{3,1},{4,6},{5,7},{6,4},{7,5},{8,10},{9,11},{10,... | collective-permute-start | bytes 98312 | tf_op jit(solution)/shard_map/ppermute | solution.py:408
  113.1 2.1 collective-permute-start.22
  117.0 5.1 %collective-permute-done.22.refs_0_ = f32[288,128]{1,0:T(8,128)S(1)} collective-permute-done((f32[288,128]{1,0:T(8,128)S(1)}, f32[288,128]{1,0:T(8,128)S(1)}, u32[]{:S(2)}, u32[]{:S(2)}) %collective-permute-start.22) | collective-permute-done | bytes 147488 | tf_op jit(solution)/shard_map/ppermute | solution.py:399
  122.1 5.4 %stage_3.1 = (f32[288,128]{1,0:T(8,128)S(1)}, f32[288,128]{1,0:T(8,128)S(1)}, f32[288,128]{1,0:T(8,128)S(1)}, f32[288,128]{1,0:T(8,128)S(1)}, f32[1152,128]{1,0:...) custom-call(f32[1152,1152]{1,0:T(8,128)S(1)} %bitcast.17, s32[1,1152]{1,0:T(1,128)S(1)} %get-tuple-element.55.codes_row, ...), custom_call_target="tpu_custom_call" | custom-call | tf_op jit(solution)/shard_map/stage_3/pallas_call | solution.py:381
  127.5 2.1 collective-permute-start.35
  129.6 2.5 %collective-permute-done.35 = f32[8,128]{1,0:T(8,128)S(1)} collective-permute-done((f32[8,128]{1,0:T(8,128)S(1)}, f32[8,128]{1,0:T(8,128)S(1)}, u32[]{:S(2)}, u32[]{:S(2)}) %collective-permute-start.35) | collective-permute-done | bytes 4128 | tf_op jit(solution)/shard_map/ppermute | solution.py:408
  133.8 1.9 collective-permute-done.36
  135.8 2.5 %collective-permute-start.37 = (f32[32,128]{1,0:T(8,128)S(1)}, f32[32,128]{1,0:T(8,128)S(1)}, u32[]{:S(2)}, u32[]{:S(2)}) collective-permute-start(f32[32,128]{1,0:T(8,128)S(1)} %pad_maximum_fusion.10), channel_id=1, source_target_pairs={{0,4},{4,0},{8,12},{12,8},{16,20},{20,16},{24,28},{28,24},{1,5},{5... | collective-permute-start | bytes 49160 | tf_op jit(solution)/shard_map/ppermute | solution.py:408
  140.0 2.6 %collective-permute-start.38 = (f32[64,128]{1,0:T(8,128)S(1)}, f32[64,128]{1,0:T(8,128)S(1)}, u32[]{:S(2)}, u32[]{:S(2)}) collective-permute-start(f32[64,128]{1,0:T(8,128)S(1)} %pad_maximum_fusion.4), channel_id=1, source_target_pairs={{0,2},{1,3},{2,0},{3,1},{4,6},{5,7},{6,4},{7,5},{8,10},{9,11},{10,... | collective-permute-start | bytes 98312 | tf_op jit(solution)/shard_map/ppermute | solution.py:408
  144.5 2.0 collective-permute-start.31
  148.0 5.3 %collective-permute-done.31.refs_0_ = f32[288,128]{1,0:T(8,128)S(1)} collective-permute-done((f32[288,128]{1,0:T(8,128)S(1)}, f32[288,128]{1,0:T(8,128)S(1)}, u32[]{:S(2)}, u32[]{:S(2)}) %collective-permute-start.31) | collective-permute-done | bytes 147488 | tf_op jit(solution)/shard_map/ppermute | solution.py:399
  153.4 5.4 %stage_4.1 = (f32[288,128]{1,0:T(8,128)S(1)}, f32[288,128]{1,0:T(8,128)S(1)}, f32[288,128]{1,0:T(8,128)S(1)}, f32[288,128]{1,0:T(8,128)S(1)}, f32[1152,128]{1,0:...) custom-call(f32[1152,1152]{1,0:T(8,128)S(1)} %bitcast.14, s32[1,1152]{1,0:T(1,128)S(1)} %get-tuple-element.55.codes_row, ...), custom_call_target="tpu_custom_call" | custom-call | tf_op jit(solution)/shard_map/stage_4/pallas_call | solution.py:381
  158.7 2.7 %collective-permute-start.44 = (f32[8,128]{1,0:T(8,128)S(1)}, f32[8,128]{1,0:T(8,128)S(1)}, u32[]{:S(2)}, u32[]{:S(2)}) collective-permute-start(f32[8,128]{1,0:T(8,128)S(1)} %get-tuple-element.96), channel_id=1, source_target_pairs={{0,16},{4,20},{8,24},{12,28},{16,0},{20,4},{24,8},{28,12},{1,17},{... | collective-permute-start | bytes 12296 | tf_op jit(solution)/shard_map/ppermute | solution.py:408
  163.3 2.6 %collective-permute-start.45 = (f32[16,128]{1,0:T(8,128)S(1)}, f32[16,128]{1,0:T(8,128)S(1)}, u32[]{:S(2)}, u32[]{:S(2)}) collective-permute-start(f32[16,128]{1,0:T(8,128)S(1)} %pad_maximum_fusion.16), channel_id=1, source_target_pairs={{0,8},{4,12},{8,0},{12,4},{16,24},{20,28},{24,16},{28,20},{1,9},{5... | collective-permute-start | bytes 24584 | tf_op jit(solution)/shard_map/ppermute | solution.py:408
  171.3 3.1 %collective-permute-start.47 = (f32[64,128]{1,0:T(8,128)S(1)}, f32[64,128]{1,0:T(8,128)S(1)}, u32[]{:S(2)}, u32[]{:S(2)}) collective-permute-start(f32[64,128]{1,0:T(8,128)S(1)} %pad_maximum_fusion.5), channel_id=1, source_target_pairs={{0,2},{1,3},{2,0},{3,1},{4,6},{5,7},{6,4},{7,5},{8,10},{9,11},{10,... | collective-permute-start | bytes 98312 | tf_op jit(solution)/shard_map/ppermute | solution.py:408
  176.3 2.0 collective-permute-start.40
  180.1 5.1 %collective-permute-done.40.refs_0_ = f32[288,128]{1,0:T(8,128)S(1)} collective-permute-done((f32[288,128]{1,0:T(8,128)S(1)}, f32[288,128]{1,0:T(8,128)S(1)}, u32[]{:S(2)}, u32[]{:S(2)}) %collective-permute-start.40) | collective-permute-done | bytes 147488 | tf_op jit(solution)/shard_map/ppermute | solution.py:399
  185.2 2.1 %stage_5.1 = (f32[1152,128]{1,0:T(8,128)S(1)}, f32[1152,128]{1,0:T(8,128)S(1)}, f32[8,128]{1,0:T(8,128)S(1)}) custom-call(s32[1,1152]{1,0:T(1,128)S(1)} %get-tuple-element.55.codes_row, s32[1152,128]{1,0:T(8,128)S(1)} %get-tuple-element.54.codes_lanes, s32[2]{0:T(128)S(1)} %pad_add_fusion.place.refs_6_.place_ref, ...), custom_call_target="tpu_custom_call" | custom-call | tf_op jit(solution)/shard_map/stage_5/pallas_call | solution.py:381
  187.3 3.5 %collective-permute-start.49 = (f32[8,128]{1,0:T(8,128)S(1)}, f32[8,128]{1,0:T(8,128)S(1)}, u32[]{:S(2)}, u32[]{:S(2)}) collective-permute-start(f32[8,128]{1,0:T(8,128)S(1)} %get-tuple-element.105), channel_id=1, source_target_pairs={{0,16},{4,20},{8,24},{12,28},{16,0},{20,4},{24,8},{28,12},{1,17},{... | collective-permute-start | bytes 12296 | tf_op jit(solution)/shard_map/ppermute | solution.py:408
  193.9 2.1 collective-permute-done.50
  196.0 1.9 collective-permute-start.51
  199.7 2.8 %collective-permute-start.52 = (f32[64,128]{1,0:T(8,128)S(1)}, f32[64,128]{1,0:T(8,128)S(1)}, u32[]{:S(2)}, u32[]{:S(2)}) collective-permute-start(f32[64,128]{1,0:T(8,128)S(1)} %pad_maximum_fusion.6), channel_id=1, source_target_pairs={{0,2},{1,3},{2,0},{3,1},{4,6},{5,7},{6,4},{7,5},{8,10},{9,11},{10,... | collective-permute-start | bytes 98312 | tf_op jit(solution)/shard_map/ppermute | solution.py:408
  204.4 3.4 %slots_to_rows.1 = (f32[1152,128]{1,0:T(8,128)S(1)}, f32[1152,128]{1,0:T(8,128)}, f32[1152,128]{1,0:T(8,128)S(1)}) custom-call(s32[1152,128]{1,0:T(8,128)S(1)} %get-tuple-element.54.codes_lanes, f32[1152,128]{1,0:T(8,128)S(1)} %get-tuple-element.100.residual, f32[1152,128]{1,0:T(8,128)S(1)} %get-tuple-element.101.multipliers, ...), custom_call_target="tpu_custom_call" | custom-call | tf_op jit(solution)/shard_map/slots_to_rows/pallas_call | solution.py:381
  207.8 2.0 residual.1
  (142 shorter events, 51.0 us)
Async XLA Ops:
  5.0 5.7 %collective-permute-start.4 = (f32[8,384]{1,0:T(8,128)S(1)}, f32[8,384]{1,0:T(8,128)S(1)}, u32[]{:S(2)}, u32[]{:S(2)}) collective-permute-start(f32[8,384]{1,0:T(8,128)S(1)} %get-tuple-element.64), channel_id=1, source_target_pairs={{0,16},{4,20},{8,24},{12,28},{16,0},{20,4},{24,8},{28,12},{1,17},{... | collective-permute-start | bytes 36872 | tf_op jit(solution)/shard_map/ppermute | solution.py:408
  10.7 3.8 %collective-permute-start.5 = (f32[16,384]{1,0:T(8,128)S(1)}, f32[16,384]{1,0:T(8,128)S(1)}, u32[]{:S(2)}, u32[]{:S(2)}) collective-permute-start(f32[16,384]{1,0:T(8,128)S(1)} %pad_maximum_fusion.7), channel_id=1, source_target_pairs={{0,8},{4,12},{8,0},{12,4},{16,24},{20,28},{24,16},{28,20},{1,9},{5... | collective-permute-start | bytes 73736 | tf_op jit(solution)/shard_map/ppermute | solution.py:408
  14.5 4.1 %collective-permute-start.6 = (f32[32,384]{1,0:T(8,128)S(1)}, f32[32,384]{1,0:T(8,128)S(1)}, u32[]{:S(2)}, u32[]{:S(2)}) collective-permute-start(f32[32,384]{1,0:T(8,128)S(1)} %pad_maximum_fusion.1), channel_id=1, source_target_pairs={{0,4},{4,0},{8,12},{12,8},{16,20},{20,16},{24,28},{28,24},{1,5},{5... | collective-permute-start | bytes 147464 | tf_op jit(solution)/shard_map/ppermute | solution.py:408
  18.6 4.7 %collective-permute-start.7 = (f32[64,384]{1,0:T(8,128)S(1)}, f32[64,384]{1,0:T(8,128)S(1)}, u32[]{:S(2)}, u32[]{:S(2)}) collective-permute-start(f32[64,384]{1,0:T(8,128)S(1)} %pad_maximum_fusion), channel_id=1, source_target_pairs={{0,2},{1,3},{2,0},{3,1},{4,6},{5,7},{6,4},{7,5},{8,10},{9,11},{10,... | collective-permute-start | bytes 294920 | tf_op jit(solution)/shard_map/ppermute | solution.py:408
  23.3 15.1 %collective-permute-start.8 = (f32[128,384]{1,0:T(8,128)S(1)}, f32[128,384]{1,0:T(8,128)S(1)}, u32[]{:S(2)}, u32[]{:S(2)}) collective-permute-start(f32[128,384]{1,0:T(8,128)S(1)} %get-tuple-element.106), channel_id=1, source_target_pairs={{0,1},{1,0},{2,3},{3,2},{4,5},{5,4},{6,7},{7,6},{8,9},{9,8},{10,11... | collective-permute-start | bytes 589832 | tf_op jit(solution)/shard_map/ppermute | solution.py:408
  23.4 3.8 %collective-permute-start = (f32[8,288]{1,0:T(8,128)S(1)}, f32[8,288]{1,0:T(8,128)S(1)}, u32[]{:S(2)}, u32[]{:S(2)}) collective-permute-start(f32[8,288]{1,0:T(8,128)S(1)} %get-tuple-element.56.refs_0_), channel_id=1, source_target_pairs={{0,4},{4,0},{8,12},{12,8},{16,20},{20,16},{24,28},{28,24},{1,5},{5... | collective-permute-start | bytes 27656 | tf_op jit(solution)/shard_map/ppermute | solution.py:399
  43.1 10.0 %collective-permute-start.9 = (f32[432,128]{1,0:T(8,128)S(1)}, f32[432,128]{1,0:T(8,128)S(1)}, u32[]{:S(2)}, u32[]{:S(2)}) collective-permute-start(f32[432,128]{1,0:T(8,128)S(1)} %get-tuple-element.66.refs_4_.refs_8_), channel_id=1, source_target_pairs={{0,4},{4,0},{8,12},{12,8},{16,20},{20,16},{24,28},{28,24},{1,5},{5... | collective-permute-start | bytes 663560 | tf_op jit(solution)/shard_map/ppermute | solution.py:399
  48.0 5.2 %collective-permute-start.10 = (f32[432,128]{1,0:T(8,128)S(1)}, f32[432,128]{1,0:T(8,128)S(1)}, u32[]{:S(2)}, u32[]{:S(2)}) collective-permute-start(f32[432,128]{1,0:T(8,128)S(1)} %get-tuple-element.67.refs_5_.refs_9_), channel_id=1, source_target_pairs={{4,8},{8,4},{12,16},{16,12},{20,24},{24,20},{5,9},{9,5},{13,17},{1... | collective-permute-start | bytes 663560 | tf_op jit(solution)/shard_map/ppermute | solution.py:399
  48.7 4.7 %collective-permute-start.11 = (f32[432,128]{1,0:T(8,128)S(1)}, f32[432,128]{1,0:T(8,128)S(1)}, u32[]{:S(2)}, u32[]{:S(2)}) collective-permute-start(f32[432,128]{1,0:T(8,128)S(1)} %get-tuple-element.68.refs_6_.refs_10_), channel_id=1, source_target_pairs={{0,1},{1,0},{2,3},{3,2},{4,5},{5,4},{6,7},{7,6},{8,9},{9,8},{10,11... | collective-permute-start | bytes 663560 | tf_op jit(solution)/shard_map/ppermute | solution.py:399
  56.8 8.1 %collective-permute-start.17 = (f32[8,128]{1,0:T(8,128)S(1)}, f32[8,128]{1,0:T(8,128)S(1)}, u32[]{:S(2)}, u32[]{:S(2)}) collective-permute-start(f32[8,128]{1,0:T(8,128)S(1)} %get-tuple-element.75), channel_id=1, source_target_pairs={{0,16},{4,20},{8,24},{12,28},{16,0},{20,4},{24,8},{28,12},{1,17},{... | collective-permute-start | bytes 12296 | tf_op jit(solution)/shard_map/ppermute | solution.py:408
  64.9 6.5 %collective-permute-start.18 = (f32[16,128]{1,0:T(8,128)S(1)}, f32[16,128]{1,0:T(8,128)S(1)}, u32[]{:S(2)}, u32[]{:S(2)}) collective-permute-start(f32[16,128]{1,0:T(8,128)S(1)} %pad_maximum_fusion.13), channel_id=1, source_target_pairs={{0,8},{4,12},{8,0},{12,4},{16,24},{20,28},{24,16},{28,20},{1,9},{5... | collective-permute-start | bytes 24584 | tf_op jit(solution)/shard_map/ppermute | solution.py:408
  71.4 3.7 %collective-permute-start.19 = (f32[32,128]{1,0:T(8,128)S(1)}, f32[32,128]{1,0:T(8,128)S(1)}, u32[]{:S(2)}, u32[]{:S(2)}) collective-permute-start(f32[32,128]{1,0:T(8,128)S(1)} %pad_maximum_fusion.8), channel_id=1, source_target_pairs={{0,4},{4,0},{8,12},{12,8},{16,20},{20,16},{24,28},{28,24},{1,5},{5... | collective-permute-start | bytes 49160 | tf_op jit(solution)/shard_map/ppermute | solution.py:408
  75.1 5.3 %collective-permute-start.20 = (f32[64,128]{1,0:T(8,128)S(1)}, f32[64,128]{1,0:T(8,128)S(1)}, u32[]{:S(2)}, u32[]{:S(2)}) collective-permute-start(f32[64,128]{1,0:T(8,128)S(1)} %pad_maximum_fusion.2), channel_id=1, source_target_pairs={{0,2},{1,3},{2,0},{3,1},{4,6},{5,7},{6,4},{7,5},{8,10},{9,11},{10,... | collective-permute-start | bytes 98312 | tf_op jit(solution)/shard_map/ppermute | solution.py:408
  80.4 3.7 %collective-permute-start.21 = (f32[128,128]{1,0:T(8,128)S(1)}, f32[128,128]{1,0:T(8,128)S(1)}, u32[]{:S(2)}, u32[]{:S(2)}) collective-permute-start(f32[128,128]{1,0:T(8,128)S(1)} %get-tuple-element.118), channel_id=1, source_target_pairs={{0,1},{1,0},{2,3},{3,2},{4,5},{5,4},{6,7},{7,6},{8,9},{9,8},{10,11... | collective-permute-start | bytes 196616 | tf_op jit(solution)/shard_map/ppermute | solution.py:408
  80.4 6.5 %collective-permute-start.13 = (f32[288,128]{1,0:T(8,128)S(1)}, f32[288,128]{1,0:T(8,128)S(1)}, u32[]{:S(2)}, u32[]{:S(2)}) collective-permute-start(f32[288,128]{1,0:T(8,128)S(1)} %get-tuple-element.71.refs_4_), channel_id=1, source_target_pairs={{0,4},{4,0},{8,12},{12,8},{16,20},{20,16},{24,28},{28,24},{1,5},{5... | collective-permute-start | bytes 442376 | tf_op jit(solution)/shard_map/ppermute | solution.py:399
  82.5 4.4 %collective-permute-start.14 = (f32[288,128]{1,0:T(8,128)S(1)}, f32[288,128]{1,0:T(8,128)S(1)}, u32[]{:S(2)}, u32[]{:S(2)}) collective-permute-start(f32[288,128]{1,0:T(8,128)S(1)} %get-tuple-element.72.refs_5_), channel_id=1, source_target_pairs={{4,8},{8,4},{12,16},{16,12},{20,24},{24,20},{5,9},{9,5},{13,17},{1... | collective-permute-start | bytes 442376 | tf_op jit(solution)/shard_map/ppermute | solution.py:399
  83.1 3.8 %collective-permute-start.15 = (f32[288,128]{1,0:T(8,128)S(1)}, f32[288,128]{1,0:T(8,128)S(1)}, u32[]{:S(2)}, u32[]{:S(2)}) collective-permute-start(f32[288,128]{1,0:T(8,128)S(1)} %get-tuple-element.73.refs_6_), channel_id=1, source_target_pairs={{0,1},{1,0},{2,3},{3,2},{4,5},{5,4},{6,7},{7,6},{8,9},{9,8},{10,11... | collective-permute-start | bytes 442376 | tf_op jit(solution)/shard_map/ppermute | solution.py:399
  83.4 3.6 %collective-permute-start.16 = (f32[288,128]{1,0:T(8,128)S(1)}, f32[288,128]{1,0:T(8,128)S(1)}, u32[]{:S(2)}, u32[]{:S(2)}) collective-permute-start(f32[288,128]{1,0:T(8,128)S(1)} %get-tuple-element.74.refs_7_), channel_id=1, source_target_pairs={{1,2},{2,1},{5,6},{6,5},{9,10},{10,9},{13,14},{14,13},{17,18},{18,... | collective-permute-start | bytes 442376 | tf_op jit(solution)/shard_map/ppermute | solution.py:399
  92.2 6.1 %collective-permute-start.26 = (f32[8,128]{1,0:T(8,128)S(1)}, f32[8,128]{1,0:T(8,128)S(1)}, u32[]{:S(2)}, u32[]{:S(2)}) collective-permute-start(f32[8,128]{1,0:T(8,128)S(1)} %get-tuple-element.82), channel_id=1, source_target_pairs={{0,16},{4,20},{8,24},{12,28},{16,0},{20,4},{24,8},{28,12},{1,17},{... | collective-permute-start | bytes 12296 | tf_op jit(solution)/shard_map/ppermute | solution.py:408
  98.3 5.9 %collective-permute-start.27 = (f32[16,128]{1,0:T(8,128)S(1)}, f32[16,128]{1,0:T(8,128)S(1)}, u32[]{:S(2)}, u32[]{:S(2)}) collective-permute-start(f32[16,128]{1,0:T(8,128)S(1)} %pad_maximum_fusion.14), channel_id=1, source_target_pairs={{0,8},{4,12},{8,0},{12,4},{16,24},{20,28},{24,16},{28,20},{1,9},{5... | collective-permute-start | bytes 24584 | tf_op jit(solution)/shard_map/ppermute | solution.py:408
  104.2 3.7 %collective-permute-start.28 = (f32[32,128]{1,0:T(8,128)S(1)}, f32[32,128]{1,0:T(8,128)S(1)}, u32[]{:S(2)}, u32[]{:S(2)}) collective-permute-start(f32[32,128]{1,0:T(8,128)S(1)} %pad_maximum_fusion.9), channel_id=1, source_target_pairs={{0,4},{4,0},{8,12},{12,8},{16,20},{20,16},{24,28},{28,24},{1,5},{5... | collective-permute-start | bytes 49160 | tf_op jit(solution)/shard_map/ppermute | solution.py:408
  108.0 5.1 %collective-permute-start.29 = (f32[64,128]{1,0:T(8,128)S(1)}, f32[64,128]{1,0:T(8,128)S(1)}, u32[]{:S(2)}, u32[]{:S(2)}) collective-permute-start(f32[64,128]{1,0:T(8,128)S(1)} %pad_maximum_fusion.3), channel_id=1, source_target_pairs={{0,2},{1,3},{2,0},{3,1},{4,6},{5,7},{6,4},{7,5},{8,10},{9,11},{10,... | collective-permute-start | bytes 98312 | tf_op jit(solution)/shard_map/ppermute | solution.py:408
  113.1 3.9 %collective-permute-start.30 = (f32[128,128]{1,0:T(8,128)S(1)}, f32[128,128]{1,0:T(8,128)S(1)}, u32[]{:S(2)}, u32[]{:S(2)}) collective-permute-start(f32[128,128]{1,0:T(8,128)S(1)} %get-tuple-element.116), channel_id=1, source_target_pairs={{0,1},{1,0},{2,3},{3,2},{4,5},{5,4},{6,7},{7,6},{8,9},{9,8},{10,11... | collective-permute-start | bytes 196616 | tf_op jit(solution)/shard_map/ppermute | solution.py:408
  113.1 9.0 %collective-permute-start.22 = (f32[288,128]{1,0:T(8,128)S(1)}, f32[288,128]{1,0:T(8,128)S(1)}, u32[]{:S(2)}, u32[]{:S(2)}) collective-permute-start(f32[288,128]{1,0:T(8,128)S(1)} %get-tuple-element.78.refs_4_), channel_id=1, source_target_pairs={{0,4},{4,0},{8,12},{12,8},{16,20},{20,16},{24,28},{28,24},{1,5},{5... | collective-permute-start | bytes 442376 | tf_op jit(solution)/shard_map/ppermute | solution.py:399
  115.2 6.9 %collective-permute-start.23 = (f32[288,128]{1,0:T(8,128)S(1)}, f32[288,128]{1,0:T(8,128)S(1)}, u32[]{:S(2)}, u32[]{:S(2)}) collective-permute-start(f32[288,128]{1,0:T(8,128)S(1)} %get-tuple-element.79.refs_5_), channel_id=1, source_target_pairs={{4,8},{8,4},{12,16},{16,12},{20,24},{24,20},{5,9},{9,5},{13,17},{1... | collective-permute-start | bytes 442376 | tf_op jit(solution)/shard_map/ppermute | solution.py:399
  115.9 6.2 %collective-permute-start.24 = (f32[288,128]{1,0:T(8,128)S(1)}, f32[288,128]{1,0:T(8,128)S(1)}, u32[]{:S(2)}, u32[]{:S(2)}) collective-permute-start(f32[288,128]{1,0:T(8,128)S(1)} %get-tuple-element.80.refs_6_), channel_id=1, source_target_pairs={{0,1},{1,0},{2,3},{3,2},{4,5},{5,4},{6,7},{7,6},{8,9},{9,8},{10,11... | collective-permute-start | bytes 442376 | tf_op jit(solution)/shard_map/ppermute | solution.py:399
  116.1 6.0 %collective-permute-start.25 = (f32[288,128]{1,0:T(8,128)S(1)}, f32[288,128]{1,0:T(8,128)S(1)}, u32[]{:S(2)}, u32[]{:S(2)}) collective-permute-start(f32[288,128]{1,0:T(8,128)S(1)} %get-tuple-element.81.refs_7_), channel_id=1, source_target_pairs={{1,2},{2,1},{5,6},{6,5},{9,10},{10,9},{13,14},{14,13},{17,18},{18,... | collective-permute-start | bytes 442376 | tf_op jit(solution)/shard_map/ppermute | solution.py:399
  127.5 4.6 %collective-permute-start.35 = (f32[8,128]{1,0:T(8,128)S(1)}, f32[8,128]{1,0:T(8,128)S(1)}, u32[]{:S(2)}, u32[]{:S(2)}) collective-permute-start(f32[8,128]{1,0:T(8,128)S(1)} %get-tuple-element.89), channel_id=1, source_target_pairs={{0,16},{4,20},{8,24},{12,28},{16,0},{20,4},{24,8},{28,12},{1,17},{... | collective-permute-start | bytes 12296 | tf_op jit(solution)/shard_map/ppermute | solution.py:408
  132.1 3.7 %collective-permute-start.36 = (f32[16,128]{1,0:T(8,128)S(1)}, f32[16,128]{1,0:T(8,128)S(1)}, u32[]{:S(2)}, u32[]{:S(2)}) collective-permute-start(f32[16,128]{1,0:T(8,128)S(1)} %pad_maximum_fusion.15), channel_id=1, source_target_pairs={{0,8},{4,12},{8,0},{12,4},{16,24},{20,28},{24,16},{28,20},{1,9},{5... | collective-permute-start | bytes 24584 | tf_op jit(solution)/shard_map/ppermute | solution.py:408
  135.8 4.2 %collective-permute-start.37 = (f32[32,128]{1,0:T(8,128)S(1)}, f32[32,128]{1,0:T(8,128)S(1)}, u32[]{:S(2)}, u32[]{:S(2)}) collective-permute-start(f32[32,128]{1,0:T(8,128)S(1)} %pad_maximum_fusion.10), channel_id=1, source_target_pairs={{0,4},{4,0},{8,12},{12,8},{16,20},{20,16},{24,28},{28,24},{1,5},{5... | collective-permute-start | bytes 49160 | tf_op jit(solution)/shard_map/ppermute | solution.py:408
  140.0 4.5 %collective-permute-start.38 = (f32[64,128]{1,0:T(8,128)S(1)}, f32[64,128]{1,0:T(8,128)S(1)}, u32[]{:S(2)}, u32[]{:S(2)}) collective-permute-start(f32[64,128]{1,0:T(8,128)S(1)} %pad_maximum_fusion.4), channel_id=1, source_target_pairs={{0,2},{1,3},{2,0},{3,1},{4,6},{5,7},{6,4},{7,5},{8,10},{9,11},{10,... | collective-permute-start | bytes 98312 | tf_op jit(solution)/shard_map/ppermute | solution.py:408
  144.5 8.9 %collective-permute-start.31 = (f32[288,128]{1,0:T(8,128)S(1)}, f32[288,128]{1,0:T(8,128)S(1)}, u32[]{:S(2)}, u32[]{:S(2)}) collective-permute-start(f32[288,128]{1,0:T(8,128)S(1)} %get-tuple-element.85.refs_4_), channel_id=1, source_target_pairs={{0,4},{4,0},{8,12},{12,8},{16,20},{20,16},{24,28},{28,24},{1,5},{5... | collective-permute-start | bytes 442376 | tf_op jit(solution)/shard_map/ppermute | solution.py:399
  146.5 6.9 %collective-permute-start.32 = (f32[288,128]{1,0:T(8,128)S(1)}, f32[288,128]{1,0:T(8,128)S(1)}, u32[]{:S(2)}, u32[]{:S(2)}) collective-permute-start(f32[288,128]{1,0:T(8,128)S(1)} %get-tuple-element.86.refs_5_), channel_id=1, source_target_pairs={{4,8},{8,4},{12,16},{16,12},{20,24},{24,20},{5,9},{9,5},{13,17},{1... | collective-permute-start | bytes 442376 | tf_op jit(solution)/shard_map/ppermute | solution.py:399
  147.1 6.2 %collective-permute-start.33 = (f32[288,128]{1,0:T(8,128)S(1)}, f32[288,128]{1,0:T(8,128)S(1)}, u32[]{:S(2)}, u32[]{:S(2)}) collective-permute-start(f32[288,128]{1,0:T(8,128)S(1)} %get-tuple-element.87.refs_6_), channel_id=1, source_target_pairs={{0,1},{1,0},{2,3},{3,2},{4,5},{5,4},{6,7},{7,6},{8,9},{9,8},{10,11... | collective-permute-start | bytes 442376 | tf_op jit(solution)/shard_map/ppermute | solution.py:399
  147.3 6.0 %collective-permute-start.34 = (f32[288,128]{1,0:T(8,128)S(1)}, f32[288,128]{1,0:T(8,128)S(1)}, u32[]{:S(2)}, u32[]{:S(2)}) collective-permute-start(f32[288,128]{1,0:T(8,128)S(1)} %get-tuple-element.88.refs_7_), channel_id=1, source_target_pairs={{1,2},{2,1},{5,6},{6,5},{9,10},{10,9},{13,14},{14,13},{17,18},{18,... | collective-permute-start | bytes 442376 | tf_op jit(solution)/shard_map/ppermute | solution.py:399
  158.7 4.6 %collective-permute-start.44 = (f32[8,128]{1,0:T(8,128)S(1)}, f32[8,128]{1,0:T(8,128)S(1)}, u32[]{:S(2)}, u32[]{:S(2)}) collective-permute-start(f32[8,128]{1,0:T(8,128)S(1)} %get-tuple-element.96), channel_id=1, source_target_pairs={{0,16},{4,20},{8,24},{12,28},{16,0},{20,4},{24,8},{28,12},{1,17},{... | collective-permute-start | bytes 12296 | tf_op jit(solution)/shard_map/ppermute | solution.py:408
  163.3 4.2 %collective-permute-start.45 = (f32[16,128]{1,0:T(8,128)S(1)}, f32[16,128]{1,0:T(8,128)S(1)}, u32[]{:S(2)}, u32[]{:S(2)}) collective-permute-start(f32[16,128]{1,0:T(8,128)S(1)} %pad_maximum_fusion.16), channel_id=1, source_target_pairs={{0,8},{4,12},{8,0},{12,4},{16,24},{20,28},{24,16},{28,20},{1,9},{5... | collective-permute-start | bytes 24584 | tf_op jit(solution)/shard_map/ppermute | solution.py:408
  167.5 3.7 %collective-permute-start.46 = (f32[32,128]{1,0:T(8,128)S(1)}, f32[32,128]{1,0:T(8,128)S(1)}, u32[]{:S(2)}, u32[]{:S(2)}) collective-permute-start(f32[32,128]{1,0:T(8,128)S(1)} %pad_maximum_fusion.11), channel_id=1, source_target_pairs={{0,4},{4,0},{8,12},{12,8},{16,20},{20,16},{24,28},{28,24},{1,5},{5... | collective-permute-start | bytes 49160 | tf_op jit(solution)/shard_map/ppermute | solution.py:408
  171.3 5.0 %collective-permute-start.47 = (f32[64,128]{1,0:T(8,128)S(1)}, f32[64,128]{1,0:T(8,128)S(1)}, u32[]{:S(2)}, u32[]{:S(2)}) collective-permute-start(f32[64,128]{1,0:T(8,128)S(1)} %pad_maximum_fusion.5), channel_id=1, source_target_pairs={{0,2},{1,3},{2,0},{3,1},{4,6},{5,7},{6,4},{7,5},{8,10},{9,11},{10,... | collective-permute-start | bytes 98312 | tf_op jit(solution)/shard_map/ppermute | solution.py:408
  176.3 3.8 %collective-permute-start.48 = (f32[128,128]{1,0:T(8,128)S(1)}, f32[128,128]{1,0:T(8,128)S(1)}, u32[]{:S(2)}, u32[]{:S(2)}) collective-permute-start(f32[128,128]{1,0:T(8,128)S(1)} %get-tuple-element.112), channel_id=1, source_target_pairs={{0,1},{1,0},{2,3},{3,2},{4,5},{5,4},{6,7},{7,6},{8,9},{9,8},{10,11... | collective-permute-start | bytes 196616 | tf_op jit(solution)/shard_map/ppermute | solution.py:408
  176.3 8.9 %collective-permute-start.40 = (f32[288,128]{1,0:T(8,128)S(1)}, f32[288,128]{1,0:T(8,128)S(1)}, u32[]{:S(2)}, u32[]{:S(2)}) collective-permute-start(f32[288,128]{1,0:T(8,128)S(1)} %get-tuple-element.92.refs_4_), channel_id=1, source_target_pairs={{0,4},{4,0},{8,12},{12,8},{16,20},{20,16},{24,28},{28,24},{1,5},{5... | collective-permute-start | bytes 442376 | tf_op jit(solution)/shard_map/ppermute | solution.py:399
  178.3 6.9 %collective-permute-start.41 = (f32[288,128]{1,0:T(8,128)S(1)}, f32[288,128]{1,0:T(8,128)S(1)}, u32[]{:S(2)}, u32[]{:S(2)}) collective-permute-start(f32[288,128]{1,0:T(8,128)S(1)} %get-tuple-element.93.refs_5_), channel_id=1, source_target_pairs={{4,8},{8,4},{12,16},{16,12},{20,24},{24,20},{5,9},{9,5},{13,17},{1... | collective-permute-start | bytes 442376 | tf_op jit(solution)/shard_map/ppermute | solution.py:399
  178.9 6.2 %collective-permute-start.42 = (f32[288,128]{1,0:T(8,128)S(1)}, f32[288,128]{1,0:T(8,128)S(1)}, u32[]{:S(2)}, u32[]{:S(2)}) collective-permute-start(f32[288,128]{1,0:T(8,128)S(1)} %get-tuple-element.94.refs_6_), channel_id=1, source_target_pairs={{0,1},{1,0},{2,3},{3,2},{4,5},{5,4},{6,7},{7,6},{8,9},{9,8},{10,11... | collective-permute-start | bytes 442376 | tf_op jit(solution)/shard_map/ppermute | solution.py:399
  179.1 6.0 %collective-permute-start.43 = (f32[288,128]{1,0:T(8,128)S(1)}, f32[288,128]{1,0:T(8,128)S(1)}, u32[]{:S(2)}, u32[]{:S(2)}) collective-permute-start(f32[288,128]{1,0:T(8,128)S(1)} %get-tuple-element.95.refs_7_), channel_id=1, source_target_pairs={{1,2},{2,1},{5,6},{6,5},{9,10},{10,9},{13,14},{14,13},{17,18},{18,... | collective-permute-start | bytes 442376 | tf_op jit(solution)/shard_map/ppermute | solution.py:399
  187.3 5.0 %collective-permute-start.49 = (f32[8,128]{1,0:T(8,128)S(1)}, f32[8,128]{1,0:T(8,128)S(1)}, u32[]{:S(2)}, u32[]{:S(2)}) collective-permute-start(f32[8,128]{1,0:T(8,128)S(1)} %get-tuple-element.105), channel_id=1, source_target_pairs={{0,16},{4,20},{8,24},{12,28},{16,0},{20,4},{24,8},{28,12},{1,17},{... | collective-permute-start | bytes 12296 | tf_op jit(solution)/shard_map/ppermute | solution.py:408
  192.3 3.7 %collective-permute-start.50 = (f32[16,128]{1,0:T(8,128)S(1)}, f32[16,128]{1,0:T(8,128)S(1)}, u32[]{:S(2)}, u32[]{:S(2)}) collective-permute-start(f32[16,128]{1,0:T(8,128)S(1)} %pad_maximum_fusion.17), channel_id=1, source_target_pairs={{0,8},{4,12},{8,0},{12,4},{16,24},{20,28},{24,16},{28,20},{1,9},{5... | collective-permute-start | bytes 24584 | tf_op jit(solution)/shard_map/ppermute | solution.py:408
  196.0 3.7 %collective-permute-start.51 = (f32[32,128]{1,0:T(8,128)S(1)}, f32[32,128]{1,0:T(8,128)S(1)}, u32[]{:S(2)}, u32[]{:S(2)}) collective-permute-start(f32[32,128]{1,0:T(8,128)S(1)} %pad_maximum_fusion.12), channel_id=1, source_target_pairs={{0,4},{4,0},{8,12},{12,8},{16,20},{20,16},{24,28},{28,24},{1,5},{5... | collective-permute-start | bytes 49160 | tf_op jit(solution)/shard_map/ppermute | solution.py:408
  199.7 4.7 %collective-permute-start.52 = (f32[64,128]{1,0:T(8,128)S(1)}, f32[64,128]{1,0:T(8,128)S(1)}, u32[]{:S(2)}, u32[]{:S(2)}) collective-permute-start(f32[64,128]{1,0:T(8,128)S(1)} %pad_maximum_fusion.6), channel_id=1, source_target_pairs={{0,2},{1,3},{2,0},{3,1},{4,6},{5,7},{6,4},{7,5},{8,10},{9,11},{10,... | collective-permute-start | bytes 98312 | tf_op jit(solution)/shard_map/ppermute | solution.py:408
  (14 other events, 46.7 us)

commit v4 on v1

--- a/solution.py
+++ b/solution.py
@@ -75,7 +75,17 @@
     return x[:, :cols] + x[:, cols:]
 
 
-def apply_local(matrix, codes_row, codes_lanes, slot_pieces, row_pieces, out_pieces, write, less=None):
+def fetch(matrix, held, arrived):
+    chunk = held.shape[0] // SIDES
+    pieces = []
+    for c in range(SIDES):
+        rows = pl.ds(c * chunk, chunk)
+        pieces.append(pltpu.make_async_copy(matrix.at[rows], held.at[rows], arrived.at[c]))
+        pieces[c].start()
+    return pieces, held
+
+
+def apply_local(fetched, codes_row, codes_lanes, slot_pieces, row_pieces, out_pieces, write, less=None):
     total = slot_pieces.shape[0]
     chunk = total // SIDES
 
@@ -83,14 +93,16 @@
         row_pieces[start : start + chunk, :] = rows.astype(jnp.bfloat16)
 
     to_rows(codes_lanes, slot_pieces, keep)
-    apply_rows(matrix, codes_row, row_pieces, out_pieces, write, less)
-
-
-def apply_rows(matrix, codes_row, row_pieces, out_pieces, write, less=None):
+    apply_rows(fetched, codes_row, row_pieces, out_pieces, write, less)
+
+
+def apply_rows(fetched, codes_row, row_pieces, out_pieces, write, less=None):
+    coming, matrix = fetched
     total = row_pieces.shape[0]
     chunk = total // SIDES
     cols = row_pieces.shape[1] // 2
     for c in range(SIDES):
+        coming[c].wait()
         high, low = two_pieces(matrix[c * chunk : (c + 1) * chunk, :])
         product = halves(one_pass(high, row_pieces[...])) + one_pass(low, row_pieces[:, :cols])
         if less is not None:
@@ -184,6 +196,8 @@
     outs = refs[8:12]
     modes_out = refs[12]
     slot_pieces, row_pieces, out_pieces = refs[13:16]
+    schur = fetch(schur, refs[16], refs[17])
+    flex = fetch(flex, refs[18], refs[19])
     total = codes_lanes.shape[0]
     cap = total // SIDES
     half = cap // 2
@@ -213,6 +227,7 @@
     outs = refs[7:11]
     start_out, inverse_out = refs[11:13]
     slot_pieces, row_pieces, out_pieces = refs[13:16]
+    flex = fetch(flex, refs[16], refs[17])
     cap = codes_lanes.shape[0] // SIDES
     wide = gathered.shape[0]
     spread = lane_spread(mode_count, GROUP)
@@ -263,6 +278,7 @@
     outs = refs[9:13]
     gap_out, parts_out = refs[13:15]
     slot_pieces, row_pieces, out_pieces = refs[15:18]
+    schur = fetch(schur, refs[18], refs[19])
     cap = codes_lanes.shape[0] // SIDES
     for side in range(SIDES):
         block = sent[side][0:cap, :] - received[side][0:cap, :]
@@ -291,6 +307,8 @@
     states_out = take(counts[1])
     (parts_out,) = take(1)
     slot_pieces, row_pieces, out_pieces = take(3)
+    if stage < 5:
+        matrix = fetch(matrix, *take(2))
     total = codes_lanes.shape[0]
     cap = total // SIDES
     coefficients = exact(inverse_rows[...], gathered[...])
@@ -359,17 +377,23 @@
     out[...] = residual[...] + three_pass(modes[...], coefficients)
 
 
-def call(kernel, name, outs, inputs, scratch=(), smem=(), extra=0):
-    vmem = pl.BlockSpec(memory_space=pltpu.VMEM)
-    scalar = pl.BlockSpec(memory_space=pltpu.SMEM)
+def call(kernel, name, outs, inputs, scratch=(), smem=(), left=()):
+    spaces = [pltpu.VMEM] * len(inputs)
+    for n in smem:
+        spaces[n] = pltpu.SMEM
+    for n in left:
+        spaces[n] = pl.ANY
+    shapes = []
+    for shape in outs:
+        shapes.append(jax.ShapeDtypeStruct(shape, jnp.float32) if isinstance(shape, tuple) else shape)
     return pl.pallas_call(
         kernel,
         name=name,
-        out_shape=[jax.ShapeDtypeStruct(shape, jnp.float32) if isinstance(shape, tuple) else shape for shape in outs],
-        in_specs=[scalar if n in smem else vmem for n in range(len(inputs))],
-        out_specs=[vmem] * len(outs),
+        out_shape=shapes,
+        in_specs=[pl.BlockSpec(memory_space=space) for space in spaces],
+        out_specs=[pl.BlockSpec(memory_space=pltpu.VMEM)] * len(outs),
         scratch_shapes=list(scratch),
-        compiler_params=pltpu.CompilerParams(vmem_limit_bytes=28 * 1024 * 1024 + extra),
+        compiler_params=pltpu.CompilerParams(vmem_limit_bytes=58 * 1024 * 1024),
     )(*inputs)
 
 
@@ -406,7 +430,7 @@
     block = [(cap, cols)] * SIDES
     whole = (total, cols)
     parts = (wide, cols)
-    table = 8 * wide * (wide + cols)
+    brought = [pltpu.VMEM((total, total), jnp.float32), pltpu.SemaphoreType.DMA((SIDES,))]
 
     shown = call(
         functools.partial(modes_kernel, mode_count),
@@ -416,7 +440,6 @@
         + [jax.ShapeDtypeStruct((1, total), jnp.int32)],
         [route_codes[0], modes, coarse_inverse, rigid_load, place],
         smem=(4,),
-        extra=table,
     )
     own, (inverse_load, codes_lanes, own_pieces, codes_row) = shown[:4], shown[4:]
     gathered = everywhere(inverse_load)
@@ -426,7 +449,8 @@
         "operators_on_modes",
         [(cap // 2, 4 * GROUP)] * SIDES + [(total, 4 * GROUP)],
         [flex, schur, codes_row, codes_lanes, *own, *partner],
-        scratch,
+        scratch + brought * 2,
+        left=(0, 1),
     )
     slabs, slot_modes = shown[:4], shown[4]
     shown = call(
@@ -434,9 +458,9 @@
         "start",
         [(cap + cap // 2, cols)] * SIDES + [whole, (5 * GROUP, wide)],
         [flex, gap, codes_row, codes_lanes, *slabs, gathered, slot_modes, place],
-        scratch,
+        scratch + brought,
         smem=(10,),
-        extra=table,
+        left=(0,),
     )
     sent, (start, inverse_rows) = shown[:4], shown[4:]
     received = exchange(sent)
@@ -446,7 +470,8 @@
         "stage_1",
         block + [whole, parts],
         [schur, codes_row, codes_lanes, *received, *sent, own_pieces],
-        scratch,
+        scratch + brought,
+        left=(0,),
     )
     sent, (gap_jump, components) = shown[:4], shown[4:]
 
@@ -457,11 +482,10 @@
         inputs += [own_pieces, gathered, inverse_rows, slot_modes, *states_in]
         outs = [whole] * 2 + [parts]
         kernel = functools.partial(stage_kernel, number, (len(states_in), 2))
+        name = "stage_%d" % number
         if matrix is None:
-            kernel = functools.partial(kernel, None)
-        else:
-            inputs, outs = [matrix] + inputs, block + outs
-        return call(kernel, "stage_%d" % number, outs, inputs, scratch)
+            return call(functools.partial(kernel, None), name, outs, inputs, scratch)
+        return call(kernel, name, block + outs, [matrix] + inputs, scratch + brought, left=(0,))
 
     shown = stage(2, flex, [gap_jump], sent, components)
     sent, (precond, residual, components) = shown[:4], shown[4:]

time: 225 us -> 180 us (0.80)
  local copies, waits for them, and re-layouts: 87.4 us -> 7.37 us
  Pallas kernels: 35.9 us -> 66.2 us
  starting transfers between devices: 69.8 us -> 73.7 us
    unnamed x195 -> x61, local copies, waits for them, and re-layouts: 87.4 us -> 7.37 us
    pallas_call x10, Pallas kernels: 35.9 us -> 66.2 us  [call(): pl.pallas_call(kernel, name=name, out_shape=shapes, in_specs=[pl.BlockSpe...]
    all_to_all x6, starting transfers between devices: 44.3 us -> 48.1 us  [everywhere(): lax.all_to_all(stacked, ('sub', 'layer'), split_axis=0, concat_axis=0, ti...]
  transfers between devices with their start and end apart: 30 -> 30, of which waited for: 7 -> 7; matrix products, arithmetic and copies ran while one was open for 0% -> 0% of each run, Pallas kernels for 4% -> 8%
where the time goes in v4:
time: 180 us; the launch traced here: 179 us
  starting transfers between devices  73.7 us (41%)
  Pallas kernels  66.2 us (37%)
  waiting for transfers between devices  30 us (17%)
  local copies, waits for them, and re-layouts  7.37 us (4%)
    pallas_call x10, Pallas kernels, call(): pl.pallas_call(kernel, name=name, out_shape=shapes, in_specs=[pl.BlockSpe...  66.2 us
    all_to_all x6, starting transfers between devices, everywhere(): lax.all_to_all(stacked, ('sub', 'layer'), split_axis=0, concat_axis=0, ti...  48.1 us
    ppermute x24, waiting for transfers between devices, exchange(): received.append(lax.ppermute(block, axis, pairs))  27.1 us
    ppermute x24, starting transfers between devices, exchange(): received.append(lax.ppermute(block, axis, pairs))  25.6 us
    unnamed x61, local copies, waits for them, and re-layouts  7.37 us
  transfers between devices with their start and end apart: 30, of which 7 were waited for; matrix products, arithmetic and copies ran while one was open for 0% of the time, Pallas kernels for 8%

profile of v4, /device:TPU:0, one launch (start us, length us, event | category | flops | bytes accessed | tf_op | source)
XLA Modules:
  0.0 179.0 jit_solution(11521076809929234762)
XLA Ops:
  0.6 1.4 copy.11
  2.6 2.5 %modes_to_slots.1 = (f32[8,288]{1,0:T(8,128)}, f32[8,288]{1,0:T(8,128)}, f32[8,288]{1,0:T(8,128)}, f32[8,288]{1,0:T(8,128)}, f32[256,384]{1,0:T(8,128)}, /*index...) custom-call(s32[1,1152]{1,0:T(1,128)} %bitcast.45, f32[6,1152]{1,0:T(8,128)} %bitcast.39, f32[6,192]{1,0:T(8,128)} %inverse.1, ...), custom_call_target="tpu_custom_call" | custom-call | tf_op jit(solution)/shard_map/modes_to_slots/pallas_call | solution.py:389
  5.0 7.3 %all-to-all-start = ((f32[32,8,384]{2,1,0:T(8,128)}), f32[32,8,384]{2,1,0:T(8,128)S(1)}, u32[]{:S(2)}, u32[]{:S(2)}) async-start(f32[32,8,384]{2,1,0:T(8,128)} %bitcast.38), calls=%async_computation | async-start | bytes 786432 | tf_op jit(solution)/shard_map/all_to_all | solution.py:412
  12.4 1.8 %collective-permute-start = (f32[8,288]{1,0:T(8,128)}, f32[8,288]{1,0:T(8,128)S(1)}, u32[]{:S(2)}, u32[]{:S(2)}) collective-permute-start(f32[8,288]{1,0:T(8,128)} %get-tuple-element.56.refs_0_), channel_id=1, source_target_pairs={{0,4},{4,0},{8,12},{12,8},{16,20},{20,16},{24,28},{28,24},{1,5},{5... | collective-permute-start | bytes 27656 | tf_op jit(solution)/shard_map/ppermute | solution.py:407
  14.2 0.7 collective-permute-start.1
  14.9 0.7 collective-permute-start.3
  15.6 1.3 collective-permute-done.refs_4_
  17.5 10.0 %operators_on_modes.1 = (f32[144,128]{1,0:T(8,128)}, f32[144,128]{1,0:T(8,128)}, f32[144,128]{1,0:T(8,128)}, f32[144,128]{1,0:T(8,128)}, f32[1152,128]{1,0:T(8,128)}) custom-call(f32[1152,1152]{1,0:T(8,128)} %bitcast.23, f32[1152,1152]{1,0:T(8,128)} %bitcast.27, s32[1,1152]{1,0:T(1,128)} %get-tuple-element.55.codes_row, ...), custom_call_target="tpu_custom_call" | custom-call | tf_op jit(solution)/shard_map/operators_on_modes/pallas_call | solution.py:389
  27.6 0.7 copy-done.4
  28.3 7.6 %start.1 = (f32[432,128]{1,0:T(8,128)}, f32[432,128]{1,0:T(8,128)}, f32[432,128]{1,0:T(8,128)}, f32[432,128]{1,0:T(8,128)}, f32[1152,128]{1,0:T(8,128)}, /*index=5*/f32[160,256]{1,0:T(8,128)}) custom-call(f32[1152,1152]{1,0:T(8,128)} %bitcast.24, f32[1152,128]{1,0:T(8,128)} %bitcast.32, s32[1,1152]{1,0:T(1,128)} %get-tuple-element.55.codes_row, ...), custom_call_target="tpu_custom_call" | custom-call | tf_op jit(solution)/shard_map/start/pallas_call | solution.py:389
  35.9 4.5 %collective-permute-start.4 = (f32[432,128]{1,0:T(8,128)}, f32[432,128]{1,0:T(8,128)S(1)}, u32[]{:S(2)}, u32[]{:S(2)}) collective-permute-start(f32[432,128]{1,0:T(8,128)} %get-tuple-element.66.refs_4_.refs_8_), channel_id=1, source_target_pairs={{0,4},{4,0},{8,12},{12,8},{16,20},{20,16},{24,28},{28,24},{1,5},{5... | collective-permute-start | bytes 663560 | tf_op jit(solution)/shard_map/ppermute | solution.py:407
  40.4 0.8 collective-permute-start.5
  41.3 3.3 %collective-permute-start.6 = (f32[432,128]{1,0:T(8,128)}, f32[432,128]{1,0:T(8,128)S(1)}, u32[]{:S(2)}, u32[]{:S(2)}) collective-permute-start(f32[432,128]{1,0:T(8,128)} %get-tuple-element.68.refs_6_.refs_10_), channel_id=1, source_target_pairs={{0,1},{1,0},{2,3},{3,2},{4,5},{5,4},{6,7},{7,6},{8,9},{9,8},{10,11... | collective-permute-start | bytes 663560 | tf_op jit(solution)/shard_map/ppermute | solution.py:407
  44.5 0.7 collective-permute-start.7
  45.2 0.6 collective-permute-done.6.refs_2_.refs_14_
  46.6 6.8 %stage_1.1 = (f32[288,128]{1,0:T(8,128)}, f32[288,128]{1,0:T(8,128)}, f32[288,128]{1,0:T(8,128)}, f32[288,128]{1,0:T(8,128)}, f32[1152,128]{1,0:T(8,128)}, /*index=5*/f32[256,128]{1,0:T(8,128)}) custom-call(f32[1152,1152]{1,0:T(8,128)} %bitcast.28, s32[1,1152]{1,0:T(1,128)} %get-tuple-element.55.codes_row, s32[1152,128]{1,0:T(8,128)} %get-tuple-element.54.codes_lanes, ...), custom_call_target="tpu_custom_call" | custom-call | tf_op jit(solution)/shard_map/stage_1/pallas_call | solution.py:389
  53.5 13.2 %all-to-all-start.1 = ((f32[32,8,128]{2,1,0:T(8,128)}), f32[32,8,128]{2,1,0:T(8,128)S(1)}, u32[]{:S(2)}, u32[]{:S(2)}) async-start(f32[32,8,128]{2,1,0:T(8,128)} %bitcast.43), calls=%async_computation.1 | async-start | bytes 262144 | tf_op jit(solution)/shard_map/all_to_all | solution.py:412
  66.7 1.8 %collective-permute-start.8 = (f32[288,128]{1,0:T(8,128)}, f32[288,128]{1,0:T(8,128)S(1)}, u32[]{:S(2)}, u32[]{:S(2)}) collective-permute-start(f32[288,128]{1,0:T(8,128)} %get-tuple-element.71.refs_4_), channel_id=1, source_target_pairs={{0,4},{4,0},{8,12},{12,8},{16,20},{20,16},{24,28},{28,24},{1,5},{5... | collective-permute-start | bytes 442376 | tf_op jit(solution)/shard_map/ppermute | solution.py:407
  68.5 0.7 collective-permute-start.9
  69.3 0.7 collective-permute-start.11
  70.0 6.4 %collective-permute-done.8.refs_0_ = f32[288,128]{1,0:T(8,128)S(1)} collective-permute-done((f32[288,128]{1,0:T(8,128)}, f32[288,128]{1,0:T(8,128)S(1)}, u32[]{:S(2)}, u32[]{:S(2)}) %collective-permute-start.8) | collective-permute-done | bytes 147488 | tf_op jit(solution)/shard_map/ppermute | solution.py:407
  77.2 8.6 %stage_2.1 = (f32[288,128]{1,0:T(8,128)}, f32[288,128]{1,0:T(8,128)}, f32[288,128]{1,0:T(8,128)}, f32[288,128]{1,0:T(8,128)}, f32[1152,128]{1,0:T(8,128)}, /*index=5*/f32[1152,128]{1,0:T(8,128)}, f32[256,128]{1,0:T(8,128)}) custom-call(f32[1152,1152]{1,0:T(8,128)} %bitcast.25, s32[1,1152]{1,0:T(1,128)} %get-tuple-element.55.codes_row, ...), custom_call_target="tpu_custom_call" | custom-call | tf_op jit(solution)/shard_map/stage_2/pallas_call | solution.py:389
  85.8 6.8 %all-to-all-start.2 = ((f32[32,8,128]{2,1,0:T(8,128)}), f32[32,8,128]{2,1,0:T(8,128)S(1)}, u32[]{:S(2)}, u32[]{:S(2)}) async-start(f32[32,8,128]{2,1,0:T(8,128)} %bitcast.41), calls=%async_computation.2 | async-start | bytes 262144 | tf_op jit(solution)/shard_map/all_to_all | solution.py:412
  92.7 1.8 %collective-permute-start.12 = (f32[288,128]{1,0:T(8,128)}, f32[288,128]{1,0:T(8,128)S(1)}, u32[]{:S(2)}, u32[]{:S(2)}) collective-permute-start(f32[288,128]{1,0:T(8,128)} %get-tuple-element.78.refs_4_), channel_id=1, source_target_pairs={{0,4},{4,0},{8,12},{12,8},{16,20},{20,16},{24,28},{28,24},{1,5},{5... | collective-permute-start | bytes 442376 | tf_op jit(solution)/shard_map/ppermute | solution.py:407
  94.5 0.7 collective-permute-start.13
  95.2 0.9 collective-permute-start.15
  96.1 6.1 %collective-permute-done.12.refs_0_ = f32[288,128]{1,0:T(8,128)S(1)} collective-permute-done((f32[288,128]{1,0:T(8,128)}, f32[288,128]{1,0:T(8,128)S(1)}, u32[]{:S(2)}, u32[]{:S(2)}) %collective-permute-start.12) | collective-permute-done | bytes 147488 | tf_op jit(solution)/shard_map/ppermute | solution.py:407
  102.3 0.6 copy-done.14
  103.1 8.9 %stage_3.1 = (f32[288,128]{1,0:T(8,128)}, f32[288,128]{1,0:T(8,128)}, f32[288,128]{1,0:T(8,128)}, f32[288,128]{1,0:T(8,128)}, f32[1152,128]{1,0:T(8,128)}, /*index=5*/f32[1152,128]{1,0:T(8,128)}, f32[256,128]{1,0:T(8,128)}) custom-call(f32[1152,1152]{1,0:T(8,128)} %bitcast.29, s32[1,1152]{1,0:T(1,128)} %get-tuple-element.55.codes_row, ...), custom_call_target="tpu_custom_call" | custom-call | tf_op jit(solution)/shard_map/stage_3/pallas_call | solution.py:389
  112.0 6.8 %all-to-all-start.3 = ((f32[32,8,128]{2,1,0:T(8,128)}), f32[32,8,128]{2,1,0:T(8,128)S(1)}, u32[]{:S(2)}, u32[]{:S(2)}) async-start(f32[32,8,128]{2,1,0:T(8,128)} %bitcast.40), calls=%async_computation.3 | async-start | bytes 262144 | tf_op jit(solution)/shard_map/all_to_all | solution.py:412
  118.8 1.8 %collective-permute-start.16 = (f32[288,128]{1,0:T(8,128)}, f32[288,128]{1,0:T(8,128)S(1)}, u32[]{:S(2)}, u32[]{:S(2)}) collective-permute-start(f32[288,128]{1,0:T(8,128)} %get-tuple-element.85.refs_4_), channel_id=1, source_target_pairs={{0,4},{4,0},{8,12},{12,8},{16,20},{20,16},{24,28},{28,24},{1,5},{5... | collective-permute-start | bytes 442376 | tf_op jit(solution)/shard_map/ppermute | solution.py:407
  120.7 0.7 collective-permute-start.17
  121.4 0.7 collective-permute-start.19
  122.1 6.4 %collective-permute-done.16.refs_0_ = f32[288,128]{1,0:T(8,128)S(1)} collective-permute-done((f32[288,128]{1,0:T(8,128)}, f32[288,128]{1,0:T(8,128)S(1)}, u32[]{:S(2)}, u32[]{:S(2)}) %collective-permute-start.16) | collective-permute-done | bytes 147488 | tf_op jit(solution)/shard_map/ppermute | solution.py:407
  128.5 0.6 copy-done.16
  129.3 8.8 %stage_4.1 = (f32[288,128]{1,0:T(8,128)}, f32[288,128]{1,0:T(8,128)}, f32[288,128]{1,0:T(8,128)}, f32[288,128]{1,0:T(8,128)}, f32[1152,128]{1,0:T(8,128)}, /*index=5*/f32[1152,128]{1,0:T(8,128)}, f32[256,128]{1,0:T(8,128)}) custom-call(f32[1152,1152]{1,0:T(8,128)} %bitcast.26, s32[1,1152]{1,0:T(1,128)} %get-tuple-element.55.codes_row, ...), custom_call_target="tpu_custom_call" | custom-call | tf_op jit(solution)/shard_map/stage_4/pallas_call | solution.py:389
  138.2 6.8 %all-to-all-start.4 = ((f32[32,8,128]{2,1,0:T(8,128)}), f32[32,8,128]{2,1,0:T(8,128)S(1)}, u32[]{:S(2)}, u32[]{:S(2)}) async-start(f32[32,8,128]{2,1,0:T(8,128)} %bitcast.42), calls=%async_computation.4 | async-start | bytes 262144 | tf_op jit(solution)/shard_map/all_to_all | solution.py:412
  145.0 1.8 %collective-permute-start.20 = (f32[288,128]{1,0:T(8,128)}, f32[288,128]{1,0:T(8,128)S(1)}, u32[]{:S(2)}, u32[]{:S(2)}) collective-permute-start(f32[288,128]{1,0:T(8,128)} %get-tuple-element.92.refs_4_), channel_id=1, source_target_pairs={{0,4},{4,0},{8,12},{12,8},{16,20},{20,16},{24,28},{28,24},{1,5},{5... | collective-permute-start | bytes 442376 | tf_op jit(solution)/shard_map/ppermute | solution.py:407
  146.8 0.7 collective-permute-start.21
  147.6 0.7 collective-permute-start.23
  148.2 6.4 %collective-permute-done.20.refs_0_ = f32[288,128]{1,0:T(8,128)S(1)} collective-permute-done((f32[288,128]{1,0:T(8,128)}, f32[288,128]{1,0:T(8,128)S(1)}, u32[]{:S(2)}, u32[]{:S(2)}) %collective-permute-start.20) | collective-permute-done | bytes 147488 | tf_op jit(solution)/shard_map/ppermute | solution.py:407
  154.7 0.6 copy-done.10
  155.5 5.2 %stage_5.1 = (f32[1152,128]{1,0:T(8,128)}, f32[1152,128]{1,0:T(8,128)}, f32[256,128]{1,0:T(8,128)}) custom-call(s32[1,1152]{1,0:T(1,128)} %get-tuple-element.55.codes_row, s32[1152,128]{1,0:T(8,128)} %get-tuple-element.54.codes_lanes, f32[288,128]{1,0:T(8,128)} %copy-done.10, f32[288,128]{1,0:T(8,128)} %copy-done.11, f32[288,128]{1,0:T(8,128)} %copy-done.12, ...), custom_call_target="tpu_custom_call" | custom-call | tf_op jit(solution)/shard_map/stage_5/pallas_call | solution.py:389
  160.6 7.1 %all-to-all-start.5 = ((f32[32,8,128]{2,1,0:T(8,128)}), f32[32,8,128]{2,1,0:T(8,128)S(1)}, u32[]{:S(2)}, u32[]{:S(2)}) async-start(f32[32,8,128]{2,1,0:T(8,128)} %bitcast.44), calls=%async_computation.5 | async-start | bytes 262144 | tf_op jit(solution)/shard_map/all_to_all | solution.py:412
  167.7 5.1 %slots_to_rows.1 = (f32[1152,128]{1,0:T(8,128)}, f32[1152,128]{1,0:T(8,128)}, f32[1152,128]{1,0:T(8,128)}) custom-call(s32[1152,128]{1,0:T(8,128)} %get-tuple-element.54.codes_lanes, f32[1152,128]{1,0:T(8,128)} %get-tuple-element.100.residual, f32[1152,128]{1,0:T(8,128)} %get-tuple-element.101.multipliers, f32[1152,128]{1,0:T(8,128)} %get-tuple-element.65.refs_5_.refs_19_.modes), custom_call_target="tpu_custom_call" | custom-call | tf_op jit(solution)/shard_map/slots_to_rows/pallas_call | solution.py:389
  172.8 2.8 %all-to-all-done.5 = f32[32,8,128]{2,1,0:T(8,128)S(1)} async-done(((f32[32,8,128]{2,1,0:T(8,128)}), f32[32,8,128]{2,1,0:T(8,128)S(1)}, u32[]{:S(2)}, u32[]{:S(2)}) %all-to-all-start.5) | async-done | bytes 131104 | tf_op jit(solution)/shard_map/all_to_all | solution.py:412
  175.7 0.7 copy-done.9
  176.3 2.7 %residual.1 = f32[1152,128]{1,0:T(8,128)} custom-call(f32[1152,128]{1,0:T(8,128)} %get-tuple-element.103.residual, f32[1152,128]{1,0:T(8,128)} %get-tuple-element.104.modes, f32[256,128]{1,0:T(8,128)} %bitcast.37, f32[160,256]{1,0:T(8,128)} %get-tuple-element.76.refs_18_.inverse_rows), custom_call_target="tpu_custom_call" | custom-call | tf_op jit(solution)/shard_map/residual/pallas_call | solution.py:389
  (84 shorter events, 3.8 us)
Async XLA Ops:
  5.0 22.5 %all-to-all-start = ((f32[32,8,384]{2,1,0:T(8,128)}), f32[32,8,384]{2,1,0:T(8,128)S(1)}, u32[]{:S(2)}, u32[]{:S(2)}) async-start(f32[32,8,384]{2,1,0:T(8,128)} %bitcast.38), calls=%async_computation | async-start | bytes 786432 | tf_op jit(solution)/shard_map/all_to_all | solution.py:412
  12.4 4.5 %collective-permute-start = (f32[8,288]{1,0:T(8,128)}, f32[8,288]{1,0:T(8,128)S(1)}, u32[]{:S(2)}, u32[]{:S(2)}) collective-permute-start(f32[8,288]{1,0:T(8,128)} %get-tuple-element.56.refs_0_), channel_id=1, source_target_pairs={{0,4},{4,0},{8,12},{12,8},{16,20},{20,16},{24,28},{28,24},{1,5},{5... | collective-permute-start | bytes 27656 | tf_op jit(solution)/shard_map/ppermute | solution.py:407
  14.2 2.7 %collective-permute-start.1 = (f32[8,288]{1,0:T(8,128)}, f32[8,288]{1,0:T(8,128)S(1)}, u32[]{:S(2)}, u32[]{:S(2)}) collective-permute-start(f32[8,288]{1,0:T(8,128)} %get-tuple-element.57.refs_1_), channel_id=1, source_target_pairs={{4,8},{8,4},{12,16},{16,12},{20,24},{24,20},{5,9},{9,5},{13,17},{1... | collective-permute-start | bytes 27656 | tf_op jit(solution)/shard_map/ppermute | solution.py:407
  14.8 2.1 %collective-permute-start.2 = (f32[8,288]{1,0:T(8,128)}, f32[8,288]{1,0:T(8,128)S(1)}, u32[]{:S(2)}, u32[]{:S(2)}) collective-permute-start(f32[8,288]{1,0:T(8,128)} %get-tuple-element.58.refs_2_), channel_id=1, source_target_pairs={{0,1},{1,0},{2,3},{3,2},{4,5},{5,4},{6,7},{7,6},{8,9},{9,8},{10,11... | collective-permute-start | bytes 27656 | tf_op jit(solution)/shard_map/ppermute | solution.py:407
  14.9 2.0 %collective-permute-start.3 = (f32[8,288]{1,0:T(8,128)}, f32[8,288]{1,0:T(8,128)S(1)}, u32[]{:S(2)}, u32[]{:S(2)}) collective-permute-start(f32[8,288]{1,0:T(8,128)} %get-tuple-element.59.refs_3_), channel_id=1, source_target_pairs={{1,2},{2,1},{5,6},{6,5},{9,10},{10,9},{13,14},{14,13},{17,18},{18,... | collective-permute-start | bytes 27656 | tf_op jit(solution)/shard_map/ppermute | solution.py:407
  27.6 0.7 copy-start.4
  35.9 9.3 %collective-permute-start.4 = (f32[432,128]{1,0:T(8,128)}, f32[432,128]{1,0:T(8,128)S(1)}, u32[]{:S(2)}, u32[]{:S(2)}) collective-permute-start(f32[432,128]{1,0:T(8,128)} %get-tuple-element.66.refs_4_.refs_8_), channel_id=1, source_target_pairs={{0,4},{4,0},{8,12},{12,8},{16,20},{20,16},{24,28},{28,24},{1,5},{5... | collective-permute-start | bytes 663560 | tf_op jit(solution)/shard_map/ppermute | solution.py:407
  40.4 4.8 %collective-permute-start.5 = (f32[432,128]{1,0:T(8,128)}, f32[432,128]{1,0:T(8,128)S(1)}, u32[]{:S(2)}, u32[]{:S(2)}) collective-permute-start(f32[432,128]{1,0:T(8,128)} %get-tuple-element.67.refs_5_.refs_9_), channel_id=1, source_target_pairs={{4,8},{8,4},{12,16},{16,12},{20,24},{24,20},{5,9},{9,5},{13,17},{1... | collective-permute-start | bytes 663560 | tf_op jit(solution)/shard_map/ppermute | solution.py:407
  41.3 4.6 %collective-permute-start.6 = (f32[432,128]{1,0:T(8,128)}, f32[432,128]{1,0:T(8,128)S(1)}, u32[]{:S(2)}, u32[]{:S(2)}) collective-permute-start(f32[432,128]{1,0:T(8,128)} %get-tuple-element.68.refs_6_.refs_10_), channel_id=1, source_target_pairs={{0,1},{1,0},{2,3},{3,2},{4,5},{5,4},{6,7},{7,6},{8,9},{9,8},{10,11... | collective-permute-start | bytes 663560 | tf_op jit(solution)/shard_map/ppermute | solution.py:407
  44.5 1.3 collective-permute-start.7
  45.2 0.8 copy-start.1
  45.8 0.8 copy-start.3
  53.5 22.9 %all-to-all-start.1 = ((f32[32,8,128]{2,1,0:T(8,128)}), f32[32,8,128]{2,1,0:T(8,128)S(1)}, u32[]{:S(2)}, u32[]{:S(2)}) async-start(f32[32,8,128]{2,1,0:T(8,128)} %bitcast.43), calls=%async_computation.1 | async-start | bytes 262144 | tf_op jit(solution)/shard_map/all_to_all | solution.py:412
  66.7 9.6 %collective-permute-start.8 = (f32[288,128]{1,0:T(8,128)}, f32[288,128]{1,0:T(8,128)S(1)}, u32[]{:S(2)}, u32[]{:S(2)}) collective-permute-start(f32[288,128]{1,0:T(8,128)} %get-tuple-element.71.refs_4_), channel_id=1, source_target_pairs={{0,4},{4,0},{8,12},{12,8},{16,20},{20,16},{24,28},{28,24},{1,5},{5... | collective-permute-start | bytes 442376 | tf_op jit(solution)/shard_map/ppermute | solution.py:407
  68.5 7.8 %collective-permute-start.9 = (f32[288,128]{1,0:T(8,128)}, f32[288,128]{1,0:T(8,128)S(1)}, u32[]{:S(2)}, u32[]{:S(2)}) collective-permute-start(f32[288,128]{1,0:T(8,128)} %get-tuple-element.72.refs_5_), channel_id=1, source_target_pairs={{4,8},{8,4},{12,16},{16,12},{20,24},{24,20},{5,9},{9,5},{13,17},{1... | collective-permute-start | bytes 442376 | tf_op jit(solution)/shard_map/ppermute | solution.py:407
  69.2 7.1 %collective-permute-start.10 = (f32[288,128]{1,0:T(8,128)}, f32[288,128]{1,0:T(8,128)S(1)}, u32[]{:S(2)}, u32[]{:S(2)}) collective-permute-start(f32[288,128]{1,0:T(8,128)} %get-tuple-element.73.refs_6_), channel_id=1, source_target_pairs={{0,1},{1,0},{2,3},{3,2},{4,5},{5,4},{6,7},{7,6},{8,9},{9,8},{10,11... | collective-permute-start | bytes 442376 | tf_op jit(solution)/shard_map/ppermute | solution.py:407
  69.3 7.1 %collective-permute-start.11 = (f32[288,128]{1,0:T(8,128)}, f32[288,128]{1,0:T(8,128)S(1)}, u32[]{:S(2)}, u32[]{:S(2)}) collective-permute-start(f32[288,128]{1,0:T(8,128)} %get-tuple-element.74.refs_7_), channel_id=1, source_target_pairs={{1,2},{2,1},{5,6},{6,5},{9,10},{10,9},{13,14},{14,13},{17,18},{18,... | collective-permute-start | bytes 442376 | tf_op jit(solution)/shard_map/ppermute | solution.py:407
  76.3 0.7 copy-start.18
  76.3 0.7 copy-start.21
  76.3 0.8 copy-start.24
  76.4 0.8 copy-start.6
  85.8 16.5 %all-to-all-start.2 = ((f32[32,8,128]{2,1,0:T(8,128)}), f32[32,8,128]{2,1,0:T(8,128)S(1)}, u32[]{:S(2)}, u32[]{:S(2)}) async-start(f32[32,8,128]{2,1,0:T(8,128)} %bitcast.41), calls=%async_computation.2 | async-start | bytes 262144 | tf_op jit(solution)/shard_map/all_to_all | solution.py:412
  92.7 9.6 %collective-permute-start.12 = (f32[288,128]{1,0:T(8,128)}, f32[288,128]{1,0:T(8,128)S(1)}, u32[]{:S(2)}, u32[]{:S(2)}) collective-permute-start(f32[288,128]{1,0:T(8,128)} %get-tuple-element.78.refs_4_), channel_id=1, source_target_pairs={{0,4},{4,0},{8,12},{12,8},{16,20},{20,16},{24,28},{28,24},{1,5},{5... | collective-permute-start | bytes 442376 | tf_op jit(solution)/shard_map/ppermute | solution.py:407
  94.5 7.8 %collective-permute-start.13 = (f32[288,128]{1,0:T(8,128)}, f32[288,128]{1,0:T(8,128)S(1)}, u32[]{:S(2)}, u32[]{:S(2)}) collective-permute-start(f32[288,128]{1,0:T(8,128)} %get-tuple-element.79.refs_5_), channel_id=1, source_target_pairs={{4,8},{8,4},{12,16},{16,12},{20,24},{24,20},{5,9},{9,5},{13,17},{1... | collective-permute-start | bytes 442376 | tf_op jit(solution)/shard_map/ppermute | solution.py:407
  95.2 7.1 %collective-permute-start.14 = (f32[288,128]{1,0:T(8,128)}, f32[288,128]{1,0:T(8,128)S(1)}, u32[]{:S(2)}, u32[]{:S(2)}) collective-permute-start(f32[288,128]{1,0:T(8,128)} %get-tuple-element.80.refs_6_), channel_id=1, source_target_pairs={{0,1},{1,0},{2,3},{3,2},{4,5},{5,4},{6,7},{7,6},{8,9},{9,8},{10,11... | collective-permute-start | bytes 442376 | tf_op jit(solution)/shard_map/ppermute | solution.py:407
  95.2 7.1 %collective-permute-start.15 = (f32[288,128]{1,0:T(8,128)}, f32[288,128]{1,0:T(8,128)S(1)}, u32[]{:S(2)}, u32[]{:S(2)}) collective-permute-start(f32[288,128]{1,0:T(8,128)} %get-tuple-element.81.refs_7_), channel_id=1, source_target_pairs={{1,2},{2,1},{5,6},{6,5},{9,10},{10,9},{13,14},{14,13},{17,18},{18,... | collective-permute-start | bytes 442376 | tf_op jit(solution)/shard_map/ppermute | solution.py:407
  102.3 0.7 copy-start.17
  102.3 0.7 copy-start.20
  102.3 0.8 copy-start.23
  102.3 0.8 copy-start.5
  112.0 16.5 %all-to-all-start.3 = ((f32[32,8,128]{2,1,0:T(8,128)}), f32[32,8,128]{2,1,0:T(8,128)S(1)}, u32[]{:S(2)}, u32[]{:S(2)}) async-start(f32[32,8,128]{2,1,0:T(8,128)} %bitcast.40), calls=%async_computation.3 | async-start | bytes 262144 | tf_op jit(solution)/shard_map/all_to_all | solution.py:412
  118.8 9.6 %collective-permute-start.16 = (f32[288,128]{1,0:T(8,128)}, f32[288,128]{1,0:T(8,128)S(1)}, u32[]{:S(2)}, u32[]{:S(2)}) collective-permute-start(f32[288,128]{1,0:T(8,128)} %get-tuple-element.85.refs_4_), channel_id=1, source_target_pairs={{0,4},{4,0},{8,12},{12,8},{16,20},{20,16},{24,28},{28,24},{1,5},{5... | collective-permute-start | bytes 442376 | tf_op jit(solution)/shard_map/ppermute | solution.py:407
  120.7 7.8 %collective-permute-start.17 = (f32[288,128]{1,0:T(8,128)}, f32[288,128]{1,0:T(8,128)S(1)}, u32[]{:S(2)}, u32[]{:S(2)}) collective-permute-start(f32[288,128]{1,0:T(8,128)} %get-tuple-element.86.refs_5_), channel_id=1, source_target_pairs={{4,8},{8,4},{12,16},{16,12},{20,24},{24,20},{5,9},{9,5},{13,17},{1... | collective-permute-start | bytes 442376 | tf_op jit(solution)/shard_map/ppermute | solution.py:407
  121.3 7.1 %collective-permute-start.18 = (f32[288,128]{1,0:T(8,128)}, f32[288,128]{1,0:T(8,128)S(1)}, u32[]{:S(2)}, u32[]{:S(2)}) collective-permute-start(f32[288,128]{1,0:T(8,128)} %get-tuple-element.87.refs_6_), channel_id=1, source_target_pairs={{0,1},{1,0},{2,3},{3,2},{4,5},{5,4},{6,7},{7,6},{8,9},{9,8},{10,11... | collective-permute-start | bytes 442376 | tf_op jit(solution)/shard_map/ppermute | solution.py:407
  121.4 7.1 %collective-permute-start.19 = (f32[288,128]{1,0:T(8,128)}, f32[288,128]{1,0:T(8,128)S(1)}, u32[]{:S(2)}, u32[]{:S(2)}) collective-permute-start(f32[288,128]{1,0:T(8,128)} %get-tuple-element.88.refs_7_), channel_id=1, source_target_pairs={{1,2},{2,1},{5,6},{6,5},{9,10},{10,9},{13,14},{14,13},{17,18},{18,... | collective-permute-start | bytes 442376 | tf_op jit(solution)/shard_map/ppermute | solution.py:407
  128.4 0.7 copy-start.19
  128.5 0.7 copy-start.22
  128.5 0.8 copy-start.25
  128.5 0.8 copy-start.7
  138.2 16.5 %all-to-all-start.4 = ((f32[32,8,128]{2,1,0:T(8,128)}), f32[32,8,128]{2,1,0:T(8,128)S(1)}, u32[]{:S(2)}, u32[]{:S(2)}) async-start(f32[32,8,128]{2,1,0:T(8,128)} %bitcast.42), calls=%async_computation.4 | async-start | bytes 262144 | tf_op jit(solution)/shard_map/all_to_all | solution.py:412
  145.0 9.6 %collective-permute-start.20 = (f32[288,128]{1,0:T(8,128)}, f32[288,128]{1,0:T(8,128)S(1)}, u32[]{:S(2)}, u32[]{:S(2)}) collective-permute-start(f32[288,128]{1,0:T(8,128)} %get-tuple-element.92.refs_4_), channel_id=1, source_target_pairs={{0,4},{4,0},{8,12},{12,8},{16,20},{20,16},{24,28},{28,24},{1,5},{5... | collective-permute-start | bytes 442376 | tf_op jit(solution)/shard_map/ppermute | solution.py:407
  146.8 7.8 %collective-permute-start.21 = (f32[288,128]{1,0:T(8,128)}, f32[288,128]{1,0:T(8,128)S(1)}, u32[]{:S(2)}, u32[]{:S(2)}) collective-permute-start(f32[288,128]{1,0:T(8,128)} %get-tuple-element.93.refs_5_), channel_id=1, source_target_pairs={{4,8},{8,4},{12,16},{16,12},{20,24},{24,20},{5,9},{9,5},{13,17},{1... | collective-permute-start | bytes 442376 | tf_op jit(solution)/shard_map/ppermute | solution.py:407
  147.5 7.1 %collective-permute-start.22 = (f32[288,128]{1,0:T(8,128)}, f32[288,128]{1,0:T(8,128)S(1)}, u32[]{:S(2)}, u32[]{:S(2)}) collective-permute-start(f32[288,128]{1,0:T(8,128)} %get-tuple-element.94.refs_6_), channel_id=1, source_target_pairs={{0,1},{1,0},{2,3},{3,2},{4,5},{5,4},{6,7},{7,6},{8,9},{9,8},{10,11... | collective-permute-start | bytes 442376 | tf_op jit(solution)/shard_map/ppermute | solution.py:407
  147.6 7.1 %collective-permute-start.23 = (f32[288,128]{1,0:T(8,128)}, f32[288,128]{1,0:T(8,128)S(1)}, u32[]{:S(2)}, u32[]{:S(2)}) collective-permute-start(f32[288,128]{1,0:T(8,128)} %get-tuple-element.95.refs_7_), channel_id=1, source_target_pairs={{1,2},{2,1},{5,6},{6,5},{9,10},{10,9},{13,14},{14,13},{17,18},{18,... | collective-permute-start | bytes 442376 | tf_op jit(solution)/shard_map/ppermute | solution.py:407
  154.6 0.7 copy-start.12
  154.6 0.8 copy-start.13
  154.6 0.8 copy-start.8
  160.6 15.1 %all-to-all-start.5 = ((f32[32,8,128]{2,1,0:T(8,128)}), f32[32,8,128]{2,1,0:T(8,128)S(1)}, u32[]{:S(2)}, u32[]{:S(2)}) async-start(f32[32,8,128]{2,1,0:T(8,128)} %bitcast.44), calls=%async_computation.5 | async-start | bytes 262144 | tf_op jit(solution)/shard_map/all_to_all | solution.py:412
  (12 other events, 7.8 us)

commit v5 on v4

--- a/solution.py
+++ b/solution.py
@@ -268,7 +268,7 @@
 
 
 def lagged(side, first, mine, theirs, coefficients):
-    left = jnp.concatenate([grouped(mine[...], first), grouped(theirs[...], first)], axis=1)
+    left = jnp.concatenate([grouped(mine, first), grouped(theirs, first)], axis=1)
     near = coefficients[(side + 1) * GROUP : (side + 2) * GROUP]
     return three_pass(left, jnp.concatenate([repeated(coefficients[0:GROUP]), repeated(-near)], axis=0))
 
@@ -276,20 +276,30 @@
 def first_kernel(schur, codes_row, codes_lanes, *refs):
     received, sent, own = refs[0:4], refs[4:8], refs[8]
     outs = refs[9:13]
-    gap_out, parts_out = refs[13:15]
-    slot_pieces, row_pieces, out_pieces = refs[15:18]
-    schur = fetch(schur, refs[18], refs[19])
+    gap_out, parts_out, mine_out, theirs_out = refs[13:17]
+    slot_pieces, row_pieces, out_pieces = refs[17:20]
+    schur = fetch(schur, refs[20], refs[21])
+    half = sent[0].shape[0] - codes_lanes.shape[0] // SIDES
     cap = codes_lanes.shape[0] // SIDES
     for side in range(SIDES):
         block = sent[side][0:cap, :] - received[side][0:cap, :]
         gap_out[side * cap : (side + 1) * cap, :] = block
         fill_pieces(slot_pieces, side * cap, block)
+        mine_out[side * half : (side + 1) * half, :] = sent[side][cap:, :]
+        theirs_out[side * half : (side + 1) * half, :] = received[side][cap:, :]
     copies(parts_out, components_of(own, slot_pieces))
 
     def write(side, block):
         outs[side][...] = block
 
     apply_local(schur, codes_row, codes_lanes, slot_pieces, row_pieces, out_pieces, write)
+
+
+def jump_kernel(*refs):
+    received, sent, out = refs[0:4], refs[4:8], refs[8]
+    cap = out.shape[0] // SIDES
+    for side in range(SIDES):
+        out[side * cap : (side + 1) * cap, :] = sent[side][...] - received[side][...]
 
 
 def stage_kernel(stage, counts, matrix, codes_row, codes_lanes, *refs):
@@ -300,7 +310,7 @@
         del refs[:count]
         return taken
 
-    received, sent, mine, theirs = take(4), take(4), take(4), take(4)
+    jumps, mine, theirs = take(3)
     own, gathered, inverse_rows, modes = take(4)
     states_in = take(counts[0])
     outs = take(4) if stage < 5 else []
@@ -313,12 +323,13 @@
     cap = total // SIDES
     coefficients = exact(inverse_rows[...], gathered[...])
     direct_all = three_pass(modes[...], repeated(coefficients[0:GROUP]))
-    tail = pl.ds(cap, cap // 2)
+    half = mine.shape[0] // SIDES
     for side in range(SIDES):
         rows = slice(side * cap, (side + 1) * cap)
-        jump = sent[side][...] - received[side][...]
+        jump = jumps[rows, :]
+        slab = slice(side * half, (side + 1) * half)
         first = 0 if stage in (2, 4) else 2
-        behind = lagged(side, first, mine[side].at[tail], theirs[side].at[tail], coefficients)
+        behind = lagged(side, first, mine[slab, :], theirs[slab, :], coefficients)
         direct = direct_all[rows, :]
         nextin = None
         if stage == 2:
@@ -377,7 +388,7 @@
     out[...] = residual[...] + three_pass(modes[...], coefficients)
 
 
-def call(kernel, name, outs, inputs, scratch=(), smem=(), left=()):
+def call(kernel, name, outs, inputs, scratch=(), smem=(), left=(), flops=None, room=58):
     spaces = [pltpu.VMEM] * len(inputs)
     for n in smem:
         spaces[n] = pltpu.SMEM
@@ -393,7 +404,10 @@
         in_specs=[pl.BlockSpec(memory_space=space) for space in spaces],
         out_specs=[pl.BlockSpec(memory_space=pltpu.VMEM)] * len(outs),
         scratch_shapes=list(scratch),
-        compiler_params=pltpu.CompilerParams(vmem_limit_bytes=58 * 1024 * 1024),
+        cost_estimate=None
+        if flops is None
+        else pl.CostEstimate(flops=flops, bytes_accessed=0, transcendentals=0),
+        compiler_params=pltpu.CompilerParams(vmem_limit_bytes=room * 1024 * 1024),
     )(*inputs)
 
 
@@ -429,6 +443,7 @@
     scratch = [pieces] * 3
     block = [(cap, cols)] * SIDES
     whole = (total, cols)
+    weight = 128 * total * total * cols
     parts = (wide, cols)
     brought = [pltpu.VMEM((total, total), jnp.float32), pltpu.SemaphoreType.DMA((SIDES,))]
 
@@ -464,21 +479,21 @@
     )
     sent, (start, inverse_rows) = shown[:4], shown[4:]
     received = exchange(sent)
-    slab_sent, slab_received = sent, received
     shown = call(
         first_kernel,
         "stage_1",
-        block + [whole, parts],
+        block + [whole, parts] + [(2 * cap, 4 * GROUP)] * 2,
         [schur, codes_row, codes_lanes, *received, *sent, own_pieces],
         scratch + brought,
         left=(0,),
     )
-    sent, (gap_jump, components) = shown[:4], shown[4:]
+    sent, (gap_jump, components, mine, theirs) = shown[:4], shown[4:]
 
     def stage(number, matrix, states_in, sent, components):
         gathered = everywhere(components)
         received = exchange(sent)
-        inputs = [codes_row, codes_lanes, *received, *sent, *slab_sent, *slab_received]
+        (jumps,) = call(jump_kernel, "jump", [whole], [*received, *sent], flops=weight)
+        inputs = [codes_row, codes_lanes, jumps, mine, theirs]
         inputs += [own_pieces, gathered, inverse_rows, slot_modes, *states_in]
         outs = [whole] * 2 + [parts]
         kernel = functools.partial(stage_kernel, number, (len(states_in), 2))

time: 180 us -> 183 us (1.017)
  waiting for transfers between devices: 30 us -> 22.9 us
  Pallas kernels: 66.2 us -> 73 us
  local copies, waits for them, and re-layouts: 7.37 us -> 12.3 us
    ppermute x24, waiting for transfers between devices: 27.1 us -> 1.95 us  [exchange(): received.append(lax.ppermute(block, axis, pairs))]
    all_to_all x6, waiting for transfers between devices: 2.86 us -> 20.9 us  [everywhere(): lax.all_to_all(stacked, ('sub', 'layer'), split_axis=0, concat_axis=0, ti...]
    all_to_all x6, starting transfers between devices: 48.1 us -> 40.3 us  [everywhere(): lax.all_to_all(stacked, ('sub', 'layer'), split_axis=0, concat_axis=0, ti...]
    pallas_call x10 -> x14, Pallas kernels: 66.2 us -> 73 us  [call(): pl.pallas_call(kernel, name=name, out_shape=shapes, in_specs=[pl.BlockSpe...]
    ppermute x24, starting transfers between devices: 25.6 us -> 31.6 us  [exchange(): received.append(lax.ppermute(block, axis, pairs))]
    unnamed x61, local copies, waits for them, and re-layouts: 7.37 us -> 12.3 us
  transfers between devices with their start and end apart: 30 -> 30, of which waited for: 7 -> 7; matrix products, arithmetic and copies ran while one was open for 0% -> 0% of each run, Pallas kernels for 8% -> 13%
where the time goes in v5:
time: 183 us; the launch traced here: 182 us
  Pallas kernels  73 us (40%)
  starting transfers between devices  71.9 us (39%)
  waiting for transfers between devices  22.9 us (13%)
  local copies, waits for them, and re-layouts  12.3 us (7%)
    pallas_call x14, Pallas kernels, call(): pl.pallas_call(kernel, name=name, out_shape=shapes, in_specs=[pl.BlockSpe...  73 us
    all_to_all x6, starting transfers between devices, everywhere(): lax.all_to_all(stacked, ('sub', 'layer'), split_axis=0, concat_axis=0, ti...  40.3 us
    ppermute x24, starting transfers between devices, exchange(): received.append(lax.ppermute(block, axis, pairs))  31.6 us
    all_to_all x6, waiting for transfers between devices, everywhere(): lax.all_to_all(stacked, ('sub', 'layer'), split_axis=0, concat_axis=0, ti...  20.9 us
    unnamed x61, local copies, waits for them, and re-layouts  12.3 us
  transfers between devices with their start and end apart: 30, of which 7 were waited for; matrix products, arithmetic and copies ran while one was open for 0% of the time, Pallas kernels for 13%

profile of v5, /device:TPU:0, one launch (start us, length us, event | category | flops | bytes accessed | tf_op | source)
XLA Modules:
  0.0 181.9 jit_solution(7097963261921856844)
XLA Ops:
  0.6 1.4 copy.11
  2.6 2.5 %modes_to_slots.1 = (f32[8,288]{1,0:T(8,128)}, f32[8,288]{1,0:T(8,128)}, f32[8,288]{1,0:T(8,128)}, f32[8,288]{1,0:T(8,128)}, f32[256,384]{1,0:T(8,128)}, /*index...) custom-call(s32[1,1152]{1,0:T(1,128)} %bitcast.45, f32[6,1152]{1,0:T(8,128)} %bitcast.39, f32[6,192]{1,0:T(8,128)} %inverse.1, ...), custom_call_target="tpu_custom_call" | custom-call | tf_op jit(solution)/shard_map/modes_to_slots/pallas_call | solution.py:400
  5.1 7.3 %all-to-all-start = ((f32[32,8,384]{2,1,0:T(8,128)}), f32[32,8,384]{2,1,0:T(8,128)S(1)}, u32[]{:S(2)}, u32[]{:S(2)}) async-start(f32[32,8,384]{2,1,0:T(8,128)} %bitcast.38), calls=%async_computation | async-start | bytes 786432 | tf_op jit(solution)/shard_map/all_to_all | solution.py:426
  12.4 1.8 %collective-permute-start = (f32[8,288]{1,0:T(8,128)}, f32[8,288]{1,0:T(8,128)S(1)}, u32[]{:S(2)}, u32[]{:S(2)}) collective-permute-start(f32[8,288]{1,0:T(8,128)} %get-tuple-element.58.refs_0_), channel_id=1, source_target_pairs={{0,4},{4,0},{8,12},{12,8},{16,20},{20,16},{24,28},{28,24},{1,5},{5... | collective-permute-start | bytes 27656 | tf_op jit(solution)/shard_map/ppermute | solution.py:421
  14.9 0.7 collective-permute-start.3
  15.6 1.3 collective-permute-done.refs_4_
  17.5 10.0 %operators_on_modes.1 = (f32[144,128]{1,0:T(8,128)}, f32[144,128]{1,0:T(8,128)}, f32[144,128]{1,0:T(8,128)}, f32[144,128]{1,0:T(8,128)}, f32[1152,128]{1,0:T(8,128)}) custom-call(f32[1152,1152]{1,0:T(8,128)} %bitcast.23, f32[1152,1152]{1,0:T(8,128)} %bitcast.27, s32[1,1152]{1,0:T(1,128)} %get-tuple-element.57.codes_row, ...), custom_call_target="tpu_custom_call" | custom-call | tf_op jit(solution)/shard_map/operators_on_modes/pallas_call | solution.py:400
  27.6 0.7 copy-done
  28.3 7.6 %start.1 = (f32[432,128]{1,0:T(8,128)}, f32[432,128]{1,0:T(8,128)}, f32[432,128]{1,0:T(8,128)}, f32[432,128]{1,0:T(8,128)}, f32[1152,128]{1,0:T(8,128)}, /*index=5*/f32[160,256]{1,0:T(8,128)}) custom-call(f32[1152,1152]{1,0:T(8,128)} %bitcast.24, f32[1152,128]{1,0:T(8,128)} %bitcast.32, s32[1,1152]{1,0:T(1,128)} %get-tuple-element.57.codes_row, ...), custom_call_target="tpu_custom_call" | custom-call | tf_op jit(solution)/shard_map/start/pallas_call | solution.py:400
  35.9 4.5 %collective-permute-start.4 = (f32[432,128]{1,0:T(8,128)}, f32[432,128]{1,0:T(8,128)S(1)}, u32[]{:S(2)}, u32[]{:S(2)}) collective-permute-start(f32[432,128]{1,0:T(8,128)} %get-tuple-element.68.refs_4_), channel_id=1, source_target_pairs={{0,4},{4,0},{8,12},{12,8},{16,20},{20,16},{24,28},{28,24},{1,5},{5... | collective-permute-start | bytes 663560 | tf_op jit(solution)/shard_map/ppermute | solution.py:421
  40.4 0.8 collective-permute-start.5
  41.3 3.3 %collective-permute-start.6 = (f32[432,128]{1,0:T(8,128)}, f32[432,128]{1,0:T(8,128)S(1)}, u32[]{:S(2)}, u32[]{:S(2)}) collective-permute-start(f32[432,128]{1,0:T(8,128)} %get-tuple-element.70.refs_6_), channel_id=1, source_target_pairs={{0,1},{1,0},{2,3},{3,2},{4,5},{5,4},{6,7},{7,6},{8,9},{9,8},{10,11... | collective-permute-start | bytes 663560 | tf_op jit(solution)/shard_map/ppermute | solution.py:421
  44.5 0.7 collective-permute-start.7
  46.6 6.9 %stage_1.1 = (f32[288,128]{1,0:T(8,128)}, f32[288,128]{1,0:T(8,128)}, f32[288,128]{1,0:T(8,128)}, f32[288,128]{1,0:T(8,128)}, f32[1152,128]{1,0:T(8,128)}, /*ind...) custom-call(f32[1152,1152]{1,0:T(8,128)} %bitcast.28, s32[1,1152]{1,0:T(1,128)} %get-tuple-element.57.codes_row, ...), custom_call_target="tpu_custom_call" | custom-call | tf_op jit(solution)/shard_map/stage_1/pallas_call | solution.py:400
  53.6 8.8 %collective-permute-start.8 = (f32[288,128]{1,0:T(8,128)}, f32[288,128]{1,0:T(8,128)S(1)}, u32[]{:S(2)}, u32[]{:S(2)}) collective-permute-start(f32[288,128]{1,0:T(8,128)} %get-tuple-element.73.refs_4_), channel_id=1, source_target_pairs={{0,4},{4,0},{8,12},{12,8},{16,20},{20,16},{24,28},{28,24},{1,5},{5... | collective-permute-start | bytes 442376 | tf_op jit(solution)/shard_map/ppermute | solution.py:421
  62.4 0.7 collective-permute-start.9
  63.0 2.6 %collective-permute-start.10 = (f32[288,128]{1,0:T(8,128)}, f32[288,128]{1,0:T(8,128)S(1)}, u32[]{:S(2)}, u32[]{:S(2)}) collective-permute-start(f32[288,128]{1,0:T(8,128)} %get-tuple-element.75.refs_6_), channel_id=1, source_target_pairs={{0,1},{1,0},{2,3},{3,2},{4,5},{5,4},{6,7},{7,6},{8,9},{9,8},{10,11... | collective-permute-start | bytes 442376 | tf_op jit(solution)/shard_map/ppermute | solution.py:421
  65.6 0.7 collective-permute-start.11
  66.3 7.7 %all-to-all-start.1 = ((f32[32,8,128]{2,1,0:T(8,128)}), f32[32,8,128]{2,1,0:T(8,128)S(1)}, u32[]{:S(2)}, u32[]{:S(2)}) async-start(f32[32,8,128]{2,1,0:T(8,128)} %bitcast.40), calls=%async_computation.1 | async-start | bytes 262144 | tf_op jit(solution)/shard_map/all_to_all | solution.py:426
  74.8 0.7 copy-done.26
  75.5 2.2 %jump.4.refs_0_ = f32[1152,128]{1,0:T(8,128)} custom-call(f32[288,128]{1,0:T(8,128)} %copy-done.14, f32[288,128]{1,0:T(8,128)} %copy-done.18, f32[288,128]{1,0:T(8,128)} %copy-done.22, f32[288,128]{1,0:T(8,128)} %copy-done.26, f32[288,128]{1,0:T(8,128)} %get-tuple-element.73.refs_4_, f32[288,128]{1,0:T(8,128)} %get-tuple-element.74.refs_5_, ...), custom_call_target="tpu_custom_call" | custom-call | flops 21743271936 | tf_op jit(solution)/shard_map/jump/pallas_call | solution.py:400
  77.7 4.6 %all-to-all-done.1 = f32[32,8,128]{2,1,0:T(8,128)S(1)} async-done(((f32[32,8,128]{2,1,0:T(8,128)}), f32[32,8,128]{2,1,0:T(8,128)S(1)}, u32[]{:S(2)}, u32[]{:S(2)}) %all-to-all-start.1) | async-done | bytes 131104 | tf_op jit(solution)/shard_map/all_to_all | solution.py:426
  82.9 8.1 %stage_2.1 = (f32[288,128]{1,0:T(8,128)}, f32[288,128]{1,0:T(8,128)}, f32[288,128]{1,0:T(8,128)}, f32[288,128]{1,0:T(8,128)}, f32[1152,128]{1,0:T(8,128)}, /*index=5*/f32[1152,128]{1,0:T(8,128)}, f32[256,128]{1,0:T(8,128)}) custom-call(f32[1152,1152]{1,0:T(8,128)} %bitcast.25, s32[1,1152]{1,0:T(1,128)} %get-tuple-element.57.codes_row, ...), custom_call_target="tpu_custom_call" | custom-call | tf_op jit(solution)/shard_map/stage_2/pallas_call | solution.py:400
  91.0 0.7 collective-permute-start.12
  91.7 0.7 collective-permute-start.13
  92.5 0.7 collective-permute-start.15
  93.2 7.6 %all-to-all-start.2 = ((f32[32,8,128]{2,1,0:T(8,128)}), f32[32,8,128]{2,1,0:T(8,128)S(1)}, u32[]{:S(2)}, u32[]{:S(2)}) async-start(f32[32,8,128]{2,1,0:T(8,128)} %bitcast.42), calls=%async_computation.2 | async-start | bytes 262144 | tf_op jit(solution)/shard_map/all_to_all | solution.py:426
  102.2 2.2 %jump.5.refs_0_ = f32[1152,128]{1,0:T(8,128)} custom-call(f32[288,128]{1,0:T(8,128)} %copy-done.15, f32[288,128]{1,0:T(8,128)} %copy-done.19, f32[288,128]{1,0:T(8,128)} %copy-done.23, f32[288,128]{1,0:T(8,128)} %copy-done.27, f32[288,128]{1,0:T(8,128)} %get-tuple-element.82.refs_4_, f32[288,128]{1,0:T(8,128)} %get-tuple-element.83.refs_5_, ...), custom_call_target="tpu_custom_call" | custom-call | flops 21743271936 | tf_op jit(solution)/shard_map/jump/pallas_call | solution.py:400
  104.4 4.4 %all-to-all-done.2 = f32[32,8,128]{2,1,0:T(8,128)S(1)} async-done(((f32[32,8,128]{2,1,0:T(8,128)}), f32[32,8,128]{2,1,0:T(8,128)S(1)}, u32[]{:S(2)}, u32[]{:S(2)}) %all-to-all-start.2) | async-done | bytes 131104 | tf_op jit(solution)/shard_map/all_to_all | solution.py:426
  109.5 8.3 %stage_3.1 = (f32[288,128]{1,0:T(8,128)}, f32[288,128]{1,0:T(8,128)}, f32[288,128]{1,0:T(8,128)}, f32[288,128]{1,0:T(8,128)}, f32[1152,128]{1,0:T(8,128)}, /*index=5*/f32[1152,128]{1,0:T(8,128)}, f32[256,128]{1,0:T(8,128)}) custom-call(f32[1152,1152]{1,0:T(8,128)} %bitcast.29, s32[1,1152]{1,0:T(1,128)} %get-tuple-element.57.codes_row, ...), custom_call_target="tpu_custom_call" | custom-call | tf_op jit(solution)/shard_map/stage_3/pallas_call | solution.py:400
  117.8 0.7 collective-permute-start.16
  119.3 0.7 collective-permute-start.19
  119.9 7.4 %all-to-all-start.3 = ((f32[32,8,128]{2,1,0:T(8,128)}), f32[32,8,128]{2,1,0:T(8,128)S(1)}, u32[]{:S(2)}, u32[]{:S(2)}) async-start(f32[32,8,128]{2,1,0:T(8,128)} %bitcast.41), calls=%async_computation.3 | async-start | bytes 262144 | tf_op jit(solution)/shard_map/all_to_all | solution.py:426
  128.2 0.7 copy-done.28
  128.8 2.2 %jump.6.refs_0_ = f32[1152,128]{1,0:T(8,128)} custom-call(f32[288,128]{1,0:T(8,128)} %copy-done.16, f32[288,128]{1,0:T(8,128)} %copy-done.20, f32[288,128]{1,0:T(8,128)} %copy-done.24, f32[288,128]{1,0:T(8,128)} %copy-done.28, f32[288,128]{1,0:T(8,128)} %get-tuple-element.89.refs_4_, f32[288,128]{1,0:T(8,128)} %get-tuple-element.90.refs_5_, ...), custom_call_target="tpu_custom_call" | custom-call | flops 21743271936 | tf_op jit(solution)/shard_map/jump/pallas_call | solution.py:400
  131.0 4.6 %all-to-all-done.3 = f32[32,8,128]{2,1,0:T(8,128)S(1)} async-done(((f32[32,8,128]{2,1,0:T(8,128)}), f32[32,8,128]{2,1,0:T(8,128)S(1)}, u32[]{:S(2)}, u32[]{:S(2)}) %all-to-all-start.3) | async-done | bytes 131104 | tf_op jit(solution)/shard_map/all_to_all | solution.py:426
  136.3 8.3 %stage_4.1 = (f32[288,128]{1,0:T(8,128)}, f32[288,128]{1,0:T(8,128)}, f32[288,128]{1,0:T(8,128)}, f32[288,128]{1,0:T(8,128)}, f32[1152,128]{1,0:T(8,128)}, /*index=5*/f32[1152,128]{1,0:T(8,128)}, f32[256,128]{1,0:T(8,128)}) custom-call(f32[1152,1152]{1,0:T(8,128)} %bitcast.26, s32[1,1152]{1,0:T(1,128)} %get-tuple-element.57.codes_row, ...), custom_call_target="tpu_custom_call" | custom-call | tf_op jit(solution)/shard_map/stage_4/pallas_call | solution.py:400
  144.6 0.7 collective-permute-start.20
  146.1 0.7 collective-permute-start.23
  146.8 7.4 %all-to-all-start.4 = ((f32[32,8,128]{2,1,0:T(8,128)}), f32[32,8,128]{2,1,0:T(8,128)S(1)}, u32[]{:S(2)}, u32[]{:S(2)}) async-start(f32[32,8,128]{2,1,0:T(8,128)} %bitcast.43), calls=%async_computation.4 | async-start | bytes 262144 | tf_op jit(solution)/shard_map/all_to_all | solution.py:426
  155.0 0.7 copy-done.29
  155.6 2.2 %jump.7.refs_0_ = f32[1152,128]{1,0:T(8,128)} custom-call(f32[288,128]{1,0:T(8,128)} %copy-done.17, f32[288,128]{1,0:T(8,128)} %copy-done.21, f32[288,128]{1,0:T(8,128)} %copy-done.25, f32[288,128]{1,0:T(8,128)} %copy-done.29, f32[288,128]{1,0:T(8,128)} %get-tuple-element.96.refs_4_, f32[288,128]{1,0:T(8,128)} %get-tuple-element.97.refs_5_, ...), custom_call_target="tpu_custom_call" | custom-call | flops 21743271936 | tf_op jit(solution)/shard_map/jump/pallas_call | solution.py:400
  157.8 4.6 %all-to-all-done.4 = f32[32,8,128]{2,1,0:T(8,128)S(1)} async-done(((f32[32,8,128]{2,1,0:T(8,128)}), f32[32,8,128]{2,1,0:T(8,128)S(1)}, u32[]{:S(2)}, u32[]{:S(2)}) %all-to-all-start.4) | async-done | bytes 131104 | tf_op jit(solution)/shard_map/all_to_all | solution.py:426
  163.1 4.6 %stage_5.1 = (f32[1152,128]{1,0:T(8,128)}, f32[1152,128]{1,0:T(8,128)}, f32[256,128]{1,0:T(8,128)}) custom-call(s32[1,1152]{1,0:T(1,128)} %get-tuple-element.57.codes_row, s32[1152,128]{1,0:T(8,128)} %get-tuple-element.56.codes_lanes, f32[1152,128]{1,0:T(8,128)} %jump.7.refs_0_, f32[576,128]{1,0:T(8,128)} %get-tuple-element.77.refs_1_, ...), custom_call_target="tpu_custom_call" | custom-call | tf_op jit(solution)/shard_map/stage_5/pallas_call | solution.py:400
  167.7 2.8 %all-to-all-start.5 = ((f32[32,8,128]{2,1,0:T(8,128)}), f32[32,8,128]{2,1,0:T(8,128)S(1)}, u32[]{:S(2)}, u32[]{:S(2)}) async-start(f32[32,8,128]{2,1,0:T(8,128)} %bitcast.44), calls=%async_computation.5 | async-start | bytes 262144 | tf_op jit(solution)/shard_map/all_to_all | solution.py:426
  170.6 5.1 %slots_to_rows.1 = (f32[1152,128]{1,0:T(8,128)}, f32[1152,128]{1,0:T(8,128)}, f32[1152,128]{1,0:T(8,128)}) custom-call(s32[1152,128]{1,0:T(8,128)} %get-tuple-element.56.codes_lanes, f32[1152,128]{1,0:T(8,128)} %get-tuple-element.104.residual, f32[1152,128]{1,0:T(8,128)} %get-tuple-element.105.multipliers, f32[1152,128]{1,0:T(8,128)} %get-tuple-element.67.refs_5_.refs_6_.modes), custom_call_target="tpu_custom_call" | custom-call | tf_op jit(solution)/shard_map/slots_to_rows/pallas_call | solution.py:400
  175.7 2.8 %all-to-all-done.5 = f32[32,8,128]{2,1,0:T(8,128)S(1)} async-done(((f32[32,8,128]{2,1,0:T(8,128)}), f32[32,8,128]{2,1,0:T(8,128)S(1)}, u32[]{:S(2)}, u32[]{:S(2)}) %all-to-all-start.5) | async-done | bytes 131104 | tf_op jit(solution)/shard_map/all_to_all | solution.py:426
  179.2 2.7 %residual.1 = f32[1152,128]{1,0:T(8,128)} custom-call(f32[1152,128]{1,0:T(8,128)} %get-tuple-element.107.residual, f32[1152,128]{1,0:T(8,128)} %get-tuple-element.108.modes, f32[256,128]{1,0:T(8,128)} %bitcast.37, f32[160,256]{1,0:T(8,128)} %get-tuple-element.80.refs_5_.inverse_rows), custom_call_target="tpu_custom_call" | custom-call | tf_op jit(solution)/shard_map/residual/pallas_call | solution.py:400
  (88 shorter events, 11.7 us)
Async XLA Ops:
  5.1 22.5 %all-to-all-start = ((f32[32,8,384]{2,1,0:T(8,128)}), f32[32,8,384]{2,1,0:T(8,128)S(1)}, u32[]{:S(2)}, u32[]{:S(2)}) async-start(f32[32,8,384]{2,1,0:T(8,128)} %bitcast.38), calls=%async_computation | async-start | bytes 786432 | tf_op jit(solution)/shard_map/all_to_all | solution.py:426
  12.4 4.5 %collective-permute-start = (f32[8,288]{1,0:T(8,128)}, f32[8,288]{1,0:T(8,128)S(1)}, u32[]{:S(2)}, u32[]{:S(2)}) collective-permute-start(f32[8,288]{1,0:T(8,128)} %get-tuple-element.58.refs_0_), channel_id=1, source_target_pairs={{0,4},{4,0},{8,12},{12,8},{16,20},{20,16},{24,28},{28,24},{1,5},{5... | collective-permute-start | bytes 27656 | tf_op jit(solution)/shard_map/ppermute | solution.py:421
  14.2 2.7 %collective-permute-start.1 = (f32[8,288]{1,0:T(8,128)}, f32[8,288]{1,0:T(8,128)S(1)}, u32[]{:S(2)}, u32[]{:S(2)}) collective-permute-start(f32[8,288]{1,0:T(8,128)} %get-tuple-element.59.refs_1_), channel_id=1, source_target_pairs={{4,8},{8,4},{12,16},{16,12},{20,24},{24,20},{5,9},{9,5},{13,17},{1... | collective-permute-start | bytes 27656 | tf_op jit(solution)/shard_map/ppermute | solution.py:421
  14.9 2.1 %collective-permute-start.2 = (f32[8,288]{1,0:T(8,128)}, f32[8,288]{1,0:T(8,128)S(1)}, u32[]{:S(2)}, u32[]{:S(2)}) collective-permute-start(f32[8,288]{1,0:T(8,128)} %get-tuple-element.60.refs_2_), channel_id=1, source_target_pairs={{0,1},{1,0},{2,3},{3,2},{4,5},{5,4},{6,7},{7,6},{8,9},{9,8},{10,11... | collective-permute-start | bytes 27656 | tf_op jit(solution)/shard_map/ppermute | solution.py:421
  14.9 2.0 %collective-permute-start.3 = (f32[8,288]{1,0:T(8,128)}, f32[8,288]{1,0:T(8,128)S(1)}, u32[]{:S(2)}, u32[]{:S(2)}) collective-permute-start(f32[8,288]{1,0:T(8,128)} %get-tuple-element.61.refs_3_), channel_id=1, source_target_pairs={{1,2},{2,1},{5,6},{6,5},{9,10},{10,9},{13,14},{14,13},{17,18},{18,... | collective-permute-start | bytes 27656 | tf_op jit(solution)/shard_map/ppermute | solution.py:421
  27.6 0.7 copy-start
  35.9 9.3 %collective-permute-start.4 = (f32[432,128]{1,0:T(8,128)}, f32[432,128]{1,0:T(8,128)S(1)}, u32[]{:S(2)}, u32[]{:S(2)}) collective-permute-start(f32[432,128]{1,0:T(8,128)} %get-tuple-element.68.refs_4_), channel_id=1, source_target_pairs={{0,4},{4,0},{8,12},{12,8},{16,20},{20,16},{24,28},{28,24},{1,5},{5... | collective-permute-start | bytes 663560 | tf_op jit(solution)/shard_map/ppermute | solution.py:421
  40.4 4.8 %collective-permute-start.5 = (f32[432,128]{1,0:T(8,128)}, f32[432,128]{1,0:T(8,128)S(1)}, u32[]{:S(2)}, u32[]{:S(2)}) collective-permute-start(f32[432,128]{1,0:T(8,128)} %get-tuple-element.69.refs_5_), channel_id=1, source_target_pairs={{4,8},{8,4},{12,16},{16,12},{20,24},{24,20},{5,9},{9,5},{13,17},{1... | collective-permute-start | bytes 663560 | tf_op jit(solution)/shard_map/ppermute | solution.py:421
  41.3 4.6 %collective-permute-start.6 = (f32[432,128]{1,0:T(8,128)}, f32[432,128]{1,0:T(8,128)S(1)}, u32[]{:S(2)}, u32[]{:S(2)}) collective-permute-start(f32[432,128]{1,0:T(8,128)} %get-tuple-element.70.refs_6_), channel_id=1, source_target_pairs={{0,1},{1,0},{2,3},{3,2},{4,5},{5,4},{6,7},{7,6},{8,9},{9,8},{10,11... | collective-permute-start | bytes 663560 | tf_op jit(solution)/shard_map/ppermute | solution.py:421
  44.5 1.3 collective-permute-start.7
  45.2 0.7 copy-start.6
  45.2 0.8 copy-start.7
  45.8 0.7 copy-start.8
  45.8 0.8 copy-start.9
  53.6 20.4 %collective-permute-start.8 = (f32[288,128]{1,0:T(8,128)}, f32[288,128]{1,0:T(8,128)S(1)}, u32[]{:S(2)}, u32[]{:S(2)}) collective-permute-start(f32[288,128]{1,0:T(8,128)} %get-tuple-element.73.refs_4_), channel_id=1, source_target_pairs={{0,4},{4,0},{8,12},{12,8},{16,20},{20,16},{24,28},{28,24},{1,5},{5... | collective-permute-start | bytes 442376 | tf_op jit(solution)/shard_map/ppermute | solution.py:421
  62.4 11.7 %collective-permute-start.9 = (f32[288,128]{1,0:T(8,128)}, f32[288,128]{1,0:T(8,128)S(1)}, u32[]{:S(2)}, u32[]{:S(2)}) collective-permute-start(f32[288,128]{1,0:T(8,128)} %get-tuple-element.74.refs_5_), channel_id=1, source_target_pairs={{4,8},{8,4},{12,16},{16,12},{20,24},{24,20},{5,9},{9,5},{13,17},{1... | collective-permute-start | bytes 442376 | tf_op jit(solution)/shard_map/ppermute | solution.py:421
  63.0 11.0 %collective-permute-start.10 = (f32[288,128]{1,0:T(8,128)}, f32[288,128]{1,0:T(8,128)S(1)}, u32[]{:S(2)}, u32[]{:S(2)}) collective-permute-start(f32[288,128]{1,0:T(8,128)} %get-tuple-element.75.refs_6_), channel_id=1, source_target_pairs={{0,1},{1,0},{2,3},{3,2},{4,5},{5,4},{6,7},{7,6},{8,9},{9,8},{10,11... | collective-permute-start | bytes 442376 | tf_op jit(solution)/shard_map/ppermute | solution.py:421
  65.6 8.4 %collective-permute-start.11 = (f32[288,128]{1,0:T(8,128)}, f32[288,128]{1,0:T(8,128)S(1)}, u32[]{:S(2)}, u32[]{:S(2)}) collective-permute-start(f32[288,128]{1,0:T(8,128)} %get-tuple-element.76.refs_7_), channel_id=1, source_target_pairs={{1,2},{2,1},{5,6},{6,5},{9,10},{10,9},{13,14},{14,13},{17,18},{18,... | collective-permute-start | bytes 442376 | tf_op jit(solution)/shard_map/ppermute | solution.py:421
  66.3 15.9 %all-to-all-start.1 = ((f32[32,8,128]{2,1,0:T(8,128)}), f32[32,8,128]{2,1,0:T(8,128)S(1)}, u32[]{:S(2)}, u32[]{:S(2)}) async-start(f32[32,8,128]{2,1,0:T(8,128)} %bitcast.40), calls=%async_computation.1 | async-start | bytes 262144 | tf_op jit(solution)/shard_map/all_to_all | solution.py:426
  74.0 0.7 copy-start.18
  74.0 0.7 copy-start.22
  74.8 0.7 copy-start.26
  91.0 9.8 %collective-permute-start.12 = (f32[288,128]{1,0:T(8,128)}, f32[288,128]{1,0:T(8,128)S(1)}, u32[]{:S(2)}, u32[]{:S(2)}) collective-permute-start(f32[288,128]{1,0:T(8,128)} %get-tuple-element.82.refs_4_), channel_id=1, source_target_pairs={{0,4},{4,0},{8,12},{12,8},{16,20},{20,16},{24,28},{28,24},{1,5},{5... | collective-permute-start | bytes 442376 | tf_op jit(solution)/shard_map/ppermute | solution.py:421
  91.7 9.1 %collective-permute-start.13 = (f32[288,128]{1,0:T(8,128)}, f32[288,128]{1,0:T(8,128)S(1)}, u32[]{:S(2)}, u32[]{:S(2)}) collective-permute-start(f32[288,128]{1,0:T(8,128)} %get-tuple-element.83.refs_5_), channel_id=1, source_target_pairs={{4,8},{8,4},{12,16},{16,12},{20,24},{24,20},{5,9},{9,5},{13,17},{1... | collective-permute-start | bytes 442376 | tf_op jit(solution)/shard_map/ppermute | solution.py:421
  92.4 8.5 %collective-permute-start.14 = (f32[288,128]{1,0:T(8,128)}, f32[288,128]{1,0:T(8,128)S(1)}, u32[]{:S(2)}, u32[]{:S(2)}) collective-permute-start(f32[288,128]{1,0:T(8,128)} %get-tuple-element.84.refs_6_), channel_id=1, source_target_pairs={{0,1},{1,0},{2,3},{3,2},{4,5},{5,4},{6,7},{7,6},{8,9},{9,8},{10,11... | collective-permute-start | bytes 442376 | tf_op jit(solution)/shard_map/ppermute | solution.py:421
  92.5 8.4 %collective-permute-start.15 = (f32[288,128]{1,0:T(8,128)}, f32[288,128]{1,0:T(8,128)S(1)}, u32[]{:S(2)}, u32[]{:S(2)}) collective-permute-start(f32[288,128]{1,0:T(8,128)} %get-tuple-element.85.refs_7_), channel_id=1, source_target_pairs={{1,2},{2,1},{5,6},{6,5},{9,10},{10,9},{13,14},{14,13},{17,18},{18,... | collective-permute-start | bytes 442376 | tf_op jit(solution)/shard_map/ppermute | solution.py:421
  93.2 15.7 %all-to-all-start.2 = ((f32[32,8,128]{2,1,0:T(8,128)}), f32[32,8,128]{2,1,0:T(8,128)S(1)}, u32[]{:S(2)}, u32[]{:S(2)}) async-start(f32[32,8,128]{2,1,0:T(8,128)} %bitcast.42), calls=%async_computation.2 | async-start | bytes 262144 | tf_op jit(solution)/shard_map/all_to_all | solution.py:426
  100.8 0.7 copy-start.19
  100.9 0.7 copy-start.23
  117.8 9.6 %collective-permute-start.16 = (f32[288,128]{1,0:T(8,128)}, f32[288,128]{1,0:T(8,128)S(1)}, u32[]{:S(2)}, u32[]{:S(2)}) collective-permute-start(f32[288,128]{1,0:T(8,128)} %get-tuple-element.89.refs_4_), channel_id=1, source_target_pairs={{0,4},{4,0},{8,12},{12,8},{16,20},{20,16},{24,28},{28,24},{1,5},{5... | collective-permute-start | bytes 442376 | tf_op jit(solution)/shard_map/ppermute | solution.py:421
  118.5 8.9 %collective-permute-start.17 = (f32[288,128]{1,0:T(8,128)}, f32[288,128]{1,0:T(8,128)S(1)}, u32[]{:S(2)}, u32[]{:S(2)}) collective-permute-start(f32[288,128]{1,0:T(8,128)} %get-tuple-element.90.refs_5_), channel_id=1, source_target_pairs={{4,8},{8,4},{12,16},{16,12},{20,24},{24,20},{5,9},{9,5},{13,17},{1... | collective-permute-start | bytes 442376 | tf_op jit(solution)/shard_map/ppermute | solution.py:421
  119.2 8.2 %collective-permute-start.18 = (f32[288,128]{1,0:T(8,128)}, f32[288,128]{1,0:T(8,128)S(1)}, u32[]{:S(2)}, u32[]{:S(2)}) collective-permute-start(f32[288,128]{1,0:T(8,128)} %get-tuple-element.91.refs_6_), channel_id=1, source_target_pairs={{0,1},{1,0},{2,3},{3,2},{4,5},{5,4},{6,7},{7,6},{8,9},{9,8},{10,11... | collective-permute-start | bytes 442376 | tf_op jit(solution)/shard_map/ppermute | solution.py:421
  119.3 8.2 %collective-permute-start.19 = (f32[288,128]{1,0:T(8,128)}, f32[288,128]{1,0:T(8,128)S(1)}, u32[]{:S(2)}, u32[]{:S(2)}) collective-permute-start(f32[288,128]{1,0:T(8,128)} %get-tuple-element.92.refs_7_), channel_id=1, source_target_pairs={{1,2},{2,1},{5,6},{6,5},{9,10},{10,9},{13,14},{14,13},{17,18},{18,... | collective-permute-start | bytes 442376 | tf_op jit(solution)/shard_map/ppermute | solution.py:421
  119.9 15.7 %all-to-all-start.3 = ((f32[32,8,128]{2,1,0:T(8,128)}), f32[32,8,128]{2,1,0:T(8,128)S(1)}, u32[]{:S(2)}, u32[]{:S(2)}) async-start(f32[32,8,128]{2,1,0:T(8,128)} %bitcast.41), calls=%async_computation.3 | async-start | bytes 262144 | tf_op jit(solution)/shard_map/all_to_all | solution.py:426
  127.4 0.7 copy-start.16
  127.4 0.7 copy-start.20
  127.4 0.7 copy-start.24
  128.2 0.7 copy-start.28
  144.6 9.6 %collective-permute-start.20 = (f32[288,128]{1,0:T(8,128)}, f32[288,128]{1,0:T(8,128)S(1)}, u32[]{:S(2)}, u32[]{:S(2)}) collective-permute-start(f32[288,128]{1,0:T(8,128)} %get-tuple-element.96.refs_4_), channel_id=1, source_target_pairs={{0,4},{4,0},{8,12},{12,8},{16,20},{20,16},{24,28},{28,24},{1,5},{5... | collective-permute-start | bytes 442376 | tf_op jit(solution)/shard_map/ppermute | solution.py:421
  145.3 8.9 %collective-permute-start.21 = (f32[288,128]{1,0:T(8,128)}, f32[288,128]{1,0:T(8,128)S(1)}, u32[]{:S(2)}, u32[]{:S(2)}) collective-permute-start(f32[288,128]{1,0:T(8,128)} %get-tuple-element.97.refs_5_), channel_id=1, source_target_pairs={{4,8},{8,4},{12,16},{16,12},{20,24},{24,20},{5,9},{9,5},{13,17},{1... | collective-permute-start | bytes 442376 | tf_op jit(solution)/shard_map/ppermute | solution.py:421
  146.0 8.2 %collective-permute-start.22 = (f32[288,128]{1,0:T(8,128)}, f32[288,128]{1,0:T(8,128)S(1)}, u32[]{:S(2)}, u32[]{:S(2)}) collective-permute-start(f32[288,128]{1,0:T(8,128)} %get-tuple-element.98.refs_6_), channel_id=1, source_target_pairs={{0,1},{1,0},{2,3},{3,2},{4,5},{5,4},{6,7},{7,6},{8,9},{9,8},{10,11... | collective-permute-start | bytes 442376 | tf_op jit(solution)/shard_map/ppermute | solution.py:421
  146.1 8.2 %collective-permute-start.23 = (f32[288,128]{1,0:T(8,128)}, f32[288,128]{1,0:T(8,128)S(1)}, u32[]{:S(2)}, u32[]{:S(2)}) collective-permute-start(f32[288,128]{1,0:T(8,128)} %get-tuple-element.99.refs_7_), channel_id=1, source_target_pairs={{1,2},{2,1},{5,6},{6,5},{9,10},{10,9},{13,14},{14,13},{17,18},{18,... | collective-permute-start | bytes 442376 | tf_op jit(solution)/shard_map/ppermute | solution.py:421
  146.8 15.7 %all-to-all-start.4 = ((f32[32,8,128]{2,1,0:T(8,128)}), f32[32,8,128]{2,1,0:T(8,128)S(1)}, u32[]{:S(2)}, u32[]{:S(2)}) async-start(f32[32,8,128]{2,1,0:T(8,128)} %bitcast.43), calls=%async_computation.4 | async-start | bytes 262144 | tf_op jit(solution)/shard_map/all_to_all | solution.py:426
  154.2 0.7 copy-start.21
  154.2 0.7 copy-start.25
  155.0 0.7 copy-start.29
  162.4 0.7 copy-start.4
  167.7 10.8 %all-to-all-start.5 = ((f32[32,8,128]{2,1,0:T(8,128)}), f32[32,8,128]{2,1,0:T(8,128)S(1)}, u32[]{:S(2)}, u32[]{:S(2)}) async-start(f32[32,8,128]{2,1,0:T(8,128)} %bitcast.44), calls=%async_computation.5 | async-start | bytes 262144 | tf_op jit(solution)/shard_map/all_to_all | solution.py:426
  (12 other events, 7.6 us)

commit v6 on v5

--- a/solution.py
+++ b/solution.py
@@ -273,36 +273,32 @@
     return three_pass(left, jnp.concatenate([repeated(coefficients[0:GROUP]), repeated(-near)], axis=0))
 
 
-def first_kernel(schur, codes_row, codes_lanes, *refs):
+def first_kernel(*refs):
     received, sent, own = refs[0:4], refs[4:8], refs[8]
-    outs = refs[9:13]
-    gap_out, parts_out, mine_out, theirs_out = refs[13:17]
-    slot_pieces, row_pieces, out_pieces = refs[17:20]
-    schur = fetch(schur, refs[20], refs[21])
-    half = sent[0].shape[0] - codes_lanes.shape[0] // SIDES
-    cap = codes_lanes.shape[0] // SIDES
+    gap_out, parts_out, mine_out, theirs_out, pieces_out = refs[9:14]
+    cap = gap_out.shape[0] // SIDES
+    half = mine_out.shape[0] // SIDES
     for side in range(SIDES):
         block = sent[side][0:cap, :] - received[side][0:cap, :]
         gap_out[side * cap : (side + 1) * cap, :] = block
-        fill_pieces(slot_pieces, side * cap, block)
+        fill_pieces(pieces_out, side * cap, block)
         mine_out[side * half : (side + 1) * half, :] = sent[side][cap:, :]
         theirs_out[side * half : (side + 1) * half, :] = received[side][cap:, :]
-    copies(parts_out, components_of(own, slot_pieces))
+    copies(parts_out, components_of(own, pieces_out))
+
+
+def product_kernel(matrix, codes_row, codes_lanes, slot_pieces, *refs):
+    outs = refs[0:4]
+    row_pieces, out_pieces = refs[4:6]
+    matrix = fetch(matrix, refs[6], refs[7])
 
     def write(side, block):
         outs[side][...] = block
 
-    apply_local(schur, codes_row, codes_lanes, slot_pieces, row_pieces, out_pieces, write)
-
-
-def jump_kernel(*refs):
-    received, sent, out = refs[0:4], refs[4:8], refs[8]
-    cap = out.shape[0] // SIDES
-    for side in range(SIDES):
-        out[side * cap : (side + 1) * cap, :] = sent[side][...] - received[side][...]
-
-
-def stage_kernel(stage, counts, matrix, codes_row, codes_lanes, *refs):
+    apply_local(matrix, codes_row, codes_lanes, slot_pieces, row_pieces, out_pieces, write)
+
+
+def stage_kernel(stage, counts, *refs):
     refs = list(refs)
 
     def take(count):
@@ -310,23 +306,21 @@
         del refs[:count]
         return taken
 
-    jumps, mine, theirs = take(3)
-    own, gathered, inverse_rows, modes = take(4)
+    received, sent = take(4), take(4)
+    mine, theirs, own, gathered, inverse_rows, modes = take(6)
     states_in = take(counts[0])
-    outs = take(4) if stage < 5 else []
     states_out = take(counts[1])
     (parts_out,) = take(1)
-    slot_pieces, row_pieces, out_pieces = take(3)
-    if stage < 5:
-        matrix = fetch(matrix, *take(2))
-    total = codes_lanes.shape[0]
+    pieces_out = take(1)[0] if stage < 5 else None
+    (block_pieces,) = take(1)
+    total = modes.shape[0]
     cap = total // SIDES
     coefficients = exact(inverse_rows[...], gathered[...])
     direct_all = three_pass(modes[...], repeated(coefficients[0:GROUP]))
     half = mine.shape[0] // SIDES
     for side in range(SIDES):
         rows = slice(side * cap, (side + 1) * cap)
-        jump = jumps[rows, :]
+        jump = sent[side][...] - received[side][...]
         slab = slice(side * half, (side + 1) * half)
         first = 0 if stage in (2, 4) else 2
         behind = lagged(side, first, mine[slab, :], theirs[slab, :], coefficients)
@@ -357,15 +351,9 @@
             second = raw_step[rows, :] - new_step * direct
             states_out[1][rows, :] = second + start[rows, :] + step[rows, :]
         if nextin is not None:
-            fill_pieces(slot_pieces, side * cap, nextin)
-        fill_pieces(out_pieces, side * cap, block)
-    copies(parts_out, components_of(own, out_pieces))
-    if stage < 5:
-
-        def write(side, block):
-            outs[side][...] = block
-
-        apply_local(matrix, codes_row, codes_lanes, slot_pieces, row_pieces, out_pieces, write)
+            fill_pieces(pieces_out, side * cap, nextin)
+        fill_pieces(block_pieces, side * cap, block)
+    copies(parts_out, components_of(own, block_pieces))
 
 
 def rows_kernel(codes_lanes, residual, multipliers, modes, residual_out, multipliers_out, modes_out, pieces):
@@ -406,7 +394,7 @@
         scratch_shapes=list(scratch),
         cost_estimate=None
         if flops is None
-        else pl.CostEstimate(flops=flops, bytes_accessed=0, transcendentals=0),
+        else pl.CostEstimate(flops=flops, bytes_accessed=8 * inputs[0].size, transcendentals=0),
         compiler_params=pltpu.CompilerParams(vmem_limit_bytes=room * 1024 * 1024),
     )(*inputs)
 
@@ -443,7 +431,6 @@
     scratch = [pieces] * 3
     block = [(cap, cols)] * SIDES
     whole = (total, cols)
-    weight = 128 * total * total * cols
     parts = (wide, cols)
     brought = [pltpu.VMEM((total, total), jnp.float32), pltpu.SemaphoreType.DMA((SIDES,))]
 
@@ -479,36 +466,52 @@
     )
     sent, (start, inverse_rows) = shown[:4], shown[4:]
     received = exchange(sent)
-    shown = call(
+    in_pieces = jax.ShapeDtypeStruct((total, 2 * cols), jnp.bfloat16)
+    gap_jump, components, mine, theirs, ready = call(
         first_kernel,
         "stage_1",
-        block + [whole, parts] + [(2 * cap, 4 * GROUP)] * 2,
-        [schur, codes_row, codes_lanes, *received, *sent, own_pieces],
-        scratch + brought,
-        left=(0,),
-    )
-    sent, (gap_jump, components, mine, theirs) = shown[:4], shown[4:]
-
-    def stage(number, matrix, states_in, sent, components):
-        gathered = everywhere(components)
-        received = exchange(sent)
-        (jumps,) = call(jump_kernel, "jump", [whole], [*received, *sent], flops=weight)
-        inputs = [codes_row, codes_lanes, jumps, mine, theirs]
-        inputs += [own_pieces, gathered, inverse_rows, slot_modes, *states_in]
+        [whole, parts, (2 * cap, 4 * GROUP), (2 * cap, 4 * GROUP), in_pieces],
+        [*received, *sent, own_pieces],
+    )
+
+    def product(matrix, name, ready):
+        return call(
+            product_kernel,
+            name,
+            block,
+            [matrix, codes_row, codes_lanes, ready],
+            [pieces] * 2 + brought,
+            left=(0,),
+            flops=16 * total * total * cols,
+        )
+
+    def stage(number, states_in, sent, received, components):
+        inputs = [*received, *sent, mine, theirs, own_pieces, components, inverse_rows, slot_modes]
         outs = [whole] * 2 + [parts]
+        if number < 5:
+            outs = outs + [in_pieces]
         kernel = functools.partial(stage_kernel, number, (len(states_in), 2))
-        name = "stage_%d" % number
-        if matrix is None:
-            return call(functools.partial(kernel, None), name, outs, inputs, scratch)
-        return call(kernel, name, block + outs, [matrix] + inputs, scratch + brought, left=(0,))
-
-    shown = stage(2, flex, [gap_jump], sent, components)
-    sent, (precond, residual, components) = shown[:4], shown[4:]
-    shown = stage(3, schur, [precond, residual], sent, components)
-    sent, (residual, step, components) = shown[:4], shown[4:]
-    shown = stage(4, flex, [residual, step], sent, components)
-    sent, (residual, raw_step, components) = shown[:4], shown[4:]
-    shown = stage(5, None, [residual, raw_step, start, step], sent, components)
+        return call(kernel, "stage_%d" % number, outs, inputs + states_in, [pieces])
+
+    components = everywhere(components)
+    sent = product(schur, "product_1", ready)
+    received = exchange(sent)
+    shown = stage(2, [gap_jump], sent, received, components)
+    precond, residual, components, ready = shown
+    components = everywhere(components)
+    sent = product(flex, "product_2", ready)
+    received = exchange(sent)
+    shown = stage(3, [precond, residual], sent, received, components)
+    residual, step, components, ready = shown
+    components = everywhere(components)
+    sent = product(schur, "product_3", ready)
+    received = exchange(sent)
+    shown = stage(4, [residual, step], sent, received, components)
+    residual, raw_step, components, ready = shown
+    components = everywhere(components)
+    sent = product(flex, "product_4", ready)
+    received = exchange(sent)
+    shown = stage(5, [residual, raw_step, start, step], sent, received, components)
     residual, multipliers, components = shown
 
     gathered = everywhere(components)

time: 183 us -> 189 us (1.033)
  starting transfers between devices: 71.9 us -> 76.9 us
  local copies, waits for them, and re-layouts: 12.3 us -> 7.36 us
  waiting for transfers between devices: 22.9 us -> 26.8 us
    ppermute x24, waiting for transfers between devices: 1.95 us -> 24 us  [exchange(): received.append(lax.ppermute(block, axis, pairs))]
    all_to_all x6, waiting for transfers between devices: 20.9 us -> 2.86 us  [everywhere(): lax.all_to_all(stacked, ('sub', 'layer'), split_axis=0, concat_axis=0, ti...]
    all_to_all x6, starting transfers between devices: 40.3 us -> 51.7 us  [everywhere(): lax.all_to_all(stacked, ('sub', 'layer'), split_axis=0, concat_axis=0, ti...]
    ppermute x24, starting transfers between devices: 31.6 us -> 25.2 us  [exchange(): received.append(lax.ppermute(block, axis, pairs))]
    unnamed x61, local copies, waits for them, and re-layouts: 12.3 us -> 7.36 us
  transfers between devices with their start and end apart: 30 -> 30, of which waited for: 7 -> 7; matrix products, arithmetic and copies ran while one was open for 0% -> 0% of each run, Pallas kernels for 13% -> 22%
where the time goes in v6:
time: 189 us; the launch traced here: 187 us
  starting transfers between devices  76.9 us (41%)
  Pallas kernels  74.7 us (40%)
  waiting for transfers between devices  26.8 us (14%)
  local copies, waits for them, and re-layouts  7.36 us (4%)
    pallas_call x14, Pallas kernels, call(): pl.pallas_call(kernel, name=name, out_shape=shapes, in_specs=[pl.BlockSpe...  74.7 us
    all_to_all x6, starting transfers between devices, everywhere(): lax.all_to_all(stacked, ('sub', 'layer'), split_axis=0, concat_axis=0, ti...  51.7 us
    ppermute x24, starting transfers between devices, exchange(): received.append(lax.ppermute(block, axis, pairs))  25.2 us
    ppermute x24, waiting for transfers between devices, exchange(): received.append(lax.ppermute(block, axis, pairs))  24 us
    unnamed x61, local copies, waits for them, and re-layouts  7.36 us
  transfers between devices with their start and end apart: 30, of which 7 were waited for; matrix products, arithmetic and copies ran while one was open for 0% of the time, Pallas kernels for 22%

profile of v6, /device:TPU:0, one launch (start us, length us, event | category | flops | bytes accessed | tf_op | source)
XLA Modules:
  0.0 187.4 jit_solution(17716357077080490060)
XLA Ops:
  0.6 1.4 copy.11
  2.6 2.5 %modes_to_slots.1 = (f32[8,288]{1,0:T(8,128)}, f32[8,288]{1,0:T(8,128)}, f32[8,288]{1,0:T(8,128)}, f32[8,288]{1,0:T(8,128)}, f32[256,384]{1,0:T(8,128)}, /*index...) custom-call(s32[1,1152]{1,0:T(1,128)} %bitcast.45, f32[6,1152]{1,0:T(8,128)} %bitcast.39, f32[6,192]{1,0:T(8,128)} %inverse.1, ...), custom_call_target="tpu_custom_call" | custom-call | tf_op jit(solution)/shard_map/modes_to_slots/pallas_call | solution.py:388
  5.0 7.3 %all-to-all-start = ((f32[32,8,384]{2,1,0:T(8,128)}), f32[32,8,384]{2,1,0:T(8,128)S(1)}, u32[]{:S(2)}, u32[]{:S(2)}) async-start(f32[32,8,384]{2,1,0:T(8,128)} %bitcast.38), calls=%async_computation | async-start | bytes 786432 | tf_op jit(solution)/shard_map/all_to_all | solution.py:414
  12.3 1.8 collective-permute-start
  14.2 0.7 collective-permute-start.1
  14.9 0.7 collective-permute-start.3
  15.6 1.3 collective-permute-done.refs_4_
  17.5 10.0 %operators_on_modes.1 = (f32[144,128]{1,0:T(8,128)}, f32[144,128]{1,0:T(8,128)}, f32[144,128]{1,0:T(8,128)}, f32[144,128]{1,0:T(8,128)}, f32[1152,128]{1,0:T(8,128)}) custom-call(f32[1152,1152]{1,0:T(8,128)} %bitcast.23, f32[1152,1152]{1,0:T(8,128)} %bitcast.27, s32[1,1152]{1,0:T(1,128)} %get-tuple-element.61.codes_row, ...), custom_call_target="tpu_custom_call" | custom-call | tf_op jit(solution)/shard_map/operators_on_modes/pallas_call | solution.py:388
  27.5 0.7 copy-done
  28.3 7.6 %start.1 = (f32[432,128]{1,0:T(8,128)}, f32[432,128]{1,0:T(8,128)}, f32[432,128]{1,0:T(8,128)}, f32[432,128]{1,0:T(8,128)}, f32[1152,128]{1,0:T(8,128)}, /*index=5*/f32[160,256]{1,0:T(8,128)}) custom-call(f32[1152,1152]{1,0:T(8,128)} %bitcast.24, f32[1152,128]{1,0:T(8,128)} %bitcast.32, s32[1,1152]{1,0:T(1,128)} %get-tuple-element.61.codes_row, ...), custom_call_target="tpu_custom_call" | custom-call | tf_op jit(solution)/shard_map/start/pallas_call | solution.py:388
  35.9 4.5 %collective-permute-start.4 = (f32[432,128]{1,0:T(8,128)}, f32[432,128]{1,0:T(8,128)S(1)}, u32[]{:S(2)}, u32[]{:S(2)}) collective-permute-start(f32[432,128]{1,0:T(8,128)} %get-tuple-element.72.refs_4_), channel_id=1, source_target_pairs={{0,4},{4,0},{8,12},{12,8},{16,20},{20,16},{24,28},{28,24},{1,5},{5... | collective-permute-start | bytes 663560 | tf_op jit(solution)/shard_map/ppermute | solution.py:409
  40.4 0.8 collective-permute-start.5
  41.2 3.3 %collective-permute-start.6 = (f32[432,128]{1,0:T(8,128)}, f32[432,128]{1,0:T(8,128)S(1)}, u32[]{:S(2)}, u32[]{:S(2)}) collective-permute-start(f32[432,128]{1,0:T(8,128)} %get-tuple-element.74.refs_6_), channel_id=1, source_target_pairs={{0,1},{1,0},{2,3},{3,2},{4,5},{5,4},{6,7},{7,6},{8,9},{9,8},{10,11... | collective-permute-start | bytes 663560 | tf_op jit(solution)/shard_map/ppermute | solution.py:409
  44.5 0.7 collective-permute-start.7
  46.6 3.0 %stage_1.1 = (f32[1152,128]{1,0:T(8,128)}, f32[256,128]{1,0:T(8,128)}, f32[576,128]{1,0:T(8,128)}, f32[576,128]{1,0:T(8,128)}, bf16[1152,256]{1,0:T(8,128)(2,1)}) custom-call(f32[432,128]{1,0:T(8,128)} %copy-done.6, f32[432,128]{1,0:T(8,128)} %copy-done.7, f32[432,128]{1,0:T(8,128)} %copy-done.8, f32[432,128]{1,0:T(8,128)} %copy-done.9, ...), custom_call_target="tpu_custom_call" | custom-call | tf_op jit(solution)/shard_map/stage_1/pallas_call | solution.py:388
  49.6 13.2 %all-to-all-start.1 = ((f32[32,8,128]{2,1,0:T(8,128)}), f32[32,8,128]{2,1,0:T(8,128)S(1)}, u32[]{:S(2)}, u32[]{:S(2)}) async-start(f32[32,8,128]{2,1,0:T(8,128)} %bitcast.43), calls=%async_computation.1 | async-start | bytes 262144 | tf_op jit(solution)/shard_map/all_to_all | solution.py:414
  62.8 6.3 %product_1.1 = (f32[288,128]{1,0:T(8,128)}, f32[288,128]{1,0:T(8,128)}, f32[288,128]{1,0:T(8,128)}, f32[288,128]{1,0:T(8,128)}) custom-call(f32[1152,1152]{1,0:T(8,128)} %bitcast.28, s32[1,1152]{1,0:T(1,128)} %get-tuple-element.61.codes_row, s32[1152,128]{1,0:T(8,128)} %get-tuple-element.60.codes_lanes, bf16[1152,256]{1,0:T(8,128)(2,1)} %get-tuple-element.77.slot_pieces), custom_call_target="tpu_custom_call" | custom-call | flops 2717908992 | bytes 10616832 | tf_op jit(solution)/shard_map/product_1/pallas_call | solution.py:388
  69.1 1.8 collective-permute-start.8
  71.0 0.7 collective-permute-start.9
  71.7 0.7 collective-permute-start.11
  72.4 5.5 %collective-permute-done.8.refs_0_ = f32[288,128]{1,0:T(8,128)S(1)} collective-permute-done((f32[288,128]{1,0:T(8,128)}, f32[288,128]{1,0:T(8,128)S(1)}, u32[]{:S(2)}, u32[]{:S(2)}) %collective-permute-start.8) | collective-permute-done | bytes 147488 | tf_op jit(solution)/shard_map/ppermute | solution.py:409
  78.7 4.4 %stage_2.1 = (f32[1152,128]{1,0:T(8,128)}, f32[1152,128]{1,0:T(8,128)}, f32[256,128]{1,0:T(8,128)}, bf16[1152,256]{1,0:T(8,128)(2,1)}) custom-call(f32[288,128]{1,0:T(8,128)} %copy-done.12, f32[288,128]{1,0:T(8,128)} %copy-done.14, f32[288,128]{1,0:T(8,128)} %copy-done.16, f32[288,128]{1,0:T(8,128)} %copy-done.17, f32[288,128]{1,0:T(8,128)} %get-tuple-element.78.refs_4_, ...), custom_call_target="tpu_custom_call" | custom-call | tf_op jit(solution)/shard_map/stage_2/pallas_call | solution.py:388
  83.2 7.7 %all-to-all-start.2 = ((f32[32,8,128]{2,1,0:T(8,128)}), f32[32,8,128]{2,1,0:T(8,128)S(1)}, u32[]{:S(2)}, u32[]{:S(2)}) async-start(f32[32,8,128]{2,1,0:T(8,128)} %bitcast.42), calls=%async_computation.2 | async-start | bytes 262144 | tf_op jit(solution)/shard_map/all_to_all | solution.py:414
  90.9 6.3 %product_2.1 = (f32[288,128]{1,0:T(8,128)}, f32[288,128]{1,0:T(8,128)}, f32[288,128]{1,0:T(8,128)}, f32[288,128]{1,0:T(8,128)}) custom-call(f32[1152,1152]{1,0:T(8,128)} %bitcast.25, s32[1,1152]{1,0:T(1,128)} %get-tuple-element.61.codes_row, s32[1152,128]{1,0:T(8,128)} %get-tuple-element.60.codes_lanes, bf16[1152,256]{1,0:T(8,128)(2,1)} %get-tuple-element.87.slot_pieces), custom_call_target="tpu_custom_call" | custom-call | flops 2717908992 | bytes 10616832 | tf_op jit(solution)/shard_map/product_2/pallas_call | solution.py:388
  97.2 1.8 collective-permute-start.12
  99.0 0.7 collective-permute-start.13
  99.7 0.7 collective-permute-start.15
  100.4 5.5 %collective-permute-done.12.refs_0_ = f32[288,128]{1,0:T(8,128)S(1)} collective-permute-done((f32[288,128]{1,0:T(8,128)}, f32[288,128]{1,0:T(8,128)S(1)}, u32[]{:S(2)}, u32[]{:S(2)}) %collective-permute-start.12) | collective-permute-done | bytes 147488 | tf_op jit(solution)/shard_map/ppermute | solution.py:409
  106.8 4.7 %stage_3.1 = (f32[1152,128]{1,0:T(8,128)}, f32[1152,128]{1,0:T(8,128)}, f32[256,128]{1,0:T(8,128)}, bf16[1152,256]{1,0:T(8,128)(2,1)}) custom-call(f32[288,128]{1,0:T(8,128)} %copy-done.18, f32[288,128]{1,0:T(8,128)} %copy-done.20, f32[288,128]{1,0:T(8,128)} %copy-done.22, f32[288,128]{1,0:T(8,128)} %copy-done.24, f32[288,128]{1,0:T(8,128)} %get-tuple-element.88.refs_4_, ...), custom_call_target="tpu_custom_call" | custom-call | tf_op jit(solution)/shard_map/stage_3/pallas_call | solution.py:388
  111.5 7.9 %all-to-all-start.3 = ((f32[32,8,128]{2,1,0:T(8,128)}), f32[32,8,128]{2,1,0:T(8,128)S(1)}, u32[]{:S(2)}, u32[]{:S(2)}) async-start(f32[32,8,128]{2,1,0:T(8,128)} %bitcast.40), calls=%async_computation.3 | async-start | bytes 262144 | tf_op jit(solution)/shard_map/all_to_all | solution.py:414
  119.4 6.3 %product_3.1 = (f32[288,128]{1,0:T(8,128)}, f32[288,128]{1,0:T(8,128)}, f32[288,128]{1,0:T(8,128)}, f32[288,128]{1,0:T(8,128)}) custom-call(f32[1152,1152]{1,0:T(8,128)} %bitcast.29, s32[1,1152]{1,0:T(1,128)} %get-tuple-element.61.codes_row, s32[1152,128]{1,0:T(8,128)} %get-tuple-element.60.codes_lanes, bf16[1152,256]{1,0:T(8,128)(2,1)} %get-tuple-element.95.slot_pieces), custom_call_target="tpu_custom_call" | custom-call | flops 2717908992 | bytes 10616832 | tf_op jit(solution)/shard_map/product_3/pallas_call | solution.py:388
  125.7 1.6 collective-permute-start.16
  127.3 0.7 collective-permute-start.17
  128.1 0.7 collective-permute-start.19
  128.8 5.5 %collective-permute-done.16.refs_0_ = f32[288,128]{1,0:T(8,128)S(1)} collective-permute-done((f32[288,128]{1,0:T(8,128)}, f32[288,128]{1,0:T(8,128)S(1)}, u32[]{:S(2)}, u32[]{:S(2)}) %collective-permute-start.16) | collective-permute-done | bytes 147488 | tf_op jit(solution)/shard_map/ppermute | solution.py:409
  135.1 4.7 %stage_4.1 = (f32[1152,128]{1,0:T(8,128)}, f32[1152,128]{1,0:T(8,128)}, f32[256,128]{1,0:T(8,128)}, bf16[1152,256]{1,0:T(8,128)(2,1)}) custom-call(f32[288,128]{1,0:T(8,128)} %copy-done.19, f32[288,128]{1,0:T(8,128)} %copy-done.21, f32[288,128]{1,0:T(8,128)} %copy-done.23, f32[288,128]{1,0:T(8,128)} %copy-done.25, f32[288,128]{1,0:T(8,128)} %get-tuple-element.96.refs_4_, ...), custom_call_target="tpu_custom_call" | custom-call | tf_op jit(solution)/shard_map/stage_4/pallas_call | solution.py:388
  139.8 7.7 %all-to-all-start.4 = ((f32[32,8,128]{2,1,0:T(8,128)}), f32[32,8,128]{2,1,0:T(8,128)S(1)}, u32[]{:S(2)}, u32[]{:S(2)}) async-start(f32[32,8,128]{2,1,0:T(8,128)} %bitcast.41), calls=%async_computation.4 | async-start | bytes 262144 | tf_op jit(solution)/shard_map/all_to_all | solution.py:414
  147.5 6.3 %product_4.1 = (f32[288,128]{1,0:T(8,128)}, f32[288,128]{1,0:T(8,128)}, f32[288,128]{1,0:T(8,128)}, f32[288,128]{1,0:T(8,128)}) custom-call(f32[1152,1152]{1,0:T(8,128)} %bitcast.26, s32[1,1152]{1,0:T(1,128)} %get-tuple-element.61.codes_row, s32[1152,128]{1,0:T(8,128)} %get-tuple-element.60.codes_lanes, bf16[1152,256]{1,0:T(8,128)(2,1)} %get-tuple-element.103.slot_pieces), custom_call_target="tpu_custom_call" | custom-call | flops 2717908992 | bytes 10616832 | tf_op jit(solution)/shard_map/product_4/pallas_call | solution.py:388
  153.8 1.8 collective-permute-start.20
  155.6 0.7 collective-permute-start.21
  156.3 0.7 collective-permute-start.23
  157.0 5.5 %collective-permute-done.20.refs_0_ = f32[288,128]{1,0:T(8,128)S(1)} collective-permute-done((f32[288,128]{1,0:T(8,128)}, f32[288,128]{1,0:T(8,128)S(1)}, u32[]{:S(2)}, u32[]{:S(2)}) %collective-permute-start.20) | collective-permute-done | bytes 147488 | tf_op jit(solution)/shard_map/ppermute | solution.py:409
  163.4 4.7 %stage_5.1 = (f32[1152,128]{1,0:T(8,128)}, f32[1152,128]{1,0:T(8,128)}, f32[256,128]{1,0:T(8,128)}) custom-call(f32[288,128]{1,0:T(8,128)} %copy-done.10, f32[288,128]{1,0:T(8,128)} %copy-done.11, f32[288,128]{1,0:T(8,128)} %copy-done.13, f32[288,128]{1,0:T(8,128)} %copy-done.15, f32[288,128]{1,0:T(8,128)} %get-tuple-element.104.refs_4_, ...), custom_call_target="tpu_custom_call" | custom-call | tf_op jit(solution)/shard_map/stage_5/pallas_call | solution.py:388
  168.1 7.9 %all-to-all-start.5 = ((f32[32,8,128]{2,1,0:T(8,128)}), f32[32,8,128]{2,1,0:T(8,128)S(1)}, u32[]{:S(2)}, u32[]{:S(2)}) async-start(f32[32,8,128]{2,1,0:T(8,128)} %bitcast.44), calls=%async_computation.5 | async-start | bytes 262144 | tf_op jit(solution)/shard_map/all_to_all | solution.py:414
  176.1 5.1 %slots_to_rows.1 = (f32[1152,128]{1,0:T(8,128)}, f32[1152,128]{1,0:T(8,128)}, f32[1152,128]{1,0:T(8,128)}) custom-call(s32[1152,128]{1,0:T(8,128)} %get-tuple-element.60.codes_lanes, f32[1152,128]{1,0:T(8,128)} %get-tuple-element.112.residual, f32[1152,128]{1,0:T(8,128)} %get-tuple-element.113.multipliers, f32[1152,128]{1,0:T(8,128)} %get-tuple-element.71.refs_5_.refs_13_.modes), custom_call_target="tpu_custom_call" | custom-call | tf_op jit(solution)/shard_map/slots_to_rows/pallas_call | solution.py:388
  181.2 2.8 %all-to-all-done.5 = f32[32,8,128]{2,1,0:T(8,128)S(1)} async-done(((f32[32,8,128]{2,1,0:T(8,128)}), f32[32,8,128]{2,1,0:T(8,128)S(1)}, u32[]{:S(2)}, u32[]{:S(2)}) %all-to-all-start.5) | async-done | bytes 131104 | tf_op jit(solution)/shard_map/all_to_all | solution.py:414
  184.1 0.7 copy-done.3
  184.7 2.7 %residual.1 = f32[1152,128]{1,0:T(8,128)} custom-call(f32[1152,128]{1,0:T(8,128)} %get-tuple-element.115.residual, f32[1152,128]{1,0:T(8,128)} %get-tuple-element.116.modes, f32[256,128]{1,0:T(8,128)} %bitcast.35, f32[160,256]{1,0:T(8,128)} %get-tuple-element.85.refs_12_.inverse_rows), custom_call_target="tpu_custom_call" | custom-call | tf_op jit(solution)/shard_map/residual/pallas_call | solution.py:388
  (88 shorter events, 6.2 us)
Async XLA Ops:
  5.0 22.5 %all-to-all-start = ((f32[32,8,384]{2,1,0:T(8,128)}), f32[32,8,384]{2,1,0:T(8,128)S(1)}, u32[]{:S(2)}, u32[]{:S(2)}) async-start(f32[32,8,384]{2,1,0:T(8,128)} %bitcast.38), calls=%async_computation | async-start | bytes 786432 | tf_op jit(solution)/shard_map/all_to_all | solution.py:414
  12.3 4.5 %collective-permute-start = (f32[8,288]{1,0:T(8,128)}, f32[8,288]{1,0:T(8,128)S(1)}, u32[]{:S(2)}, u32[]{:S(2)}) collective-permute-start(f32[8,288]{1,0:T(8,128)} %get-tuple-element.62.refs_0_), channel_id=1, source_target_pairs={{0,4},{4,0},{8,12},{12,8},{16,20},{20,16},{24,28},{28,24},{1,5},{5... | collective-permute-start | bytes 27656 | tf_op jit(solution)/shard_map/ppermute | solution.py:409
  14.2 2.7 %collective-permute-start.1 = (f32[8,288]{1,0:T(8,128)}, f32[8,288]{1,0:T(8,128)S(1)}, u32[]{:S(2)}, u32[]{:S(2)}) collective-permute-start(f32[8,288]{1,0:T(8,128)} %get-tuple-element.63.refs_1_), channel_id=1, source_target_pairs={{4,8},{8,4},{12,16},{16,12},{20,24},{24,20},{5,9},{9,5},{13,17},{1... | collective-permute-start | bytes 27656 | tf_op jit(solution)/shard_map/ppermute | solution.py:409
  14.8 2.1 %collective-permute-start.2 = (f32[8,288]{1,0:T(8,128)}, f32[8,288]{1,0:T(8,128)S(1)}, u32[]{:S(2)}, u32[]{:S(2)}) collective-permute-start(f32[8,288]{1,0:T(8,128)} %get-tuple-element.64.refs_2_), channel_id=1, source_target_pairs={{0,1},{1,0},{2,3},{3,2},{4,5},{5,4},{6,7},{7,6},{8,9},{9,8},{10,11... | collective-permute-start | bytes 27656 | tf_op jit(solution)/shard_map/ppermute | solution.py:409
  14.9 2.0 %collective-permute-start.3 = (f32[8,288]{1,0:T(8,128)}, f32[8,288]{1,0:T(8,128)S(1)}, u32[]{:S(2)}, u32[]{:S(2)}) collective-permute-start(f32[8,288]{1,0:T(8,128)} %get-tuple-element.65.refs_3_), channel_id=1, source_target_pairs={{1,2},{2,1},{5,6},{6,5},{9,10},{10,9},{13,14},{14,13},{17,18},{18,... | collective-permute-start | bytes 27656 | tf_op jit(solution)/shard_map/ppermute | solution.py:409
  27.5 0.7 copy-start
  35.9 9.3 %collective-permute-start.4 = (f32[432,128]{1,0:T(8,128)}, f32[432,128]{1,0:T(8,128)S(1)}, u32[]{:S(2)}, u32[]{:S(2)}) collective-permute-start(f32[432,128]{1,0:T(8,128)} %get-tuple-element.72.refs_4_), channel_id=1, source_target_pairs={{0,4},{4,0},{8,12},{12,8},{16,20},{20,16},{24,28},{28,24},{1,5},{5... | collective-permute-start | bytes 663560 | tf_op jit(solution)/shard_map/ppermute | solution.py:409
  40.4 4.8 %collective-permute-start.5 = (f32[432,128]{1,0:T(8,128)}, f32[432,128]{1,0:T(8,128)S(1)}, u32[]{:S(2)}, u32[]{:S(2)}) collective-permute-start(f32[432,128]{1,0:T(8,128)} %get-tuple-element.73.refs_5_), channel_id=1, source_target_pairs={{4,8},{8,4},{12,16},{16,12},{20,24},{24,20},{5,9},{9,5},{13,17},{1... | collective-permute-start | bytes 663560 | tf_op jit(solution)/shard_map/ppermute | solution.py:409
  41.2 4.6 %collective-permute-start.6 = (f32[432,128]{1,0:T(8,128)}, f32[432,128]{1,0:T(8,128)S(1)}, u32[]{:S(2)}, u32[]{:S(2)}) collective-permute-start(f32[432,128]{1,0:T(8,128)} %get-tuple-element.74.refs_6_), channel_id=1, source_target_pairs={{0,1},{1,0},{2,3},{3,2},{4,5},{5,4},{6,7},{7,6},{8,9},{9,8},{10,11... | collective-permute-start | bytes 663560 | tf_op jit(solution)/shard_map/ppermute | solution.py:409
  44.5 1.3 collective-permute-start.7
  45.2 0.7 copy-start.7
  45.8 0.7 copy-start.8
  45.8 0.8 copy-start.9
  49.6 28.4 %all-to-all-start.1 = ((f32[32,8,128]{2,1,0:T(8,128)}), f32[32,8,128]{2,1,0:T(8,128)S(1)}, u32[]{:S(2)}, u32[]{:S(2)}) async-start(f32[32,8,128]{2,1,0:T(8,128)} %bitcast.43), calls=%async_computation.1 | async-start | bytes 262144 | tf_op jit(solution)/shard_map/all_to_all | solution.py:414
  69.1 8.8 %collective-permute-start.8 = (f32[288,128]{1,0:T(8,128)}, f32[288,128]{1,0:T(8,128)S(1)}, u32[]{:S(2)}, u32[]{:S(2)}) collective-permute-start(f32[288,128]{1,0:T(8,128)} %get-tuple-element.78.refs_4_), channel_id=1, source_target_pairs={{0,4},{4,0},{8,12},{12,8},{16,20},{20,16},{24,28},{28,24},{1,5},{5... | collective-permute-start | bytes 442376 | tf_op jit(solution)/shard_map/ppermute | solution.py:409
  71.0 6.9 %collective-permute-start.9 = (f32[288,128]{1,0:T(8,128)}, f32[288,128]{1,0:T(8,128)S(1)}, u32[]{:S(2)}, u32[]{:S(2)}) collective-permute-start(f32[288,128]{1,0:T(8,128)} %get-tuple-element.79.refs_5_), channel_id=1, source_target_pairs={{4,8},{8,4},{12,16},{16,12},{20,24},{24,20},{5,9},{9,5},{13,17},{1... | collective-permute-start | bytes 442376 | tf_op jit(solution)/shard_map/ppermute | solution.py:409
  71.6 6.3 %collective-permute-start.10 = (f32[288,128]{1,0:T(8,128)}, f32[288,128]{1,0:T(8,128)S(1)}, u32[]{:S(2)}, u32[]{:S(2)}) collective-permute-start(f32[288,128]{1,0:T(8,128)} %get-tuple-element.80.refs_6_), channel_id=1, source_target_pairs={{0,1},{1,0},{2,3},{3,2},{4,5},{5,4},{6,7},{7,6},{8,9},{9,8},{10,11... | collective-permute-start | bytes 442376 | tf_op jit(solution)/shard_map/ppermute | solution.py:409
  71.7 6.2 %collective-permute-start.11 = (f32[288,128]{1,0:T(8,128)}, f32[288,128]{1,0:T(8,128)S(1)}, u32[]{:S(2)}, u32[]{:S(2)}) collective-permute-start(f32[288,128]{1,0:T(8,128)} %get-tuple-element.81.refs_7_), channel_id=1, source_target_pairs={{1,2},{2,1},{5,6},{6,5},{9,10},{10,9},{13,14},{14,13},{17,18},{18,... | collective-permute-start | bytes 442376 | tf_op jit(solution)/shard_map/ppermute | solution.py:409
  77.9 0.7 copy-start.14
  77.9 0.8 copy-start.16
  77.9 0.8 copy-start.17
  77.9 0.8 copy-start.2
  83.2 22.8 %all-to-all-start.2 = ((f32[32,8,128]{2,1,0:T(8,128)}), f32[32,8,128]{2,1,0:T(8,128)S(1)}, u32[]{:S(2)}, u32[]{:S(2)}) async-start(f32[32,8,128]{2,1,0:T(8,128)} %bitcast.42), calls=%async_computation.2 | async-start | bytes 262144 | tf_op jit(solution)/shard_map/all_to_all | solution.py:414
  97.2 8.8 %collective-permute-start.12 = (f32[288,128]{1,0:T(8,128)}, f32[288,128]{1,0:T(8,128)S(1)}, u32[]{:S(2)}, u32[]{:S(2)}) collective-permute-start(f32[288,128]{1,0:T(8,128)} %get-tuple-element.88.refs_4_), channel_id=1, source_target_pairs={{0,4},{4,0},{8,12},{12,8},{16,20},{20,16},{24,28},{28,24},{1,5},{5... | collective-permute-start | bytes 442376 | tf_op jit(solution)/shard_map/ppermute | solution.py:409
  99.0 6.9 %collective-permute-start.13 = (f32[288,128]{1,0:T(8,128)}, f32[288,128]{1,0:T(8,128)S(1)}, u32[]{:S(2)}, u32[]{:S(2)}) collective-permute-start(f32[288,128]{1,0:T(8,128)} %get-tuple-element.89.refs_5_), channel_id=1, source_target_pairs={{4,8},{8,4},{12,16},{16,12},{20,24},{24,20},{5,9},{9,5},{13,17},{1... | collective-permute-start | bytes 442376 | tf_op jit(solution)/shard_map/ppermute | solution.py:409
  99.7 6.3 %collective-permute-start.14 = (f32[288,128]{1,0:T(8,128)}, f32[288,128]{1,0:T(8,128)S(1)}, u32[]{:S(2)}, u32[]{:S(2)}) collective-permute-start(f32[288,128]{1,0:T(8,128)} %get-tuple-element.90.refs_6_), channel_id=1, source_target_pairs={{0,1},{1,0},{2,3},{3,2},{4,5},{5,4},{6,7},{7,6},{8,9},{9,8},{10,11... | collective-permute-start | bytes 442376 | tf_op jit(solution)/shard_map/ppermute | solution.py:409
  99.7 6.2 %collective-permute-start.15 = (f32[288,128]{1,0:T(8,128)}, f32[288,128]{1,0:T(8,128)S(1)}, u32[]{:S(2)}, u32[]{:S(2)}) collective-permute-start(f32[288,128]{1,0:T(8,128)} %get-tuple-element.91.refs_7_), channel_id=1, source_target_pairs={{1,2},{2,1},{5,6},{6,5},{9,10},{10,9},{13,14},{14,13},{17,18},{18,... | collective-permute-start | bytes 442376 | tf_op jit(solution)/shard_map/ppermute | solution.py:409
  105.9 0.8 copy-start.22
  106.0 0.8 copy-start.24
  106.0 0.8 copy-start.4
  111.5 22.8 %all-to-all-start.3 = ((f32[32,8,128]{2,1,0:T(8,128)}), f32[32,8,128]{2,1,0:T(8,128)S(1)}, u32[]{:S(2)}, u32[]{:S(2)}) async-start(f32[32,8,128]{2,1,0:T(8,128)} %bitcast.40), calls=%async_computation.3 | async-start | bytes 262144 | tf_op jit(solution)/shard_map/all_to_all | solution.py:414
  125.7 8.5 %collective-permute-start.16 = (f32[288,128]{1,0:T(8,128)}, f32[288,128]{1,0:T(8,128)S(1)}, u32[]{:S(2)}, u32[]{:S(2)}) collective-permute-start(f32[288,128]{1,0:T(8,128)} %get-tuple-element.96.refs_4_), channel_id=1, source_target_pairs={{0,4},{4,0},{8,12},{12,8},{16,20},{20,16},{24,28},{28,24},{1,5},{5... | collective-permute-start | bytes 442376 | tf_op jit(solution)/shard_map/ppermute | solution.py:409
  127.3 6.9 %collective-permute-start.17 = (f32[288,128]{1,0:T(8,128)}, f32[288,128]{1,0:T(8,128)S(1)}, u32[]{:S(2)}, u32[]{:S(2)}) collective-permute-start(f32[288,128]{1,0:T(8,128)} %get-tuple-element.97.refs_5_), channel_id=1, source_target_pairs={{4,8},{8,4},{12,16},{16,12},{20,24},{24,20},{5,9},{9,5},{13,17},{1... | collective-permute-start | bytes 442376 | tf_op jit(solution)/shard_map/ppermute | solution.py:409
  128.0 6.3 %collective-permute-start.18 = (f32[288,128]{1,0:T(8,128)}, f32[288,128]{1,0:T(8,128)S(1)}, u32[]{:S(2)}, u32[]{:S(2)}) collective-permute-start(f32[288,128]{1,0:T(8,128)} %get-tuple-element.98.refs_6_), channel_id=1, source_target_pairs={{0,1},{1,0},{2,3},{3,2},{4,5},{5,4},{6,7},{7,6},{8,9},{9,8},{10,11... | collective-permute-start | bytes 442376 | tf_op jit(solution)/shard_map/ppermute | solution.py:409
  128.1 6.2 %collective-permute-start.19 = (f32[288,128]{1,0:T(8,128)}, f32[288,128]{1,0:T(8,128)S(1)}, u32[]{:S(2)}, u32[]{:S(2)}) collective-permute-start(f32[288,128]{1,0:T(8,128)} %get-tuple-element.99.refs_7_), channel_id=1, source_target_pairs={{1,2},{2,1},{5,6},{6,5},{9,10},{10,9},{13,14},{14,13},{17,18},{18,... | collective-permute-start | bytes 442376 | tf_op jit(solution)/shard_map/ppermute | solution.py:409
  134.3 0.7 copy-start.21
  134.3 0.8 copy-start.23
  134.3 0.8 copy-start.25
  134.3 0.8 copy-start.5
  139.8 22.8 %all-to-all-start.4 = ((f32[32,8,128]{2,1,0:T(8,128)}), f32[32,8,128]{2,1,0:T(8,128)S(1)}, u32[]{:S(2)}, u32[]{:S(2)}) async-start(f32[32,8,128]{2,1,0:T(8,128)} %bitcast.41), calls=%async_computation.4 | async-start | bytes 262144 | tf_op jit(solution)/shard_map/all_to_all | solution.py:414
  153.8 8.8 %collective-permute-start.20 = (f32[288,128]{1,0:T(8,128)}, f32[288,128]{1,0:T(8,128)S(1)}, u32[]{:S(2)}, u32[]{:S(2)}) collective-permute-start(f32[288,128]{1,0:T(8,128)} %get-tuple-element.104.refs_4_), channel_id=1, source_target_pairs={{0,4},{4,0},{8,12},{12,8},{16,20},{20,16},{24,28},{28,24},{1,5},{5... | collective-permute-start | bytes 442376 | tf_op jit(solution)/shard_map/ppermute | solution.py:409
  155.6 6.9 %collective-permute-start.21 = (f32[288,128]{1,0:T(8,128)}, f32[288,128]{1,0:T(8,128)S(1)}, u32[]{:S(2)}, u32[]{:S(2)}) collective-permute-start(f32[288,128]{1,0:T(8,128)} %get-tuple-element.105.refs_5_), channel_id=1, source_target_pairs={{4,8},{8,4},{12,16},{16,12},{20,24},{24,20},{5,9},{9,5},{13,17},{1... | collective-permute-start | bytes 442376 | tf_op jit(solution)/shard_map/ppermute | solution.py:409
  156.3 6.3 %collective-permute-start.22 = (f32[288,128]{1,0:T(8,128)}, f32[288,128]{1,0:T(8,128)S(1)}, u32[]{:S(2)}, u32[]{:S(2)}) collective-permute-start(f32[288,128]{1,0:T(8,128)} %get-tuple-element.106.refs_6_), channel_id=1, source_target_pairs={{0,1},{1,0},{2,3},{3,2},{4,5},{5,4},{6,7},{7,6},{8,9},{9,8},{10,11... | collective-permute-start | bytes 442376 | tf_op jit(solution)/shard_map/ppermute | solution.py:409
  156.3 6.2 %collective-permute-start.23 = (f32[288,128]{1,0:T(8,128)}, f32[288,128]{1,0:T(8,128)S(1)}, u32[]{:S(2)}, u32[]{:S(2)}) collective-permute-start(f32[288,128]{1,0:T(8,128)} %get-tuple-element.107.refs_7_), channel_id=1, source_target_pairs={{1,2},{2,1},{5,6},{6,5},{9,10},{10,9},{13,14},{14,13},{17,18},{18,... | collective-permute-start | bytes 442376 | tf_op jit(solution)/shard_map/ppermute | solution.py:409
  162.5 0.8 copy-start.13
  162.6 0.8 copy-start.15
  162.6 0.8 copy-start.1
  168.1 15.9 %all-to-all-start.5 = ((f32[32,8,128]{2,1,0:T(8,128)}), f32[32,8,128]{2,1,0:T(8,128)S(1)}, u32[]{:S(2)}, u32[]{:S(2)}) async-start(f32[32,8,128]{2,1,0:T(8,128)} %bitcast.44), calls=%async_computation.5 | async-start | bytes 262144 | tf_op jit(solution)/shard_map/all_to_all | solution.py:414
  (12 other events, 7.8 us)
